TPU v7x, 128 devices: a whole 4x4x4 slice. The times are simulated.
128 devices in a mesh: row: 8 (over z_lo, y), col: 16 (over z_hi, x, core).
Axes of the slice: x: 4, y: 4, z: 4 (z_hi: 2, z_lo: 2; z = z_hi * 2 + z_lo), core: 2. Of those that a mesh axis runs over, the one named last changes fastest.
Arguments:
- queries: bfloat16 [16384, 512], P(('row', 'col')), may hold values from -6 to 6
- keys: bfloat16 [8192, 512], P(('col', 'row')), may hold values from -6 to 6
- values: bfloat16 [8192, 512], P(('col', 'row')), may hold values from -6 to 6
- outputs: bfloat16 [16384, 512], P(('row', 'col')), may hold values from -3 to 3
- d_out: bfloat16 [16384, 512], P(('row', 'col')), may hold values from -816 to 816
- lse: float32 [4, 16384], P(None, ('row', 'col')), as said below
Outputs:
- grad_queries: float32 [16384, 512], P(('row', 'col'))
- grad_keys: float32 [8192, 512], P(('col', 'row'))
- grad_values: float32 [8192, 512], P(('col', 'row'))
Inputs may be any that keep to these rules, and one draw needn't show every extreme that they name: Each entry of lse exceeds the natural logarithm of 8192 by 0 to 3.
All inputs are finite; a program needn't handle non-finite values.
Results may differ from a plain program's by a relative error of at most 0.0047.
Values may be sent and summed in bfloat16 or wider, within the bound.
No kernel may reach another device: no remote copies, remote signals or barrier semaphores. Data moves between devices by JAX's collectives and lax.ppermute only.
A program may use at most 128 MiB of HBM per device.

v0:
```python
import math

import jax
import jax.numpy as jnp
from jax import lax
from jax.sharding import PartitionSpec as P

H = 4
DH = 128


def head_terms(query_rows, dout_rows, lse_rows, delta_rows, key_cols, value_cols, factor):
    scores = jnp.dot(query_rows, key_cols.T, preferred_element_type=jnp.float32) * factor
    probs = jnp.exp(scores - lse_rows[:, None])
    dprobs = jnp.dot(dout_rows, value_cols.T, preferred_element_type=jnp.float32)
    dscores = (probs * (dprobs - delta_rows[:, None]) * factor).astype(jnp.bfloat16)
    grad_query = jnp.dot(dscores, key_cols, preferred_element_type=jnp.float32)
    grad_key = jnp.dot(dscores.T, query_rows, preferred_element_type=jnp.float32)
    grad_value = jnp.dot(
        probs.astype(jnp.bfloat16).T, dout_rows, preferred_element_type=jnp.float32
    )
    return (grad_query, grad_key, grad_value)


def row_delta(dout_rows, output_rows):
    row_total = dout_rows.shape[0]
    product = dout_rows.astype(jnp.float32) * output_rows.astype(jnp.float32)
    return jnp.sum(product.reshape(row_total, H, DH), axis=2).T


def sweep_rows(query_rows, dout_rows, lse_rows, delta_rows, keys_all, values_all):
    factor = 1.0 / math.sqrt(DH)
    row_total = query_rows.shape[0]
    grad_keys = jnp.zeros(keys_all.shape, jnp.float32)
    grad_values = jnp.zeros(values_all.shape, jnp.float32)
    query_parts = []
    for first_row in range(0, row_total, 512):
        last_row = min(first_row + 512, row_total)
        head_query, head_key, head_value = ([], [], [])
        for head_index in range(H):
            low = head_index * DH
            high = low + DH
            grad_query, grad_key, grad_value = head_terms(
                query_rows[first_row:last_row, low:high],
                dout_rows[first_row:last_row, low:high],
                lse_rows[head_index, first_row:last_row],
                delta_rows[head_index, first_row:last_row],
                keys_all[:, low:high],
                values_all[:, low:high],
                factor,
            )
            head_query.append(grad_query)
            head_key.append(grad_key)
            head_value.append(grad_value)
        query_parts.append(jnp.concatenate(head_query, axis=1))
        grad_keys = grad_keys + jnp.concatenate(head_key, axis=1)
        grad_values = grad_values + jnp.concatenate(head_value, axis=1)
    return (jnp.concatenate(query_parts, axis=0), grad_keys, grad_values)


def per_device(queries, keys, values, outputs, d_out, lse):
    keys_all, values_all = (
        lax.all_gather(keys, "row", axis=0, tiled=True),
        lax.all_gather(values, "row", axis=0, tiled=True),
    )
    lse_all = lax.all_gather(lse, "col", axis=1, tiled=True)
    query_all, dout_all, output_all = (
        lax.all_gather(queries, "col", axis=0, tiled=True),
        lax.all_gather(d_out, "col", axis=0, tiled=True),
        lax.all_gather(outputs, "col", axis=0, tiled=True),
    )
    delta_rows = row_delta(dout_all, output_all)
    grad_query, grad_keys, grad_values = sweep_rows(
        query_all, dout_all, lse_all, delta_rows, keys_all, values_all
    )
    grad_keys, grad_values = (
        lax.psum_scatter(grad_keys, "row", scatter_dimension=0, tiled=True),
        lax.psum_scatter(grad_values, "row", scatter_dimension=0, tiled=True),
    )
    grad_query = lax.psum_scatter(grad_query, "col", scatter_dimension=0, tiled=True)
    return (grad_query, grad_keys, grad_values)


def solution(mesh):
    return jax.shard_map(
        per_device,
        mesh=mesh,
        in_specs=(
            P(("row", "col"), None),
            P(("col", "row"), None),
            P(("col", "row"), None),
            P(("row", "col"), None),
            P(("row", "col"), None),
            P(None, ("row", "col")),
        ),
        out_specs=(P(("row", "col"), None), P(("col", "row"), None), P(("col", "row"), None)),
        check_vma=False,
    )
```

profile of v0, /device:TPU:0, one launch (start us, length us, event | category | flops | bytes accessed | tf_op | source)
XLA Modules:
  0.0 408.3 jit_solution(4699205044477833541)
XLA Ops:
  9.4 25.4 %all_gather.20 = f32[4,2048]{1,0:T(4,128)S(1)} all-gather(f32[4,128]{1,0:T(4,128)} %param.11), channel_id=1, replica_groups=mesh['row'=8,'col'=16] {'col'}, dimensions={1}, use_global_device_ids=true | all-gather | bytes 34816 | tf_op jit(solution)/shard_map/all_gather | solution.py:66
  34.9 31.5 %all_gather.19 = bf16[512,512]{1,0:T(8,128)(2,1)} all-gather(bf16[64,512]{1,0:T(8,128)(2,1)} %param.7), channel_id=1, replica_groups=mesh['row'=8,'col'=16] {'row'}, dimensions={0}, use_global_device_ids=true | all-gather | bytes 589824 | tf_op jit(solution)/shard_map/all_gather | solution.py:63
  66.3 31.2 %all_gather.22 = bf16[512,512]{1,0:T(8,128)(2,1)} all-gather(bf16[64,512]{1,0:T(8,128)(2,1)} %param.8), channel_id=1, replica_groups=mesh['row'=8,'col'=16] {'row'}, dimensions={0}, use_global_device_ids=true | all-gather | bytes 589824 | tf_op jit(solution)/shard_map/all_gather | solution.py:64
  97.6 14.0 %all-gather.6.cloned.1.call-done = bf16[2048,512]{1,0:T(8,128)(2,1)} async-done(((bf16[128,512]{1,0:T(8,128)(2,1)}), bf16[2048,512]{1,0:T(8,128)(2,1)}) %all-gather.6.cloned.1.call-update) | async-done | bytes 2097168 | tf_op jit(solution)/shard_map/all_gather | solution.py:69
  111.6 4.9 %convert_multiply_fusion = f32[2048,512]{1,0:T(8,128)} fusion(bf16[2048,512]{1,0:T(8,128)(2,1)} %all-gather.8.cloned.1.call-done, bf16[2048,512]{1,0:T(8,128)(2,1)} %all-gather.6.cloned.1.call-done), kind=kLoop, calls=%fused_computation.1 | loop fusion | flops 3145728 | bytes 8388608 | tf_op jit(solution)/shard_map/mul | solution.py:27
  116.5 5.2 %reshape.41 = f32[2048,4,128]{2,1,0:T(4,128)} reshape(f32[2048,512]{1,0:T(8,128)} %convert_multiply_fusion) | data formatting | bytes 8388608 | tf_op jit(solution)/shard_map/reshape | solution.py:28
  121.8 5.3 %reduce_sum.9 = f32[2048,4]{1,0:T(8,128)S(1)} reduce(f32[2048,4,128]{2,1,0:T(4,128)} %reshape.41, f32[]{:T(128)} %constant.1.clone.1), dimensions={2}, to_apply=%region_0.0 | reduce | flops 1040384 | bytes 4227076 | tf_op jit(solution)/shard_map/reduce_sum | solution.py:28
  127.0 2.0 slice_reduce_fusion.15
  129.1 32.2 %all-gather.4.cloned.1.call-done = bf16[2048,512]{1,0:T(8,128)(2,1)} async-done(((bf16[128,512]{1,0:T(8,128)(2,1)}), bf16[2048,512]{1,0:T(8,128)(2,1)}) %all-gather.4.cloned.1.call-update) | async-done | bytes 2097168 | tf_op jit(solution)/shard_map/all_gather | solution.py:68
  166.5 1.6 fusion.64
  179.5 1.6 fusion.67
  183.8 1.6 fusion.68
  192.4 1.6 fusion.70
  196.8 1.6 fusion.71
  201.1 1.6 fusion.72
  214.0 1.6 fusion.75
  218.4 1.6 fusion.76
  231.5 9.1 %maximum_maximum_fusion = f32[2048,512]{0,1:T(8,128)} fusion(f32[512,128]{0,1:T(8,128)S(1)} %fusion.212, f32[512,128]{0,1:T(8,128)S(1)} %fusion.224, f32[512,128]{0,1:T(8,128)S(1)} %fusion.236, f32[512,128]{0,1:T(8,128)S(1)} %fusion.248, f32[512,128]{0,1:T(8,128)S(1)} %fusion.215, f32[512,128]{0,1:T(8,128)S(1)} %fusion.227, f32[512,128]{0,1:T(8,128)S(1)} %fusion.239, ...), kind=kLoop, calls=%fused_computation | loop fusion | flops 15728640 | bytes 8388608 | tf_op jit(solution)/shard_map/concatenate | solution.py:58
  242.2 1.6 fusion.106
  253.1 2.7 copy.20
  263.7 56.2 %reduce-scatter.8.cloned.1.call-done = f32[128,512]{0,1:T(8,128)} async-done(((f32[2048,512]{0,1:T(8,128)}), f32[128,512]{0,1:T(8,128)}) %reduce-scatter.8.cloned.1.call-update) | async-done | bytes 262160 | tf_op jit(solution)/shard_map/reduce_scatter | solution.py:80
  320.0 1.8 copy.15
  321.7 38.8 %reduce-scatter.12.cloned.1.call-done = f32[64,512]{1,0:T(8,128)} async-done(((f32[512,512]{1,0:T(8,128)}), f32[64,512]{1,0:T(8,128)}) %reduce-scatter.12.cloned.1.call-update) | async-done | bytes 131088
  360.5 40.9 %reduce-scatter.10.cloned.1.call-done = f32[64,512]{1,0:T(8,128)} async-done(((f32[512,512]{1,0:T(8,128)}), f32[64,512]{1,0:T(8,128)}) %reduce-scatter.10.cloned.1.call-update) | async-done | bytes 131088
  (210 shorter events, 76.9 us)
Async XLA Ops:
  7.2 90.4 %all-gather.8.cloned.1.call-start = ((), (), s32[]{:S(2)}) async-start(), calls=%async_computation.5 | async-start | bytes 2228224 | tf_op jit(solution)/shard_map/all_gather | solution.py:70
  7.9 103.7 %all-gather.6.cloned.1.call-start = ((), (), s32[]{:S(2)}) async-start(), calls=%async_computation.4 | async-start | bytes 2228224 | tf_op jit(solution)/shard_map/all_gather | solution.py:69
  8.6 152.6 %all-gather.4.cloned.1.call-start = ((), (), s32[]{:S(2)}) async-start(), calls=%async_computation.3 | async-start | bytes 2228224 | tf_op jit(solution)/shard_map/all_gather | solution.py:68
  9.4 310.6 %reduce-scatter.8.cloned.1.call-start = ((), (), s32[]{:S(2)}) async-start(), calls=%async_computation.6 | async-start | bytes 4456448 | tf_op jit(solution)/shard_map/reduce_scatter | solution.py:80
  166.5 5.9 %copy-start.1 = (f32[512,512]{1,0:T(8,128)}, f32[512,512]{1,0:T(8,128)S(1)}, u32[]{:S(2)}) copy-start(f32[512,512]{1,0:T(8,128)S(1)} %fusion.61) | copy-start | bytes 3145732
  170.8 5.9 %copy-start.3 = (f32[512,512]{1,0:T(8,128)}, f32[512,512]{1,0:T(8,128)S(1)}, u32[]{:S(2)}) copy-start(f32[512,512]{1,0:T(8,128)S(1)} %fusion.57) | copy-start | bytes 3145732
  175.1 6.0 %copy-start.5 = (f32[512,512]{1,0:T(8,128)}, f32[512,512]{1,0:T(8,128)S(1)}, u32[]{:S(2)}) copy-start(f32[512,512]{1,0:T(8,128)S(1)} %fusion.53) | copy-start | bytes 3145732
  176.8 5.7 %copy-start.35 = (bf16[512,512]{1,0:T(8,128)(2,1)}, bf16[512,512]{1,0:T(8,128)(2,1)S(1)}, u32[]{:S(2)}) copy-start(bf16[512,512]{1,0:T(8,128)(2,1)S(1)} %fusion.66) | copy-start | bytes 1572868
  179.4 6.0 %copy-start.9 = (f32[512,512]{1,0:T(8,128)}, f32[512,512]{1,0:T(8,128)S(1)}, u32[]{:S(2)}) copy-start(f32[512,512]{1,0:T(8,128)S(1)} %fusion.49) | copy-start | bytes 3145732
  181.1 5.7 %copy-start.37 = (bf16[512,512]{1,0:T(8,128)(2,1)}, bf16[512,512]{1,0:T(8,128)(2,1)S(1)}, u32[]{:S(2)}) copy-start(bf16[512,512]{1,0:T(8,128)(2,1)S(1)} %fusion.67) | copy-start | bytes 1572868
  183.8 6.0 %copy-start.7 = (f32[512,512]{1,0:T(8,128)}, f32[512,512]{1,0:T(8,128)S(1)}, u32[]{:S(2)}) copy-start(f32[512,512]{1,0:T(8,128)S(1)} %fusion.45) | copy-start | bytes 3145732
  188.1 5.9 %copy-start.11 = (f32[512,512]{1,0:T(8,128)}, f32[512,512]{1,0:T(8,128)S(1)}, u32[]{:S(2)}) copy-start(f32[512,512]{1,0:T(8,128)S(1)} %fusion.41) | copy-start | bytes 3145732
  192.4 6.0 %copy-start.13 = (f32[512,512]{1,0:T(8,128)}, f32[512,512]{1,0:T(8,128)S(1)}, u32[]{:S(2)}) copy-start(f32[512,512]{1,0:T(8,128)S(1)} %fusion.37) | copy-start | bytes 3145732
  196.7 6.0 %copy-start.17 = (f32[512,512]{1,0:T(8,128)}, f32[512,512]{1,0:T(8,128)S(1)}, u32[]{:S(2)}) copy-start(f32[512,512]{1,0:T(8,128)S(1)} %fusion.33) | copy-start | bytes 3145732
  198.4 5.7 %copy-start.45 = (bf16[512,512]{1,0:T(8,128)(2,1)}, bf16[512,512]{1,0:T(8,128)(2,1)S(1)}, u32[]{:S(2)}) copy-start(bf16[512,512]{1,0:T(8,128)(2,1)S(1)} %fusion.71) | copy-start | bytes 1572868
  201.1 6.0 %copy-start.15 = (f32[512,512]{1,0:T(8,128)}, f32[512,512]{1,0:T(8,128)S(1)}, u32[]{:S(2)}) copy-start(f32[512,512]{1,0:T(8,128)S(1)} %fusion.29) | copy-start | bytes 3145732
  205.4 5.9 %copy-start.18 = (f32[512,512]{1,0:T(8,128)}, f32[512,512]{1,0:T(8,128)S(1)}, u32[]{:S(2)}) copy-start(f32[512,512]{1,0:T(8,128)S(1)} %fusion.25) | copy-start | bytes 3145732
  209.7 6.0 %copy-start.24 = (f32[512,512]{1,0:T(8,128)}, f32[512,512]{1,0:T(8,128)S(1)}, u32[]{:S(2)}) copy-start(f32[512,512]{1,0:T(8,128)S(1)} %fusion.21) | copy-start | bytes 3145732
  214.0 6.0 %copy-start.28 = (f32[512,512]{1,0:T(8,128)}, f32[512,512]{1,0:T(8,128)S(1)}, u32[]{:S(2)}) copy-start(f32[512,512]{1,0:T(8,128)S(1)} %fusion.17) | copy-start | bytes 3145732
  215.7 5.7 %copy-start.53 = (bf16[512,512]{1,0:T(8,128)(2,1)}, bf16[512,512]{1,0:T(8,128)(2,1)S(1)}, u32[]{:S(2)}) copy-start(bf16[512,512]{1,0:T(8,128)(2,1)S(1)} %fusion.75) | copy-start | bytes 1572868
  218.4 6.0 %copy-start.20 = (f32[512,512]{1,0:T(8,128)}, f32[512,512]{1,0:T(8,128)S(1)}, u32[]{:S(2)}) copy-start(f32[512,512]{1,0:T(8,128)S(1)} %fusion.13) | copy-start | bytes 3145732
  222.7 6.8 %copy-start.22 = (f32[512,512]{1,0:T(8,128)}, f32[512,512]{1,0:T(8,128)S(1)}, u32[]{:S(2)}) copy-start(f32[512,512]{1,0:T(8,128)S(1)} %fusion.5) | copy-start | bytes 3145732
  240.7 119.9 %reduce-scatter.12.cloned.1.call-start = ((), (), s32[]{:S(2)}) async-start(), calls=%async_computation.8 | async-start | bytes 1179648
  255.8 145.6 %reduce-scatter.10.cloned.1.call-start = ((), (), s32[]{:S(2)}) async-start(), calls=%async_computation.7 | async-start | bytes 1179648
  (43 other events, 112.9 us)
Sparse Core Ops, SparseCore 0:
  10.4 52.0 all-gather.7
  64.9 46.6 all-gather.5
  114.1 47.0 all-gather.3
  240.8 79.1 reduce-scatter.7
  322.9 37.6 reduce-scatter.11
  363.5 37.9 reduce-scatter.9
where the time goes:
time: 410 us; the launch traced here: 408 us
  waiting for transfers between devices  184 us (45%)
  blocking collectives  88.1 us (21%)
  matrix products  80.2 us (20%)
  other arithmetic  21.2 us (5%)
  local copies, waits for them, and re-layouts  18.7 us (5%)
  between operations  15.5 us (4%)
    unnamed x8, waiting for transfers between devices  81.8 us
    reduce_scatter x1, waiting for transfers between devices, per_device(): lax.psum_scatter(grad_query, 'col', scatter_dimension=0, tiled=True)  56.2 us
    all_gather x1, waiting for transfers between devices, per_device(): lax.all_gather(queries, 'col', axis=0, tiled=True)  32.2 us
    all_gather x1, blocking collectives, per_device(): lax.all_gather(keys, 'row', axis=0, tiled=True)  31.5 us
    all_gather x1, blocking collectives, per_device(): lax.all_gather(values, 'row', axis=0, tiled=True)  31.2 us
    all_gather x1, blocking collectives, per_device(): lse_all = lax.all_gather(lse, 'col', axis=1, tiled=True)  25.4 us
    dot_general x16, matrix products, head_terms(): jnp.dot(dout_rows, value_cols.T, preferred_element_type=jnp.float32)  25.1 us
    dot_general x16, matrix products, head_terms(): grad_query = jnp.dot(dscores, key_cols, preferred_element_type=jnp.float32)  21.5 us
  transfers between devices with their start and end apart: 6, of which 5 were waited for; matrix products, arithmetic and copies ran while one was open for 9% of the time, Pallas kernels for 0%

commit v1 on v0

v1 whole, which is shorter than its diff:
```python
import functools
import math

import jax
import jax.numpy as jnp
from jax import lax
from jax.experimental import pallas as pl
from jax.experimental.pallas import tpu as pltpu
from jax.sharding import PartitionSpec as P

H = 4
DH = 128
AXES = ("row", "col")
F32 = jnp.float32
BF16 = jnp.bfloat16
QR = 128
KR = 64
AUX = 16
BLK = QR + KR + AUX
QS = 4 * QR
KS = 4 * KR
FACTOR = 1.0 / math.sqrt(DH)
LOG2E = math.log2(math.e)
VMEM = pl.BlockSpec(memory_space=pltpu.VMEM)
NT = (((1,), (1,)), ((), ()))


def linear(x, y, z, c):
    return ((z % 2) * 4 + y) * 16 + (z // 2) * 8 + x * 2 + c


def shift(value, dx=0, dy=0, dz=0, dc=0):
    pairs = []
    for x in range(4):
        for y in range(4):
            for z in range(4):
                for c in range(2):
                    there = linear((x + dx) % 4, (y + dy) % 4, (z + dz) % 4, c ^ dc)
                    pairs.append((linear(x, y, z, c), there))
    return lax.ppermute(value, AXES, pairs)


def three_parts(value):
    high = value.astype(BF16).astype(F32)
    rest = value - high
    middle = rest.astype(BF16).astype(F32)
    return [high, middle, rest - middle]


def pack_kernel(q_ref, k_ref, v_ref, o_ref, g_ref, lse_ref, *blocks):
    y = lax.axis_index("row") % 4
    for j, block in enumerate(blocks):
        head = lax.rem(y + j, 4)
        cols = pl.ds(pl.multiple_of(head * DH, DH), DH)
        g = g_ref[:, cols]
        block[:QR, :DH] = q_ref[:, cols]
        block[:QR, DH:] = g
        block[QR : QR + KR, :DH] = k_ref[:, cols]
        block[QR : QR + KR, DH:] = v_ref[:, cols]
        product = g.astype(F32) * o_ref[:, cols].astype(F32)
        delta = jnp.sum(product.T, axis=0, keepdims=True)
        both = jnp.concatenate([lse_ref[pl.ds(head, 1), :], delta], axis=1)
        rows = three_parts(both) + [jnp.zeros((AUX - 3, 2 * DH), F32)]
        block[QR + KR :, :] = jnp.concatenate(rows, axis=0).astype(BF16)


def join_kernel(b0, b1, b2, b3, q_out, kv_out):
    aux = []
    for j, block in enumerate((b0, b1, b2, b3)):
        q_out[j * QR : (j + 1) * QR, :] = block[:QR, :]
        kv_out[j * KR : (j + 1) * KR, :] = block[QR : QR + KR, :]
        aux.append(block[QR + KR :, :].astype(F32)[:3])
    aux.append(jnp.zeros((AUX - 12, 2 * DH), F32))
    q_out[QS:, :] = jnp.concatenate(aux, axis=0).astype(BF16)


def row_terms(q_ref):
    aux = q_ref[QS:, :].astype(F32)
    lse, delta = [], []
    for j in range(4):
        total = aux[3 * j : 3 * j + 1] + aux[3 * j + 1 : 3 * j + 2] + aux[3 * j + 2 : 3 * j + 3]
        lse.append(total[:, :DH])
        delta.append(total[:, DH:])
    return jnp.concatenate(lse, axis=1) * LOG2E, jnp.concatenate(delta, axis=1)


def attend_kernel(*refs):
    q_refs = refs[0:4]
    own_refs = refs[4:8]
    other_refs = refs[8:12]
    dq_own, dq_a, dq_b, dq_c, dkv_own, dkv_other = refs[12:18]
    kv, kt, dkv, dqt, terms = refs[18:]
    for i in range(4):
        kv[i * KS : (i + 1) * KS, :] = own_refs[i][...]
        kv[(4 + i) * KS : (5 + i) * KS, :] = other_refs[i][...]
    kt[...] = kv[:, :DH].T
    for b, q_ref in enumerate(q_refs):
        lse, delta = row_terms(q_ref)
        terms[b, 0:1, :] = lse
        terms[b, 1:2, :] = delta
    tile = 512
    for b, q_ref in enumerate(q_refs):

        def step(i, carry, b=b, q_ref=q_ref):
            rows = pl.ds(pl.multiple_of(i * tile, tile), tile)
            q = q_ref[:QS, :DH]
            g = q_ref[:QS, DH:]
            s = lax.dot_general(kv[rows, :DH], q, NT, preferred_element_type=F32)
            p = jnp.exp2(s * (FACTOR * LOG2E) - terms[b, 0:1, :])
            dp = lax.dot_general(kv[rows, DH:], g, NT, preferred_element_type=F32)
            ds = (p * (dp - terms[b, 1:2, :]) * FACTOR).astype(BF16)
            dv = jnp.dot(p.astype(BF16), g, preferred_element_type=F32)
            dk = jnp.dot(ds, q, preferred_element_type=F32)
            dq = jnp.dot(kt[:, rows], ds, preferred_element_type=F32)
            if b == 0:
                dkv[rows, :DH] = dk
                dkv[rows, DH:] = dv
            else:
                dkv[rows, :DH] += dk
                dkv[rows, DH:] += dv
            dqt[b] = jnp.where(i == 0, dq, dqt[b] + dq)
            return carry

        lax.fori_loop(0, 8 * KS // tile, step, 0)
    dq_own[...] = dqt[0].T
    for b, out in enumerate((dq_a, dq_b, dq_c)):
        out[...] = dqt[b + 1].T.astype(BF16)
    dkv_own[...] = dkv[: 4 * KS, :]
    dkv_other[...] = dkv[4 * KS :, :].astype(BF16)


def core_sum_kernel(own, other, s0, s1, s2, s3):
    for i, out in enumerate((s0, s1, s2, s3)):
        rows = slice(i * KS, (i + 1) * KS)
        out[...] = (own[rows, :] + other[rows, :].astype(F32)).astype(out.dtype)


def chip_sum_kernel(q0, q1, q2, q3, k0, k1, k2, k3, *outs):
    dq = q0[...] + q1[...].astype(F32) + q2[...].astype(F32) + q3[...].astype(F32)
    dkv = k0[...] + k1[...].astype(F32) + k2[...].astype(F32) + k3[...].astype(F32)
    for j, out in enumerate(outs):
        part = dq[j * QR : (j + 1) * QR]
        wide = jnp.concatenate([part[: QR // 2], part[QR // 2 :]], axis=1)
        out[:KR, :] = wide.astype(out.dtype)
        out[KR:, :] = dkv[j * KR : (j + 1) * KR].astype(out.dtype)


def unpack_kernel(b0, b1, b2, b3, dq, dk, dv):
    y = lax.axis_index("row") % 4
    for j, block in enumerate((b0, b1, b2, b3)):
        cols = pl.ds(pl.multiple_of(lax.rem(y + j, 4) * DH, DH), DH)
        dq[: QR // 2, cols] = block[:KR, :DH].astype(F32)
        dq[QR // 2 :, cols] = block[:KR, DH:].astype(F32)
        dk[:, cols] = block[KR:, :DH].astype(F32)
        dv[:, cols] = block[KR:, DH:].astype(F32)


def call(kernel, outs, args, scratch=(), flops=0):
    total = sum(a.size * a.dtype.itemsize for a in args) + sum(
        math.prod(shape) * jnp.dtype(kind).itemsize for shape, kind in outs
    )
    return pl.pallas_call(
        kernel,
        out_shape=[jax.ShapeDtypeStruct(shape, kind) for shape, kind in outs],
        in_specs=[VMEM] * len(args),
        out_specs=[VMEM] * len(outs),
        scratch_shapes=list(scratch),
        compiler_params=pltpu.CompilerParams(vmem_limit_bytes=40 * 1024 * 1024),
        cost_estimate=pl.CostEstimate(flops=flops, bytes_accessed=total, transcendentals=0),
    )(*args)


def per_device(queries, keys, values, outputs, d_out, lse):
    with jax.named_scope("pack"):
        blocks = call(
            pack_kernel, [((BLK, 2 * DH), BF16)] * 4, (queries, keys, values, outputs, d_out, lse)
        )
    with jax.named_scope("heads_over_y"):
        blocks = [blocks[0]] + [shift(blocks[j], dy=j) for j in (1, 2, 3)]
    with jax.named_scope("join"):
        q, kv = call(
            join_kernel, [((QS + AUX, 2 * DH), BF16), ((KS, 2 * DH), BF16)], blocks
        )
    with jax.named_scope("keys_over_z"):
        own = [kv] + [shift(kv, dz=d) for d in (1, 3, 2)]
        other = [shift(part, dc=1) for part in own]
    with jax.named_scope("queries_over_x"):
        qs = [q] + [shift(q, dx=d) for d in (1, 3, 2)]
    with jax.named_scope("attend"):
        dq0, dq1, dq2, dq3, dkv_own, dkv_other = call(
            attend_kernel,
            [((QS, DH), F32)]
            + [((QS, DH), BF16)] * 3
            + [((4 * KS, 2 * DH), F32), ((4 * KS, 2 * DH), BF16)],
            qs + own + other,
            scratch=[
                pltpu.VMEM((8 * KS, 2 * DH), BF16),
                pltpu.VMEM((DH, 8 * KS), BF16),
                pltpu.VMEM((8 * KS, 2 * DH), F32),
                pltpu.VMEM((4, DH, QS), F32),
                pltpu.VMEM((4, 8, QS), F32),
            ],
            flops=10 * 2048 * 2048 * 128,
        )
    with jax.named_scope("sum_queries_over_x"):
        dqs = [dq0, shift(dq1, dx=3), shift(dq2, dx=1), shift(dq3, dx=2)]
    with jax.named_scope("sum_keys_over_core"):
        dkv_other = shift(dkv_other, dc=1)
        parts = call(
            core_sum_kernel,
            [((KS, 2 * DH), F32)] + [((KS, 2 * DH), BF16)] * 3,
            (dkv_own, dkv_other),
        )
    with jax.named_scope("sum_keys_over_z"):
        dkvs = [parts[0]] + [shift(parts[1], dz=3), shift(parts[2], dz=1), shift(parts[3], dz=2)]
    with jax.named_scope("chip_sum"):
        backs = call(
            chip_sum_kernel,
            [((2 * KR, 2 * DH), F32)] + [((2 * KR, 2 * DH), BF16)] * 3,
            dqs + dkvs,
        )
    with jax.named_scope("back_over_y"):
        backs = [backs[0]] + [shift(backs[j], dy=4 - j) for j in (1, 2, 3)]
    with jax.named_scope("unpack"):
        return tuple(
            call(
                unpack_kernel,
                [((QR, H * DH), F32), ((KR, H * DH), F32), ((KR, H * DH), F32)],
                backs,
            )
        )


def solution(mesh):
    return jax.shard_map(
        per_device,
        mesh=mesh,
        in_specs=(
            P(("row", "col"), None),
            P(("col", "row"), None),
            P(("col", "row"), None),
            P(("row", "col"), None),
            P(("row", "col"), None),
            P(None, ("row", "col")),
        ),
        out_specs=(P(("row", "col"), None), P(("col", "row"), None), P(("col", "row"), None)),
        check_vma=False,
    )
```

time: 410 us -> 75 us (0.18)
  waiting for transfers between devices: 184 us -> 22.7 us
  blocking collectives: 88.1 us -> 0 us
  matrix products: 80.2 us -> 0 us
  starting transfers between devices: 0.24 us -> 31.2 us
  other arithmetic: 21.2 us -> 0 us
  Pallas kernels: 0 us -> 14.9 us
  between operations: 15.5 us -> 0.71 us
  local copies, waits for them, and re-layouts: 18.7 us -> 5.06 us
    all_gather x3 -> x0, blocking collectives: 88.1 us -> none  [the longest x1 31.5 us: per_device(): lax.all_gather(keys, 'row', axis=0, tiled=True)]
    unnamed x8 -> x0, waiting for transfers between devices: 81.8 us -> none
    dot_general x80 -> x0, matrix products: 80.2 us -> none  [the longest x16 25.1 us: head_terms(): jnp.dot(dout_rows, value_cols.T, preferred_element_type=jnp.float32)]
    reduce_scatter x1 -> x0, waiting for transfers between devices: 56.2 us -> none  [per_device(): lax.psum_scatter(grad_query, 'col', scatter_dimension=0, tiled=True)]
    all_gather x3 -> x0, waiting for transfers between devices: 46.2 us -> none  [the longest x1 32.2 us: per_device(): lax.all_gather(queries, 'col', axis=0, tiled=True)]
    ppermute x0 -> x23, starting transfers between devices: none -> 31.2 us  [shift(): return lax.ppermute(value, AXES, pairs)]
    ppermute x0 -> x23, waiting for transfers between devices: none -> 22.7 us  [shift(): return lax.ppermute(value, AXES, pairs)]
    pallas_call x0 -> x6, Pallas kernels: none -> 14.9 us  [call(): pl.pallas_call(kernel, out_shape=[jax.ShapeDtypeStruct(shape, kind) for s...]
  transfers between devices with their start and end apart: 6 -> 23, of which waited for: 5 -> 13; matrix products, arithmetic and copies ran while one was open for 9% -> 0% of each run, Pallas kernels for 0% -> 0%
where the time goes in v1:
time: 75 us; the launch traced here: 74.5 us
  starting transfers between devices  31.2 us (42%)
  waiting for transfers between devices  22.7 us (30%)
  Pallas kernels  14.9 us (20%)
  local copies, waits for them, and re-layouts  5.06 us (7%)
    ppermute x23, starting transfers between devices, shift(): return lax.ppermute(value, AXES, pairs)  31.2 us
    ppermute x23, waiting for transfers between devices, shift(): return lax.ppermute(value, AXES, pairs)  22.7 us
    pallas_call x6, Pallas kernels, call(): pl.pallas_call(kernel, out_shape=[jax.ShapeDtypeStruct(shape, kind) for s...  14.9 us
    unnamed x12, local copies, waits for them, and re-layouts  5.06 us
  transfers between devices with their start and end apart: 23, of which 13 were waited for; matrix products, arithmetic and copies ran while one was open for 0% of the time, Pallas kernels for 0%

profile of v1, /device:TPU:0, one launch (start us, length us, event | category | flops | bytes accessed | tf_op | source)
XLA Modules:
  0.0 74.5 jit_solution(12751000135166034898)
XLA Ops:
  0.6 0.9 %copy-done = bf16[128,512]{1,0:T(8,128)(2,1)S(1)} copy-done((bf16[128,512]{1,0:T(8,128)(2,1)S(1)}, bf16[128,512]{1,0:T(8,128)(2,1)}, u32[]{:S(2)}) %copy-start) | copy-done | bytes 131096
  1.5 0.9 %copy-done.1 = bf16[128,512]{1,0:T(8,128)(2,1)S(1)} copy-done((bf16[128,512]{1,0:T(8,128)(2,1)S(1)}, bf16[128,512]{1,0:T(8,128)(2,1)}, u32[]{:S(2)}) %copy-start.1) | copy-done | bytes 131096
  2.4 0.9 %copy-done.2 = bf16[128,512]{1,0:T(8,128)(2,1)S(1)} copy-done((bf16[128,512]{1,0:T(8,128)(2,1)S(1)}, bf16[128,512]{1,0:T(8,128)(2,1)}, u32[]{:S(2)}) %copy-start.2) | copy-done | bytes 131096
  5.9 1.7 %collective-permute-start = (bf16[208,256]{1,0:T(8,128)(2,1)S(1)}, bf16[208,256]{1,0:T(8,128)(2,1)S(1)}, u32[]{:S(2)}, u32[]{:S(2)}) collective-permute-start(bf16[208,256]{1,0:T(8,128)(2,1)S(1)} %get-tuple-element.24), channel_id=1, source_target_pairs={{0,16},{1,17},{64,80},{65,81},{8,24},{9,25},{72,88},{73,89},{16,32... | collective-permute-start | bytes 319496 | tf_op jit(solution)/shard_map/heads_over_y/ppermute | solution.py:40
  7.6 2.9 %collective-permute-start.1 = (bf16[208,256]{1,0:T(8,128)(2,1)S(1)}, bf16[208,256]{1,0:T(8,128)(2,1)S(1)}, u32[]{:S(2)}, u32[]{:S(2)}) collective-permute-start(bf16[208,256]{1,0:T(8,128)(2,1)S(1)} %get-tuple-element.25), channel_id=1, source_target_pairs={{0,32},{1,33},{64,96},{65,97},{8,40},{9,41},{72,104},{73,105},{16,... | collective-permute-start | bytes 319496 | tf_op jit(solution)/shard_map/heads_over_y/ppermute | solution.py:40
  10.5 1.3 %collective-permute-start.2 = (bf16[208,256]{1,0:T(8,128)(2,1)S(1)}, bf16[208,256]{1,0:T(8,128)(2,1)S(1)}, u32[]{:S(2)}, u32[]{:S(2)}) collective-permute-start(bf16[208,256]{1,0:T(8,128)(2,1)S(1)} %get-tuple-element.26), channel_id=1, source_target_pairs={{0,48},{1,49},{64,112},{65,113},{8,56},{9,57},{72,120},{73,121},{1... | collective-permute-start | bytes 319496 | tf_op jit(solution)/shard_map/heads_over_y/ppermute | solution.py:40
  12.0 3.5 %collective-permute-done.1.b2 = bf16[208,256]{1,0:T(8,128)(2,1)S(1)} collective-permute-done((bf16[208,256]{1,0:T(8,128)(2,1)S(1)}, bf16[208,256]{1,0:T(8,128)(2,1)S(1)}, u32[]{:S(2)}, u32[]{:S(2)}) %collective-permute-start.1) | collective-permute-done | bytes 106528 | tf_op jit(solution)/shard_map/heads_over_y/ppermute | solution.py:40
  15.6 4.0 %collective-permute-start.8 = (bf16[256,256]{1,0:T(8,128)(2,1)S(1)}, bf16[256,256]{1,0:T(8,128)(2,1)S(1)}, u32[]{:S(2)}, u32[]{:S(2)}) collective-permute-start(bf16[256,256]{1,0:T(8,128)(2,1)S(1)} %get-tuple-element.28.refs_4_), channel_id=1, source_target_pairs={{0,8},{1,9},{64,72},{65,73},{8,0},{9,1},{72,64},{73,65},{16,24},{1... | collective-permute-start | bytes 393224 | tf_op jit(solution)/shard_map/keys_over_z/ppermute | solution.py:40
  20.3 3.0 %collective-permute-start.5 = (bf16[528,256]{1,0:T(8,128)(2,1)S(1)}, bf16[528,256]{1,0:T(8,128)(2,1)S(1)}, u32[]{:S(2)}, u32[]{:S(2)}) collective-permute-start(bf16[528,256]{1,0:T(8,128)(2,1)S(1)} %get-tuple-element.27.refs_0_), channel_id=1, source_target_pairs={{0,4},{1,5},{64,68},{65,69},{8,12},{9,13},{72,76},{73,77},{16,20},... | collective-permute-start | bytes 811016 | tf_op jit(solution)/shard_map/queries_over_x/ppermute | solution.py:40
  23.3 1.1 %collective-permute-start.4 = (bf16[528,256]{1,0:T(8,128)(2,1)S(1)}, bf16[528,256]{1,0:T(8,128)(2,1)S(1)}, u32[]{:S(2)}, u32[]{:S(2)}) collective-permute-start(bf16[528,256]{1,0:T(8,128)(2,1)S(1)} %get-tuple-element.27.refs_0_), channel_id=1, source_target_pairs={{0,6},{1,7},{64,70},{65,71},{8,14},{9,15},{72,78},{73,79},{16,22},... | collective-permute-start | bytes 811016 | tf_op jit(solution)/shard_map/queries_over_x/ppermute | solution.py:40
  24.5 0.9 %collective-permute-start.3 = (bf16[528,256]{1,0:T(8,128)(2,1)S(1)}, bf16[528,256]{1,0:T(8,128)(2,1)S(1)}, u32[]{:S(2)}, u32[]{:S(2)}) collective-permute-start(bf16[528,256]{1,0:T(8,128)(2,1)S(1)} %get-tuple-element.27.refs_0_), channel_id=1, source_target_pairs={{0,2},{1,3},{64,66},{65,67},{8,10},{9,11},{72,74},{73,75},{16,18},... | collective-permute-start | bytes 811016 | tf_op jit(solution)/shard_map/queries_over_x/ppermute | solution.py:40
  25.4 1.3 %collective-permute-start.6 = (bf16[256,256]{1,0:T(8,128)(2,1)S(1)}, bf16[256,256]{1,0:T(8,128)(2,1)S(1)}, u32[]{:S(2)}, u32[]{:S(2)}) collective-permute-start(bf16[256,256]{1,0:T(8,128)(2,1)S(1)} %get-tuple-element.28.refs_4_), channel_id=1, source_target_pairs={{0,64},{1,65},{64,8},{65,9},{8,72},{9,73},{72,0},{73,1},{16,80},{1... | collective-permute-start | bytes 393224 | tf_op jit(solution)/shard_map/keys_over_z/ppermute | solution.py:40
  27.3 4.3 %collective-permute-done.6.refs_5_ = bf16[256,256]{1,0:T(8,128)(2,1)S(1)} collective-permute-done((bf16[256,256]{1,0:T(8,128)(2,1)S(1)}, bf16[256,256]{1,0:T(8,128)(2,1)S(1)}, u32[]{:S(2)}, u32[]{:S(2)}) %collective-permute-start.6) | collective-permute-done | bytes 131104 | tf_op jit(solution)/shard_map/keys_over_z/ppermute | solution.py:40
  33.1 2.9 %collective-permute-done.4.refs_2_ = bf16[528,256]{1,0:T(8,128)(2,1)S(1)} collective-permute-done((bf16[528,256]{1,0:T(8,128)(2,1)S(1)}, bf16[528,256]{1,0:T(8,128)(2,1)S(1)}, u32[]{:S(2)}, u32[]{:S(2)}) %collective-permute-start.4) | collective-permute-done | bytes 270368 | tf_op jit(solution)/shard_map/queries_over_x/ppermute | solution.py:40
  36.0 13.6 %attend.1 = (f32[512,128]{1,0:T(8,128)S(1)}, bf16[512,128]{1,0:T(8,128)(2,1)S(1)}, bf16[512,128]{1,0:T(8,128)(2,1)S(1)}, bf16[512,128]{1,0:T(8,128)(2,1)S(1)}, f...) custom-call(bf16[528,256]{1,0:T(8,128)(2,1)S(1)} %get-tuple-element.27.refs_0_, ...), custom_call_target="tpu_custom_call" | custom-call | flops 5368709120 | bytes 4358144 | tf_op jit(solution)/shard_map/attend/pallas_call | solution.py:162
  49.7 2.7 %collective-permute-start.13 = (bf16[512,128]{1,0:T(8,128)(2,1)S(1)}, bf16[512,128]{1,0:T(8,128)(2,1)S(1)}, u32[]{:S(2)}, u32[]{:S(2)}) collective-permute-start(bf16[512,128]{1,0:T(8,128)(2,1)S(1)} %get-tuple-element.30), channel_id=1, source_target_pairs={{0,6},{1,7},{64,70},{65,71},{8,14},{9,15},{72,78},{73,79},{16,22},... | collective-permute-start | bytes 393224 | tf_op jit(solution)/shard_map/sum_queries_over_x/ppermute | solution.py:40
  52.4 2.3 %collective-permute-start.15 = (bf16[512,128]{1,0:T(8,128)(2,1)S(1)}, bf16[512,128]{1,0:T(8,128)(2,1)S(1)}, u32[]{:S(2)}, u32[]{:S(2)}) collective-permute-start(bf16[512,128]{1,0:T(8,128)(2,1)S(1)} %get-tuple-element.32), channel_id=1, source_target_pairs={{0,4},{1,5},{64,68},{65,69},{8,12},{9,13},{72,76},{73,77},{16,20},... | collective-permute-start | bytes 393224 | tf_op jit(solution)/shard_map/sum_queries_over_x/ppermute | solution.py:40
  55.1 1.7 %collective-permute-start.18 = (bf16[256,256]{1,0:T(8,128)(2,1)S(1)}, bf16[256,256]{1,0:T(8,128)(2,1)S(1)}, u32[]{:S(2)}, u32[]{:S(2)}) collective-permute-start(bf16[256,256]{1,0:T(8,128)(2,1)S(1)} %get-tuple-element.37), channel_id=1, source_target_pairs={{0,64},{1,65},{64,8},{65,9},{8,72},{9,73},{72,0},{73,1},{16,80},{1... | collective-permute-start | bytes 393224 | tf_op jit(solution)/shard_map/sum_keys_over_z/ppermute | solution.py:40
  56.9 2.4 %collective-permute-start.19 = (bf16[256,256]{1,0:T(8,128)(2,1)S(1)}, bf16[256,256]{1,0:T(8,128)(2,1)S(1)}, u32[]{:S(2)}, u32[]{:S(2)}) collective-permute-start(bf16[256,256]{1,0:T(8,128)(2,1)S(1)} %get-tuple-element.38), channel_id=1, source_target_pairs={{0,8},{1,9},{64,72},{65,73},{8,0},{9,1},{72,64},{73,65},{16,24},{1... | collective-permute-start | bytes 393224 | tf_op jit(solution)/shard_map/sum_keys_over_z/ppermute | solution.py:40
  59.2 2.7 %collective-permute-done.14.q2 = bf16[512,128]{1,0:T(8,128)(2,1)S(1)} collective-permute-done((bf16[512,128]{1,0:T(8,128)(2,1)S(1)}, bf16[512,128]{1,0:T(8,128)(2,1)S(1)}, u32[]{:S(2)}, u32[]{:S(2)}) %collective-permute-start.14) | collective-permute-done | bytes 131104 | tf_op jit(solution)/shard_map/sum_queries_over_x/ppermute | solution.py:40
  62.4 2.4 %collective-permute-done.19.k3 = bf16[256,256]{1,0:T(8,128)(2,1)S(1)} collective-permute-done((bf16[256,256]{1,0:T(8,128)(2,1)S(1)}, bf16[256,256]{1,0:T(8,128)(2,1)S(1)}, u32[]{:S(2)}, u32[]{:S(2)}) %collective-permute-start.19) | collective-permute-done | bytes 131104 | tf_op jit(solution)/shard_map/sum_keys_over_z/ppermute | solution.py:40
  64.9 2.4 %collective-permute-start.20 = (bf16[128,256]{1,0:T(8,128)(2,1)S(1)}, bf16[128,256]{1,0:T(8,128)(2,1)S(1)}, u32[]{:S(2)}, u32[]{:S(2)}) collective-permute-start(bf16[128,256]{1,0:T(8,128)(2,1)S(1)} %get-tuple-element.40), channel_id=1, source_target_pairs={{0,48},{1,49},{64,112},{65,113},{8,56},{9,57},{72,120},{73,121},{1... | collective-permute-start | bytes 196616 | tf_op jit(solution)/shard_map/back_over_y/ppermute | solution.py:40
  67.2 1.0 %collective-permute-start.21 = (bf16[128,256]{1,0:T(8,128)(2,1)S(1)}, bf16[128,256]{1,0:T(8,128)(2,1)S(1)}, u32[]{:S(2)}, u32[]{:S(2)}) collective-permute-start(bf16[128,256]{1,0:T(8,128)(2,1)S(1)} %get-tuple-element.41), channel_id=1, source_target_pairs={{0,32},{1,33},{64,96},{65,97},{8,40},{9,41},{72,104},{73,105},{16,... | collective-permute-start | bytes 196616 | tf_op jit(solution)/shard_map/back_over_y/ppermute | solution.py:40
  69.2 3.8 %collective-permute-done.21.b2 = bf16[128,256]{1,0:T(8,128)(2,1)S(1)} collective-permute-done((bf16[128,256]{1,0:T(8,128)(2,1)S(1)}, bf16[128,256]{1,0:T(8,128)(2,1)S(1)}, u32[]{:S(2)}, u32[]{:S(2)}) %collective-permute-start.21) | collective-permute-done | bytes 65568 | tf_op jit(solution)/shard_map/back_over_y/ppermute | solution.py:40
  (40 shorter events, 9.2 us)
Async XLA Ops:
  0.6 0.9 %copy-start = (bf16[128,512]{1,0:T(8,128)(2,1)S(1)}, bf16[128,512]{1,0:T(8,128)(2,1)}, u32[]{:S(2)}) copy-start(bf16[128,512]{1,0:T(8,128)(2,1)} %q_ref.1) | copy-start | bytes 393220
  5.9 6.1 %collective-permute-start = (bf16[208,256]{1,0:T(8,128)(2,1)S(1)}, bf16[208,256]{1,0:T(8,128)(2,1)S(1)}, u32[]{:S(2)}, u32[]{:S(2)}) collective-permute-start(bf16[208,256]{1,0:T(8,128)(2,1)S(1)} %get-tuple-element.24), channel_id=1, source_target_pairs={{0,16},{1,17},{64,80},{65,81},{8,24},{9,25},{72,88},{73,89},{16,32... | collective-permute-start | bytes 319496 | tf_op jit(solution)/shard_map/heads_over_y/ppermute | solution.py:40
  7.6 7.9 %collective-permute-start.1 = (bf16[208,256]{1,0:T(8,128)(2,1)S(1)}, bf16[208,256]{1,0:T(8,128)(2,1)S(1)}, u32[]{:S(2)}, u32[]{:S(2)}) collective-permute-start(bf16[208,256]{1,0:T(8,128)(2,1)S(1)} %get-tuple-element.25), channel_id=1, source_target_pairs={{0,32},{1,33},{64,96},{65,97},{8,40},{9,41},{72,104},{73,105},{16,... | collective-permute-start | bytes 319496 | tf_op jit(solution)/shard_map/heads_over_y/ppermute | solution.py:40
  10.5 5.0 %collective-permute-start.2 = (bf16[208,256]{1,0:T(8,128)(2,1)S(1)}, bf16[208,256]{1,0:T(8,128)(2,1)S(1)}, u32[]{:S(2)}, u32[]{:S(2)}) collective-permute-start(bf16[208,256]{1,0:T(8,128)(2,1)S(1)} %get-tuple-element.26), channel_id=1, source_target_pairs={{0,48},{1,49},{64,112},{65,113},{8,56},{9,57},{72,120},{73,121},{1... | collective-permute-start | bytes 319496 | tf_op jit(solution)/shard_map/heads_over_y/ppermute | solution.py:40
  15.5 8.9 %collective-permute-start.9 = (bf16[256,256]{1,0:T(8,128)(2,1)S(1)}, bf16[256,256]{1,0:T(8,128)(2,1)S(1)}, u32[]{:S(2)}, u32[]{:S(2)}) collective-permute-start(bf16[256,256]{1,0:T(8,128)(2,1)S(1)} %get-tuple-element.28.refs_4_), channel_id=1, source_target_pairs={{0,1},{1,0},{64,65},{65,64},{8,9},{9,8},{72,73},{73,72},{16,17},{1... | collective-permute-start | bytes 393224 | tf_op jit(solution)/shard_map/keys_over_z/ppermute | solution.py:40
  15.6 9.7 %collective-permute-start.8 = (bf16[256,256]{1,0:T(8,128)(2,1)S(1)}, bf16[256,256]{1,0:T(8,128)(2,1)S(1)}, u32[]{:S(2)}, u32[]{:S(2)}) collective-permute-start(bf16[256,256]{1,0:T(8,128)(2,1)S(1)} %get-tuple-element.28.refs_4_), channel_id=1, source_target_pairs={{0,8},{1,9},{64,72},{65,73},{8,0},{9,1},{72,64},{73,65},{16,24},{1... | collective-permute-start | bytes 393224 | tf_op jit(solution)/shard_map/keys_over_z/ppermute | solution.py:40
  19.6 7.7 %collective-permute-start.7 = (bf16[256,256]{1,0:T(8,128)(2,1)S(1)}, bf16[256,256]{1,0:T(8,128)(2,1)S(1)}, u32[]{:S(2)}, u32[]{:S(2)}) collective-permute-start(bf16[256,256]{1,0:T(8,128)(2,1)S(1)} %get-tuple-element.28.refs_4_), channel_id=1, source_target_pairs={{0,72},{1,73},{64,0},{65,1},{8,64},{9,65},{72,8},{73,9},{16,88},{1... | collective-permute-start | bytes 393224 | tf_op jit(solution)/shard_map/keys_over_z/ppermute | solution.py:40
  20.3 12.8 %collective-permute-start.5 = (bf16[528,256]{1,0:T(8,128)(2,1)S(1)}, bf16[528,256]{1,0:T(8,128)(2,1)S(1)}, u32[]{:S(2)}, u32[]{:S(2)}) collective-permute-start(bf16[528,256]{1,0:T(8,128)(2,1)S(1)} %get-tuple-element.27.refs_0_), channel_id=1, source_target_pairs={{0,4},{1,5},{64,68},{65,69},{8,12},{9,13},{72,76},{73,77},{16,20},... | collective-permute-start | bytes 811016 | tf_op jit(solution)/shard_map/queries_over_x/ppermute | solution.py:40
  23.3 12.7 %collective-permute-start.4 = (bf16[528,256]{1,0:T(8,128)(2,1)S(1)}, bf16[528,256]{1,0:T(8,128)(2,1)S(1)}, u32[]{:S(2)}, u32[]{:S(2)}) collective-permute-start(bf16[528,256]{1,0:T(8,128)(2,1)S(1)} %get-tuple-element.27.refs_0_), channel_id=1, source_target_pairs={{0,6},{1,7},{64,70},{65,71},{8,14},{9,15},{72,78},{73,79},{16,22},... | collective-permute-start | bytes 811016 | tf_op jit(solution)/shard_map/queries_over_x/ppermute | solution.py:40
  24.5 11.5 %collective-permute-start.3 = (bf16[528,256]{1,0:T(8,128)(2,1)S(1)}, bf16[528,256]{1,0:T(8,128)(2,1)S(1)}, u32[]{:S(2)}, u32[]{:S(2)}) collective-permute-start(bf16[528,256]{1,0:T(8,128)(2,1)S(1)} %get-tuple-element.27.refs_0_), channel_id=1, source_target_pairs={{0,2},{1,3},{64,66},{65,67},{8,10},{9,11},{72,74},{73,75},{16,18},... | collective-permute-start | bytes 811016 | tf_op jit(solution)/shard_map/queries_over_x/ppermute | solution.py:40
  25.4 6.2 %collective-permute-start.6 = (bf16[256,256]{1,0:T(8,128)(2,1)S(1)}, bf16[256,256]{1,0:T(8,128)(2,1)S(1)}, u32[]{:S(2)}, u32[]{:S(2)}) collective-permute-start(bf16[256,256]{1,0:T(8,128)(2,1)S(1)} %get-tuple-element.28.refs_4_), channel_id=1, source_target_pairs={{0,64},{1,65},{64,8},{65,9},{8,72},{9,73},{72,0},{73,1},{16,80},{1... | collective-permute-start | bytes 393224 | tf_op jit(solution)/shard_map/keys_over_z/ppermute | solution.py:40
  27.3 4.3 %collective-permute-start.12 = (bf16[256,256]{1,0:T(8,128)(2,1)S(1)}, bf16[256,256]{1,0:T(8,128)(2,1)S(1)}, u32[]{:S(2)}, u32[]{:S(2)}) collective-permute-start(bf16[256,256]{1,0:T(8,128)(2,1)S(1)} %collective-permute-done.8.refs_7_), channel_id=1, source_target_pairs={{0,1},{1,0},{64,65},{65,64},{8,9},{9,8},{72,73},{73,72},{16,17},{1... | collective-permute-start | bytes 393224 | tf_op jit(solution)/shard_map/keys_over_z/ppermute | solution.py:40
  31.5 1.3 %collective-permute-start.11 = (bf16[256,256]{1,0:T(8,128)(2,1)S(1)}, bf16[256,256]{1,0:T(8,128)(2,1)S(1)}, u32[]{:S(2)}, u32[]{:S(2)}) collective-permute-start(bf16[256,256]{1,0:T(8,128)(2,1)S(1)} %collective-permute-done.7.refs_6_), channel_id=1, source_target_pairs={{0,1},{1,0},{64,65},{65,64},{8,9},{9,8},{72,73},{73,72},{16,17},{1... | collective-permute-start | bytes 393224 | tf_op jit(solution)/shard_map/keys_over_z/ppermute | solution.py:40
  31.5 1.5 %collective-permute-start.10 = (bf16[256,256]{1,0:T(8,128)(2,1)S(1)}, bf16[256,256]{1,0:T(8,128)(2,1)S(1)}, u32[]{:S(2)}, u32[]{:S(2)}) collective-permute-start(bf16[256,256]{1,0:T(8,128)(2,1)S(1)} %collective-permute-done.6.refs_5_), channel_id=1, source_target_pairs={{0,1},{1,0},{64,65},{65,64},{8,9},{9,8},{72,73},{73,72},{16,17},{1... | collective-permute-start | bytes 393224 | tf_op jit(solution)/shard_map/keys_over_z/ppermute | solution.py:40
  49.6 5.1 %collective-permute-start.16 = (bf16[1024,256]{1,0:T(8,128)(2,1)S(1)}, bf16[1024,256]{1,0:T(8,128)(2,1)S(1)}, u32[]{:S(2)}, u32[]{:S(2)}) collective-permute-start(bf16[1024,256]{1,0:T(8,128)(2,1)S(1)} %get-tuple-element.34), channel_id=1, source_target_pairs={{0,1},{1,0},{64,65},{65,64},{8,9},{9,8},{72,73},{73,72},{16,17},{1... | collective-permute-start | bytes 1572872 | tf_op jit(solution)/shard_map/sum_keys_over_core/ppermute | solution.py:40
  49.7 7.2 %collective-permute-start.13 = (bf16[512,128]{1,0:T(8,128)(2,1)S(1)}, bf16[512,128]{1,0:T(8,128)(2,1)S(1)}, u32[]{:S(2)}, u32[]{:S(2)}) collective-permute-start(bf16[512,128]{1,0:T(8,128)(2,1)S(1)} %get-tuple-element.30), channel_id=1, source_target_pairs={{0,6},{1,7},{64,70},{65,71},{8,14},{9,15},{72,78},{73,79},{16,22},... | collective-permute-start | bytes 393224 | tf_op jit(solution)/shard_map/sum_queries_over_x/ppermute | solution.py:40
  52.4 9.6 %collective-permute-start.14 = (bf16[512,128]{1,0:T(8,128)(2,1)S(1)}, bf16[512,128]{1,0:T(8,128)(2,1)S(1)}, u32[]{:S(2)}, u32[]{:S(2)}) collective-permute-start(bf16[512,128]{1,0:T(8,128)(2,1)S(1)} %get-tuple-element.31), channel_id=1, source_target_pairs={{0,2},{1,3},{64,66},{65,67},{8,10},{9,11},{72,74},{73,75},{16,18},... | collective-permute-start | bytes 393224 | tf_op jit(solution)/shard_map/sum_queries_over_x/ppermute | solution.py:40
  52.4 9.6 %collective-permute-start.15 = (bf16[512,128]{1,0:T(8,128)(2,1)S(1)}, bf16[512,128]{1,0:T(8,128)(2,1)S(1)}, u32[]{:S(2)}, u32[]{:S(2)}) collective-permute-start(bf16[512,128]{1,0:T(8,128)(2,1)S(1)} %get-tuple-element.32), channel_id=1, source_target_pairs={{0,4},{1,5},{64,68},{65,69},{8,12},{9,13},{72,76},{73,77},{16,20},... | collective-permute-start | bytes 393224 | tf_op jit(solution)/shard_map/sum_queries_over_x/ppermute | solution.py:40
  54.8 7.2 %collective-permute-start.17 = (bf16[256,256]{1,0:T(8,128)(2,1)S(1)}, bf16[256,256]{1,0:T(8,128)(2,1)S(1)}, u32[]{:S(2)}, u32[]{:S(2)}) collective-permute-start(bf16[256,256]{1,0:T(8,128)(2,1)S(1)} %get-tuple-element.36), channel_id=1, source_target_pairs={{0,72},{1,73},{64,0},{65,1},{8,64},{9,65},{72,8},{73,9},{16,88},{1... | collective-permute-start | bytes 393224 | tf_op jit(solution)/shard_map/sum_keys_over_z/ppermute | solution.py:40
  55.1 7.2 %collective-permute-start.18 = (bf16[256,256]{1,0:T(8,128)(2,1)S(1)}, bf16[256,256]{1,0:T(8,128)(2,1)S(1)}, u32[]{:S(2)}, u32[]{:S(2)}) collective-permute-start(bf16[256,256]{1,0:T(8,128)(2,1)S(1)} %get-tuple-element.37), channel_id=1, source_target_pairs={{0,64},{1,65},{64,8},{65,9},{8,72},{9,73},{72,0},{73,1},{16,80},{1... | collective-permute-start | bytes 393224 | tf_op jit(solution)/shard_map/sum_keys_over_z/ppermute | solution.py:40
  56.9 7.9 %collective-permute-start.19 = (bf16[256,256]{1,0:T(8,128)(2,1)S(1)}, bf16[256,256]{1,0:T(8,128)(2,1)S(1)}, u32[]{:S(2)}, u32[]{:S(2)}) collective-permute-start(bf16[256,256]{1,0:T(8,128)(2,1)S(1)} %get-tuple-element.38), channel_id=1, source_target_pairs={{0,8},{1,9},{64,72},{65,73},{8,0},{9,1},{72,64},{73,65},{16,24},{1... | collective-permute-start | bytes 393224 | tf_op jit(solution)/shard_map/sum_keys_over_z/ppermute | solution.py:40
  64.9 4.3 %collective-permute-start.20 = (bf16[128,256]{1,0:T(8,128)(2,1)S(1)}, bf16[128,256]{1,0:T(8,128)(2,1)S(1)}, u32[]{:S(2)}, u32[]{:S(2)}) collective-permute-start(bf16[128,256]{1,0:T(8,128)(2,1)S(1)} %get-tuple-element.40), channel_id=1, source_target_pairs={{0,48},{1,49},{64,112},{65,113},{8,56},{9,57},{72,120},{73,121},{1... | collective-permute-start | bytes 196616 | tf_op jit(solution)/shard_map/back_over_y/ppermute | solution.py:40
  67.2 5.8 %collective-permute-start.21 = (bf16[128,256]{1,0:T(8,128)(2,1)S(1)}, bf16[128,256]{1,0:T(8,128)(2,1)S(1)}, u32[]{:S(2)}, u32[]{:S(2)}) collective-permute-start(bf16[128,256]{1,0:T(8,128)(2,1)S(1)} %get-tuple-element.41), channel_id=1, source_target_pairs={{0,32},{1,33},{64,96},{65,97},{8,40},{9,41},{72,104},{73,105},{16,... | collective-permute-start | bytes 196616 | tf_op jit(solution)/shard_map/back_over_y/ppermute | solution.py:40
  68.2 5.5 %collective-permute-start.22 = (bf16[128,256]{1,0:T(8,128)(2,1)S(1)}, bf16[128,256]{1,0:T(8,128)(2,1)S(1)}, u32[]{:S(2)}, u32[]{:S(2)}) collective-permute-start(bf16[128,256]{1,0:T(8,128)(2,1)S(1)} %get-tuple-element.42), channel_id=1, source_target_pairs={{0,16},{1,17},{64,80},{65,81},{8,24},{9,25},{72,88},{73,89},{16,32... | collective-permute-start | bytes 196616 | tf_op jit(solution)/shard_map/back_over_y/ppermute | solution.py:40
  (5 other events, 4.2 us)

commit v2 on v1

v2 whole, which is shorter than its diff:
```python
import functools
import math

import jax
import jax.numpy as jnp
from jax import lax
from jax.experimental import pallas as pl
from jax.experimental.pallas import tpu as pltpu
from jax.sharding import PartitionSpec as P

H = 4
DH = 128
AXES = ("row", "col")
F32 = jnp.float32
BF16 = jnp.bfloat16
QR = 128
KR = 64
AUX = 16
TILE = 512
BLK = QR + KR + AUX
QS = 4 * QR
KS = 4 * KR
FACTOR = 1.0 / math.sqrt(DH)
LOG2E = math.log2(math.e)
VMEM = pl.BlockSpec(memory_space=pltpu.VMEM)
NT = (((1,), (1,)), ((), ()))


def linear(x, y, z, c):
    return ((z % 2) * 4 + y) * 16 + (z // 2) * 8 + x * 2 + c


def move(value, target):
    pairs = []
    for x in range(4):
        for y in range(4):
            for z in range(4):
                for c in range(2):
                    pairs.append((linear(x, y, z, c), linear(*target(x, y, z, c))))
    return lax.ppermute(value, AXES, pairs)


def other_core(value):
    return move(value, lambda x, y, z, c: (x, y, z, 1 - c))


def along_y(value, step):
    return move(value, lambda x, y, z, c: (x, (y + step) % 4, z, c))


def partner(place, core, kind):
    if kind == 2:
        return (place + 2) % 4
    up = place % 2 == (kind + core) % 2
    return (place + (1 if up else -1)) % 4


def swap_x(value, kind):
    return move(value, lambda x, y, z, c: (partner(x, c, kind), y, z, c))


def swap_z(value, kind):
    return move(value, lambda x, y, z, c: (x, y, partner(z, c, kind), c))


def three_parts(value):
    high = value.astype(BF16).astype(F32)
    rest = value - high
    middle = rest.astype(BF16).astype(F32)
    return [high, middle, rest - middle]


def pack_kernel(steps, *refs):
    blocks, bufs, sem = refs[6:-7], refs[-7:-1], refs[-1]
    copies = [pltpu.make_async_copy(refs[i], bufs[i], sem.at[i]) for i in range(6)]
    for copy in copies:
        copy.start()
    for copy in copies:
        copy.wait()
    q_ref, k_ref, v_ref, o_ref, g_ref, lse_ref = bufs
    y = lax.axis_index("row") % 4
    for step, block in zip(steps, blocks):
        head = lax.rem(y + step, 4)
        cols = pl.ds(pl.multiple_of(head * DH, DH), DH)
        g = g_ref[:, cols]
        block[:QR, :DH] = q_ref[:, cols]
        block[:QR, DH:] = g
        block[QR : QR + KR, :DH] = k_ref[:, cols]
        block[QR : QR + KR, DH:] = v_ref[:, cols]
        product = g.astype(F32) * o_ref[:, cols].astype(F32)
        delta = jnp.sum(product.T, axis=0, keepdims=True)
        both = jnp.concatenate([lse_ref[pl.ds(head, 1), :], delta], axis=1)
        rows = three_parts(both) + [jnp.zeros((AUX - 3, 2 * DH), F32)]
        block[QR + KR :, :] = jnp.concatenate(rows, axis=0).astype(BF16)


def copy_kernel(source, out):
    out[...] = source[...]


def join_kernel(b2, b0, b1, b3, q_out, kv_out):
    aux = []
    for j, block in enumerate((b0, b1, b2, b3)):
        q_out[j * QR : (j + 1) * QR, :] = block[:QR, :]
        kv_out[j * KR : (j + 1) * KR, :] = block[QR : QR + KR, :]
        aux.append(block[QR + KR :, :].astype(F32)[:3])
    aux.append(jnp.zeros((AUX - 12, 2 * DH), F32))
    q_out[QS:, :] = jnp.concatenate(aux, axis=0).astype(BF16)


def load_queries(blocks, q_all, terms):
    for b, block in enumerate(blocks):
        q_all[b * QS : (b + 1) * QS, :] = block[:QS, :]
        aux = block[QS:, :].astype(F32)
        for j in range(4):
            total = aux[3 * j : 3 * j + 1] + aux[3 * j + 1 : 3 * j + 2] + aux[3 * j + 2 : 3 * j + 3]
            cols = slice(b * QS + j * QR, b * QS + (j + 1) * QR)
            terms[0:1, cols] = total[:, :DH] * LOG2E
            terms[1:2, cols] = total[:, DH:]


def tile_terms(q_all, kv, terms, p_all, ds_all):
    for first in range(0, 2 * QS, QS):
        cols = slice(first, first + QS)
        q, g = q_all[cols, :DH], q_all[cols, DH:]
        s = lax.dot_general(kv[:, :DH], q, NT, preferred_element_type=F32)
        p = jnp.exp2(s * (FACTOR * LOG2E) - terms[0:1, cols])
        dp = lax.dot_general(kv[:, DH:], g, NT, preferred_element_type=F32)
        p_all[:, cols] = p.astype(BF16)
        ds_all[:, cols] = (p * (dp - terms[1:2, cols]) * FACTOR).astype(BF16)
    dv = jnp.dot(p_all[...], q_all[:, DH:], preferred_element_type=F32)
    dk = jnp.dot(ds_all[...], q_all[:, :DH], preferred_element_type=F32)
    dq = jnp.dot(kv[:, :DH].T, ds_all[...], preferred_element_type=F32)
    return dk, dv, dq


def attend_kernel(tiles, old_q, old_kv, *refs):
    refs = list(refs)
    pieces = [refs.pop(0) for _ in range(2 * tiles)]
    blocks = [refs.pop(0) for _ in range(2)]
    dq_old = refs.pop(0) if old_q else None
    dkv_old = [refs.pop(0) for _ in range(tiles)] if old_kv else None
    dkv_out = [refs.pop(0) for _ in range(tiles)]
    q_all, kv, terms, p_all, ds_all = refs[-5:]
    dq_out = refs[:-5]
    load_queries(blocks, q_all, terms)
    total = dq_old[...] if old_q else None
    for i in range(tiles):
        kv[i, :KS, :] = pieces[2 * i][...]
        kv[i, KS:, :] = pieces[2 * i + 1][...]
        dk, dv, dq = tile_terms(q_all, kv.at[i], terms, p_all, ds_all)
        if old_kv:
            dk = dk + dkv_old[i][:, :DH]
            dv = dv + dkv_old[i][:, DH:]
        dkv_out[i][:, :DH] = dk.astype(dkv_out[i].dtype)
        dkv_out[i][:, DH:] = dv.astype(dkv_out[i].dtype)
        total = dq if total is None else total + dq
    if len(dq_out) == 1:
        dq_out[0][...] = total
    else:
        for b, out in enumerate(dq_out):
            out[...] = total[:, b * QS : (b + 1) * QS].T.astype(out.dtype)


def add_kernel(a, b, out):
    out[...] = (a[...].astype(F32) + b[...].astype(F32)).astype(out.dtype)


def split_kernel(*refs):
    own, passed = refs[-2:]
    half = own.shape[0]
    for rows, out in ((slice(0, half), own), (slice(half, 2 * half), passed)):
        total = refs[0][rows, :]
        for ref in refs[1:-2]:
            total = total + ref[rows, :].astype(F32)
        out[...] = total.astype(out.dtype)


def chip_sum_kernel(q23, q0, k0, q1, k1, *outs):
    dq = q0[...] + q1[...].astype(F32) + q23[...]
    dkv = k0[...] + k1[...].astype(F32)
    for j, out in enumerate(outs):
        part = dq[j * QR : (j + 1) * QR]
        wide = jnp.concatenate([part[: QR // 2], part[QR // 2 :]], axis=1)
        out[:KR, :] = wide.astype(out.dtype)
        out[KR:, :] = dkv[j * KR : (j + 1) * KR].astype(out.dtype)


def unpack_kernel(b2, b0, b1, b3, dq, dk, dv):
    y = lax.axis_index("row") % 4
    for j, block in enumerate((b0, b1, b2, b3)):
        cols = pl.ds(pl.multiple_of(lax.rem(y + j, 4) * DH, DH), DH)
        dq[: QR // 2, cols] = block[:KR, :DH].astype(F32)
        dq[QR // 2 :, cols] = block[:KR, DH:].astype(F32)
        dk[:, cols] = block[KR:, :DH].astype(F32)
        dv[:, cols] = block[KR:, DH:].astype(F32)


def call(kernel, outs, args, scratch=(), flops=0, space=VMEM, limit=40):
    total = sum(a.size * a.dtype.itemsize for a in args) + sum(
        math.prod(shape) * jnp.dtype(kind).itemsize for shape, kind in outs
    )
    return pl.pallas_call(
        kernel,
        out_shape=[jax.ShapeDtypeStruct(shape, kind) for shape, kind in outs],
        in_specs=[space] * len(args),
        out_specs=[VMEM] * len(outs),
        scratch_shapes=list(scratch),
        compiler_params=pltpu.CompilerParams(vmem_limit_bytes=limit * 1024 * 1024),
        cost_estimate=pl.CostEstimate(flops=flops, bytes_accessed=total, transcendentals=0),
    )(*args)


def attend(blocks, tiles, dq_old, dkv_old, dq_out, dkv_out):
    args = [piece for tile in tiles for piece in tile] + [*blocks]
    args += ([] if dq_old is None else [dq_old]) + list(dkv_old or ())
    rows = 2 * QS
    outs = call(
        functools.partial(attend_kernel, len(tiles), dq_old is not None, dkv_old is not None),
        [((TILE, 2 * DH), kind) for kind in dkv_out] + dq_out,
        args,
        scratch=[
            pltpu.VMEM((rows, 2 * DH), BF16),
            pltpu.VMEM((len(tiles), TILE, 2 * DH), BF16),
            pltpu.VMEM((8, rows), F32),
            pltpu.VMEM((TILE, rows), BF16),
            pltpu.VMEM((TILE, rows), BF16),
        ],
        flops=10 * rows * TILE * len(tiles) * DH,
    )
    return outs[len(tiles) :], outs[: len(tiles)]


def per_device(queries, keys, values, outputs, d_out, lse):
    args = (queries, keys, values, outputs, d_out, lse)
    with jax.named_scope("pack"):
        scratch = [pltpu.VMEM(a.shape, a.dtype) for a in args] + [pltpu.SemaphoreType.DMA((6,))]
        place = pl.BlockSpec(memory_space=pltpu.HBM)
        far, plus, minus = call(
            functools.partial(pack_kernel, (2, 1, 3)),
            [((BLK, 2 * DH), BF16)] * 3,
            args,
            scratch=scratch,
            space=place,
            limit=56,
        )
        here = call(
            functools.partial(pack_kernel, (0,)),
            [((BLK, 2 * DH), BF16)],
            args,
            scratch=scratch,
            space=place,
            limit=56,
        )[0]
        here = call(copy_kernel, [((BLK, 2 * DH), BF16)], (here,))[0]
    with jax.named_scope("heads_over_y"):
        blocks = [along_y(far, 2), here, along_y(plus, 1), along_y(minus, 3)]
    with jax.named_scope("join"):
        q, kv = call(join_kernel, [((QS + AUX, 2 * DH), BF16), ((KS, 2 * DH), BF16)], blocks)
    with jax.named_scope("queries_over_x"):
        q1 = swap_x(q, 0)
        q2 = swap_x(q, 1)
        q3 = swap_x(q1, 1)
    with jax.named_scope("keys_over_z"):
        near = [(kv, swap_z(kv, 0)), (swap_z(kv, 1), swap_z(kv, 2))]
        k_a, k_b = near
        o_a, o_b = [tuple(other_core(piece) for piece in pair) for pair in near]
    sums = [((DH, 2 * QS), F32)]
    q_a = (q, q1)
    q2, k_b = lax.optimization_barrier((q2, k_b))
    with jax.named_scope("attend_a_b"):
        (dq_a,), (dkv_b,) = attend(q_a, (k_b,), None, None, sums, (F32,))
        (dq_a,), (dko_b,) = attend(q_a, (o_b,), dq_a, None, sums, (F32,))
    with jax.named_scope("attend_a_a_other"):
        (dq_a,), (dko_a,) = attend(q_a, (o_a,), dq_a, None, sums, (F32,))
    q3, dq_a = lax.optimization_barrier((q3, dq_a))
    q_b = (q2, q3)
    with jax.named_scope("attend_b_b"):
        (dq_b,), (dko_b, dkv_b) = attend(q_b, (o_b, k_b), None, (dko_b, dkv_b), sums, (BF16, F32))
    with jax.named_scope("sum_keys_over_core"):
        sent_b = call(add_kernel, [((TILE, 2 * DH), BF16)], (dkv_b, other_core(dko_b)))[0]
    with jax.named_scope("attend_b_a_other"):
        (dq_b,), (dko_a,) = attend(q_b, (o_a,), dq_b, (dko_a,), sums, (BF16,))
    dq_b, sent_b = lax.optimization_barrier((dq_b, sent_b))
    with jax.named_scope("attend_b_a"):
        (dq2, dq3), (dkv_a,) = attend(q_b, (k_a,), dq_b, None, [((QS, DH), BF16)] * 2, (F32,))
    with jax.named_scope("sum_queries_over_x"):
        got2, got3 = swap_x(dq2, 1), swap_x(dq3, 2)
    with jax.named_scope("sum_keys_over_z"):
        got_b = swap_z(sent_b, 1)
    with jax.named_scope("sum_keys_over_core"):
        got_other = other_core(dko_a)
    with jax.named_scope("attend_a_a"):
        (dq0, dq1), (dkv_own,) = attend(
            q_a, (k_a,), dq_a, (dkv_a,), [((QS, DH), F32), ((QS, DH), BF16)], (F32,)
        )
    with jax.named_scope("sum_queries_over_x"):
        got1 = swap_x(dq1, 0)
        got23 = call(add_kernel, [((QS, DH), F32)], (got2, got3), flops=4 * 10**9)[0]
    with jax.named_scope("sum_keys_over_z"):
        k_own, k_sent = call(
            split_kernel, [((KS, 2 * DH), F32), ((KS, 2 * DH), BF16)], (dkv_own, got_other, got_b)
        )
        k_got = swap_z(k_sent, 0)
    with jax.named_scope("chip_sum"):
        backs = call(
            chip_sum_kernel,
            [((2 * KR, 2 * DH), F32)] + [((2 * KR, 2 * DH), BF16)] * 3,
            (got23, dq0, k_own, got1, k_got),
        )
    with jax.named_scope("back_over_y"):
        far = along_y(backs[2], 2)
        backs = [far, backs[0], along_y(backs[1], 3), along_y(backs[3], 1)]
    with jax.named_scope("unpack"):
        return tuple(
            call(
                unpack_kernel,
                [((QR, H * DH), F32), ((KR, H * DH), F32), ((KR, H * DH), F32)],
                backs,
            )
        )


def solution(mesh):
    return jax.shard_map(
        per_device,
        mesh=mesh,
        in_specs=(
            P(("row", "col"), None),
            P(("col", "row"), None),
            P(("col", "row"), None),
            P(("row", "col"), None),
            P(("row", "col"), None),
            P(None, ("row", "col")),
        ),
        out_specs=(P(("row", "col"), None), P(("col", "row"), None), P(("col", "row"), None)),
        check_vma=False,
    )
```

time: 75 us -> 61.7 us (0.82)
  waiting for transfers between devices: 22.7 us -> 14 us
  local copies, waits for them, and re-layouts: 5.06 us -> 0.89 us
  starting transfers between devices: 31.2 us -> 28.9 us
  Pallas kernels: 14.9 us -> 16.8 us
    ppermute x23, waiting for transfers between devices: 22.7 us -> 14 us  [move(): return lax.ppermute(value, AXES, pairs)]
    unnamed x12 -> x2, local copies, waits for them, and re-layouts: 5.06 us -> 0.89 us
    ppermute x23, starting transfers between devices: 31.2 us -> 28.9 us  [move(): return lax.ppermute(value, AXES, pairs)]
    pallas_call x6 -> x16, Pallas kernels: 14.9 us -> 16.8 us  [call(): pl.pallas_call(kernel, out_shape=[jax.ShapeDtypeStruct(shape, kind) for s...]
  transfers between devices with their start and end apart: 23 -> 23, of which waited for: 13 -> 9; matrix products, arithmetic and copies ran while one was open for 0% -> 0% of each run, Pallas kernels for 0% -> 18%
where the time goes in v2:
time: 61.7 us; the launch traced here: 61.4 us
  starting transfers between devices  28.9 us (47%)
  Pallas kernels  16.8 us (27%)
  waiting for transfers between devices  14 us (23%)
  local copies, waits for them, and re-layouts  0.89 us (1%)
  between operations  0.81 us (1%)
    ppermute x23, starting transfers between devices, move(): return lax.ppermute(value, AXES, pairs)  28.9 us
    pallas_call x16, Pallas kernels, call(): pl.pallas_call(kernel, out_shape=[jax.ShapeDtypeStruct(shape, kind) for s...  16.8 us
    ppermute x23, waiting for transfers between devices, move(): return lax.ppermute(value, AXES, pairs)  14 us
  transfers between devices with their start and end apart: 23, of which 9 were waited for; matrix products, arithmetic and copies ran while one was open for 0% of the time, Pallas kernels for 18%

profile of v2, /device:TPU:0, one launch (start us, length us, event | category | flops | bytes accessed | tf_op | source)
XLA Modules:
  0.0 61.4 jit_solution(15679702132920776818)
XLA Ops:
  0.6 2.0 %pack.3 = (bf16[208,256]{1,0:T(8,128)(2,1)}, bf16[208,256]{1,0:T(8,128)(2,1)}, bf16[208,256]{1,0:T(8,128)(2,1)}) custom-call(bf16[128,512]{1,0:T(8,128)(2,1)} %refs_0_.3, bf16[64,512]{1,0:T(8,128)(2,1)} %refs_1_.3, bf16[64,512]{1,0:T(8,128)(2,1)} %refs_2_.3, bf16[128,512]{1,0:T(8,128)(2,1)} %refs_3_.3, bf16[128,512]{1,0:T(8,128)(2,1)} %refs_4_.3, ...), custom_call_target="tpu_custom_call" | custom-call | bytes 845824 | tf_op jit(solution)/shard_map/pack/pallas_call | solution.py:203
  2.6 3.4 %collective-permute-start = (bf16[208,256]{1,0:T(8,128)(2,1)}, bf16[208,256]{1,0:T(8,128)(2,1)S(1)}, u32[]{:S(2)}, u32[]{:S(2)}) collective-permute-start(bf16[208,256]{1,0:T(8,128)(2,1)} %get-tuple-element.38), channel_id=1, source_target_pairs={{0,32},{1,33},{64,96},{65,97},{8,40},{9,41},{72,104},{73,105},{16,... | collective-permute-start | bytes 319496 | tf_op jit(solution)/shard_map/heads_over_y/ppermute | solution.py:40
  6.7 2.6 %collective-permute-start.2 = (bf16[208,256]{1,0:T(8,128)(2,1)}, bf16[208,256]{1,0:T(8,128)(2,1)S(1)}, u32[]{:S(2)}, u32[]{:S(2)}) collective-permute-start(bf16[208,256]{1,0:T(8,128)(2,1)} %get-tuple-element.40), channel_id=1, source_target_pairs={{0,48},{1,49},{64,112},{65,113},{8,56},{9,57},{72,120},{73,121},{1... | collective-permute-start | bytes 319496 | tf_op jit(solution)/shard_map/heads_over_y/ppermute | solution.py:40
  9.2 1.9 %pack.4.source = bf16[208,256]{1,0:T(8,128)(2,1)} custom-call(bf16[128,512]{1,0:T(8,128)(2,1)} %refs_0_.3, bf16[64,512]{1,0:T(8,128)(2,1)} %refs_1_.3, bf16[64,512]{1,0:T(8,128)(2,1)} %refs_2_.3, bf16[128,512]{1,0:T(8,128)(2,1)} %refs_3_.3, bf16[128,512]{1,0:T(8,128)(2,1)} %refs_4_.3, f32[4,128]{1,0:T(4,128)} %refs_5_.3), custom_call_target="tpu_custom_call" | custom-call | bytes 632832 | tf_op jit(solution)/shard_map/pack/pallas_call | solution.py:203
  12.2 1.6 %collective-permute-start.7 = (bf16[528,256]{1,0:T(8,128)(2,1)S(1)}, bf16[528,256]{1,0:T(8,128)(2,1)S(1)}, u32[]{:S(2)}, u32[]{:S(2)}) collective-permute-start(bf16[528,256]{1,0:T(8,128)(2,1)S(1)} %get-tuple-element.42.refs_2_), channel_id=1, source_target_pairs={{0,2},{1,7},{64,66},{65,71},{8,10},{9,15},{72,74},{73,79},{16,18},... | collective-permute-start | bytes 811016 | tf_op jit(solution)/shard_map/queries_over_x/ppermute | solution.py:40
  13.7 2.1 %collective-permute-start.4 = (bf16[528,256]{1,0:T(8,128)(2,1)S(1)}, bf16[528,256]{1,0:T(8,128)(2,1)S(1)}, u32[]{:S(2)}, u32[]{:S(2)}) collective-permute-start(bf16[528,256]{1,0:T(8,128)(2,1)S(1)} %get-tuple-element.42.refs_2_), channel_id=1, source_target_pairs={{0,6},{1,3},{64,70},{65,67},{8,14},{9,11},{72,78},{73,75},{16,22},... | collective-permute-start | bytes 811016 | tf_op jit(solution)/shard_map/queries_over_x/ppermute | solution.py:40
  15.8 3.9 %collective-permute-start.6 = (bf16[256,256]{1,0:T(8,128)(2,1)S(1)}, bf16[256,256]{1,0:T(8,128)(2,1)S(1)}, u32[]{:S(2)}, u32[]{:S(2)}) collective-permute-start(bf16[256,256]{1,0:T(8,128)(2,1)S(1)} %get-tuple-element.41.refs_0_), channel_id=1, source_target_pairs={{0,8},{1,9},{64,72},{65,73},{8,0},{9,1},{72,64},{73,65},{16,24},{1... | collective-permute-start | bytes 393224 | tf_op jit(solution)/shard_map/keys_over_z/ppermute | solution.py:40
  23.0 2.9 %collective-permute-done.5.refs_0_.refs_2_ = bf16[256,256]{1,0:T(8,128)(2,1)S(1)} collective-permute-done((bf16[256,256]{1,0:T(8,128)(2,1)S(1)}, bf16[256,256]{1,0:T(8,128)(2,1)S(1)}, u32[]{:S(2)}, u32[]{:S(2)}) %collective-permute-start.5) | collective-permute-done | bytes 131104 | tf_op jit(solution)/shard_map/keys_over_z/ppermute | solution.py:40
  26.5 1.4 %attend_a_b.2 = (f32[512,256]{1,0:T(8,128)S(1)}, f32[128,1024]{1,0:T(8,128)S(1)}) custom-call(bf16[256,256]{1,0:T(8,128)(2,1)S(1)} %collective-permute-done.5.refs_0_.refs_2_, bf16[256,256]{1,0:T(8,128)(2,1)S(1)} %collective-permute-done.6.refs_1_.refs_3_, bf16[528,256]{1,0:T(8,128)(2,1)S(1)} %get-tuple-element.42.refs_2_, ...), custom_call_target="tpu_custom_call" | custom-call | flops 671088640 | bytes 1851392 | tf_op jit(solution)/shard_map/attend_a_b/pallas_call | solution.py:203
  28.0 1.5 %attend_a_b.3 = (f32[512,256]{1,0:T(8,128)S(1)}, f32[128,1024]{1,0:T(8,128)S(1)}) custom-call(bf16[256,256]{1,0:T(8,128)(2,1)S(1)} %collective-permute-done.11.refs_0_, bf16[256,256]{1,0:T(8,128)(2,1)S(1)} %collective-permute-done.12.refs_1_, bf16[528,256]{1,0:T(8,128)(2,1)S(1)} %get-tuple-element.42.refs_2_, ...), custom_call_target="tpu_custom_call" | custom-call | flops 671088640 | bytes 2375680 | tf_op jit(solution)/shard_map/attend_a_b/pallas_call | solution.py:203
  29.5 1.5 %attend_a_a_other.1 = (f32[512,256]{1,0:T(8,128)S(1)}, f32[128,1024]{1,0:T(8,128)S(1)}) custom-call(bf16[256,256]{1,0:T(8,128)(2,1)S(1)} %collective-permute-done.9.refs_0_, bf16[256,256]{1,0:T(8,128)(2,1)S(1)} %collective-permute-done.10.refs_1_, bf16[528,256]{1,0:T(8,128)(2,1)S(1)} %get-tuple-element.42.refs_2_, ...), custom_call_target="tpu_custom_call" | custom-call | flops 671088640 | bytes 2375680 | tf_op jit(solution)/shard_map/attend_a_a_other/pallas_call | solution.py:203
  30.9 2.8 %attend_b_b.1 = (bf16[512,256]{1,0:T(8,128)(2,1)S(1)}, f32[512,256]{1,0:T(8,128)S(1)}, f32[128,1024]{1,0:T(8,128)S(1)}) custom-call(bf16[256,256]{1,0:T(8,128)(2,1)S(1)} %collective-permute-done.11.refs_0_, bf16[256,256]{1,0:T(8,128)(2,1)S(1)} %collective-permute-done.12.refs_1_, bf16[256,256]{1,0:T(8,128)(2,1)S(1)} %collective-permute-done.5.refs_0_.refs_2_, ...), custom_call_target="tpu_custom_call" | custom-call | flops 1342177280 | bytes 3424256 | tf_op jit(solution)/shard_map/attend_b_b/pallas_call | solution.py:203
  34.4 1.5 %attend_b_a_other.1 = (bf16[512,256]{1,0:T(8,128)(2,1)S(1)}, f32[128,1024]{1,0:T(8,128)S(1)}) custom-call(bf16[256,256]{1,0:T(8,128)(2,1)S(1)} %collective-permute-done.9.refs_0_, bf16[256,256]{1,0:T(8,128)(2,1)S(1)} %collective-permute-done.10.refs_1_, bf16[528,256]{1,0:T(8,128)(2,1)S(1)} %collective-permute-done.4.refs_4_.refs_2_, ...), custom_call_target="tpu_custom_call" | custom-call | flops 671088640 | bytes 2637824 | tf_op jit(solution)/shard_map/attend_b_a_other/pallas_call | solution.py:203
  36.2 2.0 %collective-permute-start.17 = (bf16[512,256]{1,0:T(8,128)(2,1)S(1)}, bf16[512,256]{1,0:T(8,128)(2,1)S(1)}, u32[]{:S(2)}, u32[]{:S(2)}) collective-permute-start(bf16[512,256]{1,0:T(8,128)(2,1)S(1)} %sum_keys_over_core.1), channel_id=1, source_target_pairs={{0,72},{1,65},{64,8},{65,1},{8,64},{9,73},{72,0},{73,9},{16,88},{1... | collective-permute-start | bytes 786440 | tf_op jit(solution)/shard_map/sum_keys_over_z/ppermute | solution.py:40
  38.3 1.5 %attend_b_a.1 = (f32[512,256]{1,0:T(8,128)S(1)}, bf16[512,128]{1,0:T(8,128)(2,1)S(1)}, bf16[512,128]{1,0:T(8,128)(2,1)S(1)}) custom-call(bf16[256,256]{1,0:T(8,128)(2,1)S(1)} %get-tuple-element.41.refs_0_, bf16[256,256]{1,0:T(8,128)(2,1)S(1)} %collective-permute-done.3.refs_1_, bf16[528,256]{1,0:T(8,128)(2,1)S(1)} %collective-permute-done.4.refs_4_.refs_2_, ...), custom_call_target="tpu_custom_call" | custom-call | flops 671088640 | bytes 2113536 | tf_op jit(solution)/shard_map/attend_b_a/pallas_call | solution.py:203
  39.8 1.5 %collective-permute-start.14 = (bf16[512,128]{1,0:T(8,128)(2,1)S(1)}, bf16[512,128]{1,0:T(8,128)(2,1)S(1)}, u32[]{:S(2)}, u32[]{:S(2)}) collective-permute-start(bf16[512,128]{1,0:T(8,128)(2,1)S(1)} %get-tuple-element.58), channel_id=1, source_target_pairs={{0,6},{1,3},{64,70},{65,67},{8,14},{9,11},{72,78},{73,75},{16,22},... | collective-permute-start | bytes 393224 | tf_op jit(solution)/shard_map/sum_queries_over_x/ppermute | solution.py:40
  41.2 2.1 %collective-permute-start.15 = (bf16[512,128]{1,0:T(8,128)(2,1)S(1)}, bf16[512,128]{1,0:T(8,128)(2,1)S(1)}, u32[]{:S(2)}, u32[]{:S(2)}) collective-permute-start(bf16[512,128]{1,0:T(8,128)(2,1)S(1)} %get-tuple-element.59), channel_id=1, source_target_pairs={{0,4},{1,5},{64,68},{65,69},{8,12},{9,13},{72,76},{73,77},{16,20},... | collective-permute-start | bytes 393224 | tf_op jit(solution)/shard_map/sum_queries_over_x/ppermute | solution.py:40
  43.3 1.5 %attend_a_a.1 = (f32[512,256]{1,0:T(8,128)S(1)}, f32[512,128]{1,0:T(8,128)S(1)}, bf16[512,128]{1,0:T(8,128)(2,1)S(1)}) custom-call(bf16[256,256]{1,0:T(8,128)(2,1)S(1)} %get-tuple-element.41.refs_0_, bf16[256,256]{1,0:T(8,128)(2,1)S(1)} %collective-permute-done.3.refs_1_, bf16[528,256]{1,0:T(8,128)(2,1)S(1)} %get-tuple-element.42.refs_2_, ...), custom_call_target="tpu_custom_call" | custom-call | flops 671088640 | bytes 2768896 | tf_op jit(solution)/shard_map/attend_a_a/pallas_call | solution.py:203
  45.8 2.6 %collective-permute-done.14.a = bf16[512,128]{1,0:T(8,128)(2,1)S(1)} collective-permute-done((bf16[512,128]{1,0:T(8,128)(2,1)S(1)}, bf16[512,128]{1,0:T(8,128)(2,1)S(1)}, u32[]{:S(2)}, u32[]{:S(2)}) %collective-permute-start.14) | collective-permute-done | bytes 131104 | tf_op jit(solution)/shard_map/sum_queries_over_x/ppermute | solution.py:40
  48.4 1.5 %collective-permute-done.18.q1 = bf16[512,128]{1,0:T(8,128)(2,1)S(1)} collective-permute-done((bf16[512,128]{1,0:T(8,128)(2,1)S(1)}, bf16[512,128]{1,0:T(8,128)(2,1)S(1)}, u32[]{:S(2)}, u32[]{:S(2)}) %collective-permute-start.18) | collective-permute-done | bytes 131104 | tf_op jit(solution)/shard_map/sum_queries_over_x/ppermute | solution.py:40
  50.8 2.0 %collective-permute-start.20 = (bf16[128,256]{1,0:T(8,128)(2,1)S(1)}, bf16[128,256]{1,0:T(8,128)(2,1)S(1)}, u32[]{:S(2)}, u32[]{:S(2)}) collective-permute-start(bf16[128,256]{1,0:T(8,128)(2,1)S(1)} %get-tuple-element.69), channel_id=1, source_target_pairs={{0,32},{1,33},{64,96},{65,97},{8,40},{9,41},{72,104},{73,105},{16,... | collective-permute-start | bytes 196616 | tf_op jit(solution)/shard_map/back_over_y/ppermute | solution.py:40
  52.8 2.3 %collective-permute-start.21 = (bf16[128,256]{1,0:T(8,128)(2,1)S(1)}, bf16[128,256]{1,0:T(8,128)(2,1)S(1)}, u32[]{:S(2)}, u32[]{:S(2)}) collective-permute-start(bf16[128,256]{1,0:T(8,128)(2,1)S(1)} %get-tuple-element.71), channel_id=1, source_target_pairs={{0,48},{1,49},{64,112},{65,113},{8,56},{9,57},{72,120},{73,121},{1... | collective-permute-start | bytes 196616 | tf_op jit(solution)/shard_map/back_over_y/ppermute | solution.py:40
  55.3 1.8 %collective-permute-done.20.b2 = bf16[128,256]{1,0:T(8,128)(2,1)S(1)} collective-permute-done((bf16[128,256]{1,0:T(8,128)(2,1)S(1)}, bf16[128,256]{1,0:T(8,128)(2,1)S(1)}, u32[]{:S(2)}, u32[]{:S(2)}) %collective-permute-start.20) | collective-permute-done | bytes 65568 | tf_op jit(solution)/shard_map/back_over_y/ppermute | solution.py:40
  58.3 2.3 %collective-permute-done.22.b3 = bf16[128,256]{1,0:T(8,128)(2,1)S(1)} collective-permute-done((bf16[128,256]{1,0:T(8,128)(2,1)S(1)}, bf16[128,256]{1,0:T(8,128)(2,1)S(1)}, u32[]{:S(2)}, u32[]{:S(2)}) %collective-permute-start.22) | collective-permute-done | bytes 65568 | tf_op jit(solution)/shard_map/back_over_y/ppermute | solution.py:40
  (40 shorter events, 10.4 us)
Async XLA Ops:
  2.6 9.4 %collective-permute-start = (bf16[208,256]{1,0:T(8,128)(2,1)}, bf16[208,256]{1,0:T(8,128)(2,1)S(1)}, u32[]{:S(2)}, u32[]{:S(2)}) collective-permute-start(bf16[208,256]{1,0:T(8,128)(2,1)} %get-tuple-element.38), channel_id=1, source_target_pairs={{0,32},{1,33},{64,96},{65,97},{8,40},{9,41},{72,104},{73,105},{16,... | collective-permute-start | bytes 319496 | tf_op jit(solution)/shard_map/heads_over_y/ppermute | solution.py:40
  6.0 6.1 %collective-permute-start.1 = (bf16[208,256]{1,0:T(8,128)(2,1)}, bf16[208,256]{1,0:T(8,128)(2,1)S(1)}, u32[]{:S(2)}, u32[]{:S(2)}) collective-permute-start(bf16[208,256]{1,0:T(8,128)(2,1)} %get-tuple-element.39), channel_id=1, source_target_pairs={{0,16},{1,17},{64,80},{65,81},{8,24},{9,25},{72,88},{73,89},{16,32... | collective-permute-start | bytes 319496 | tf_op jit(solution)/shard_map/heads_over_y/ppermute | solution.py:40
  6.7 5.5 %collective-permute-start.2 = (bf16[208,256]{1,0:T(8,128)(2,1)}, bf16[208,256]{1,0:T(8,128)(2,1)S(1)}, u32[]{:S(2)}, u32[]{:S(2)}) collective-permute-start(bf16[208,256]{1,0:T(8,128)(2,1)} %get-tuple-element.40), channel_id=1, source_target_pairs={{0,48},{1,49},{64,112},{65,113},{8,56},{9,57},{72,120},{73,121},{1... | collective-permute-start | bytes 319496 | tf_op jit(solution)/shard_map/heads_over_y/ppermute | solution.py:40
  11.2 0.9 %copy-start = (bf16[208,256]{1,0:T(8,128)(2,1)S(1)}, bf16[208,256]{1,0:T(8,128)(2,1)}, u32[]{:S(2)}) copy-start(bf16[208,256]{1,0:T(8,128)(2,1)} %pack.4.source) | copy-start | bytes 319492
  12.2 9.0 %collective-permute-start.7 = (bf16[528,256]{1,0:T(8,128)(2,1)S(1)}, bf16[528,256]{1,0:T(8,128)(2,1)S(1)}, u32[]{:S(2)}, u32[]{:S(2)}) collective-permute-start(bf16[528,256]{1,0:T(8,128)(2,1)S(1)} %get-tuple-element.42.refs_2_), channel_id=1, source_target_pairs={{0,2},{1,7},{64,66},{65,71},{8,10},{9,15},{72,74},{73,79},{16,18},... | collective-permute-start | bytes 811016 | tf_op jit(solution)/shard_map/queries_over_x/ppermute | solution.py:40
  13.7 12.7 %collective-permute-start.4 = (bf16[528,256]{1,0:T(8,128)(2,1)S(1)}, bf16[528,256]{1,0:T(8,128)(2,1)S(1)}, u32[]{:S(2)}, u32[]{:S(2)}) collective-permute-start(bf16[528,256]{1,0:T(8,128)(2,1)S(1)} %get-tuple-element.42.refs_2_), channel_id=1, source_target_pairs={{0,6},{1,3},{64,70},{65,67},{8,14},{9,11},{72,78},{73,75},{16,22},... | collective-permute-start | bytes 811016 | tf_op jit(solution)/shard_map/queries_over_x/ppermute | solution.py:40
  15.8 7.1 %collective-permute-start.6 = (bf16[256,256]{1,0:T(8,128)(2,1)S(1)}, bf16[256,256]{1,0:T(8,128)(2,1)S(1)}, u32[]{:S(2)}, u32[]{:S(2)}) collective-permute-start(bf16[256,256]{1,0:T(8,128)(2,1)S(1)} %get-tuple-element.41.refs_0_), channel_id=1, source_target_pairs={{0,8},{1,9},{64,72},{65,73},{8,0},{9,1},{72,64},{73,65},{16,24},{1... | collective-permute-start | bytes 393224 | tf_op jit(solution)/shard_map/keys_over_z/ppermute | solution.py:40
  19.7 6.2 %collective-permute-start.5 = (bf16[256,256]{1,0:T(8,128)(2,1)S(1)}, bf16[256,256]{1,0:T(8,128)(2,1)S(1)}, u32[]{:S(2)}, u32[]{:S(2)}) collective-permute-start(bf16[256,256]{1,0:T(8,128)(2,1)S(1)} %get-tuple-element.41.refs_0_), channel_id=1, source_target_pairs={{0,72},{1,65},{64,8},{65,1},{8,64},{9,73},{72,0},{73,9},{16,88},{1... | collective-permute-start | bytes 393224 | tf_op jit(solution)/shard_map/keys_over_z/ppermute | solution.py:40
  20.4 5.5 %collective-permute-start.3 = (bf16[256,256]{1,0:T(8,128)(2,1)S(1)}, bf16[256,256]{1,0:T(8,128)(2,1)S(1)}, u32[]{:S(2)}, u32[]{:S(2)}) collective-permute-start(bf16[256,256]{1,0:T(8,128)(2,1)S(1)} %get-tuple-element.41.refs_0_), channel_id=1, source_target_pairs={{0,64},{1,73},{64,0},{65,9},{8,72},{9,65},{72,8},{73,1},{16,80},{1... | collective-permute-start | bytes 393224 | tf_op jit(solution)/shard_map/keys_over_z/ppermute | solution.py:40
  21.2 9.7 %collective-permute-start.8 = (bf16[528,256]{1,0:T(8,128)(2,1)S(1)}, bf16[528,256]{1,0:T(8,128)(2,1)S(1)}, u32[]{:S(2)}, u32[]{:S(2)}) collective-permute-start(bf16[528,256]{1,0:T(8,128)(2,1)S(1)} %collective-permute-done.7.refs_3_), channel_id=1, source_target_pairs={{0,6},{1,3},{64,70},{65,67},{8,14},{9,11},{72,78},{73,75},{16,22},... | collective-permute-start | bytes 811016 | tf_op jit(solution)/shard_map/queries_over_x/ppermute | solution.py:40
  23.0 5.0 %collective-permute-start.12 = (bf16[256,256]{1,0:T(8,128)(2,1)S(1)}, bf16[256,256]{1,0:T(8,128)(2,1)S(1)}, u32[]{:S(2)}, u32[]{:S(2)}) collective-permute-start(bf16[256,256]{1,0:T(8,128)(2,1)S(1)} %collective-permute-done.6.refs_1_.refs_3_), channel_id=1, source_target_pairs={{0,1},{1,0},{64,65},{65,64},{8,9},{9,8},{72,73},{73,72},{16,17},{1... | collective-permute-start | bytes 393224 | tf_op jit(solution)/shard_map/keys_over_z/ppermute | solution.py:40
  25.9 2.1 %collective-permute-start.11 = (bf16[256,256]{1,0:T(8,128)(2,1)S(1)}, bf16[256,256]{1,0:T(8,128)(2,1)S(1)}, u32[]{:S(2)}, u32[]{:S(2)}) collective-permute-start(bf16[256,256]{1,0:T(8,128)(2,1)S(1)} %collective-permute-done.5.refs_0_.refs_2_), channel_id=1, source_target_pairs={{0,1},{1,0},{64,65},{65,64},{8,9},{9,8},{72,73},{73,72},{16,17},{1... | collective-permute-start | bytes 393224 | tf_op jit(solution)/shard_map/keys_over_z/ppermute | solution.py:40
  25.9 3.5 %collective-permute-start.9 = (bf16[256,256]{1,0:T(8,128)(2,1)S(1)}, bf16[256,256]{1,0:T(8,128)(2,1)S(1)}, u32[]{:S(2)}, u32[]{:S(2)}) collective-permute-start(bf16[256,256]{1,0:T(8,128)(2,1)S(1)} %get-tuple-element.41.refs_0_), channel_id=1, source_target_pairs={{0,1},{1,0},{64,65},{65,64},{8,9},{9,8},{72,73},{73,72},{16,17},{1... | collective-permute-start | bytes 393224 | tf_op jit(solution)/shard_map/keys_over_z/ppermute | solution.py:40
  26.4 3.0 %collective-permute-start.10 = (bf16[256,256]{1,0:T(8,128)(2,1)S(1)}, bf16[256,256]{1,0:T(8,128)(2,1)S(1)}, u32[]{:S(2)}, u32[]{:S(2)}) collective-permute-start(bf16[256,256]{1,0:T(8,128)(2,1)S(1)} %collective-permute-done.3.refs_1_), channel_id=1, source_target_pairs={{0,1},{1,0},{64,65},{65,64},{8,9},{9,8},{72,73},{73,72},{16,17},{1... | collective-permute-start | bytes 393224 | tf_op jit(solution)/shard_map/keys_over_z/ppermute | solution.py:40
  33.8 2.4 %collective-permute-start.13 = (bf16[512,256]{1,0:T(8,128)(2,1)S(1)}, bf16[512,256]{1,0:T(8,128)(2,1)S(1)}, u32[]{:S(2)}, u32[]{:S(2)}) collective-permute-start(bf16[512,256]{1,0:T(8,128)(2,1)S(1)} %get-tuple-element.56), channel_id=1, source_target_pairs={{0,1},{1,0},{64,65},{65,64},{8,9},{9,8},{72,73},{73,72},{16,17},{1... | collective-permute-start | bytes 786440 | tf_op jit(solution)/shard_map/sum_keys_over_core/ppermute | solution.py:40
  36.0 9.6 %collective-permute-start.16 = (bf16[512,256]{1,0:T(8,128)(2,1)S(1)}, bf16[512,256]{1,0:T(8,128)(2,1)S(1)}, u32[]{:S(2)}, u32[]{:S(2)}) collective-permute-start(bf16[512,256]{1,0:T(8,128)(2,1)S(1)} %get-tuple-element.64), channel_id=1, source_target_pairs={{0,1},{1,0},{64,65},{65,64},{8,9},{9,8},{72,73},{73,72},{16,17},{1... | collective-permute-start | bytes 786440 | tf_op jit(solution)/shard_map/sum_keys_over_core/ppermute | solution.py:40
  36.2 9.4 %collective-permute-start.17 = (bf16[512,256]{1,0:T(8,128)(2,1)S(1)}, bf16[512,256]{1,0:T(8,128)(2,1)S(1)}, u32[]{:S(2)}, u32[]{:S(2)}) collective-permute-start(bf16[512,256]{1,0:T(8,128)(2,1)S(1)} %sum_keys_over_core.1), channel_id=1, source_target_pairs={{0,72},{1,65},{64,8},{65,1},{8,64},{9,73},{72,0},{73,9},{16,88},{1... | collective-permute-start | bytes 786440 | tf_op jit(solution)/shard_map/sum_keys_over_z/ppermute | solution.py:40
  39.8 8.5 %collective-permute-start.14 = (bf16[512,128]{1,0:T(8,128)(2,1)S(1)}, bf16[512,128]{1,0:T(8,128)(2,1)S(1)}, u32[]{:S(2)}, u32[]{:S(2)}) collective-permute-start(bf16[512,128]{1,0:T(8,128)(2,1)S(1)} %get-tuple-element.58), channel_id=1, source_target_pairs={{0,6},{1,3},{64,70},{65,67},{8,14},{9,11},{72,78},{73,75},{16,22},... | collective-permute-start | bytes 393224 | tf_op jit(solution)/shard_map/sum_queries_over_x/ppermute | solution.py:40
  41.2 7.1 %collective-permute-start.15 = (bf16[512,128]{1,0:T(8,128)(2,1)S(1)}, bf16[512,128]{1,0:T(8,128)(2,1)S(1)}, u32[]{:S(2)}, u32[]{:S(2)}) collective-permute-start(bf16[512,128]{1,0:T(8,128)(2,1)S(1)} %get-tuple-element.59), channel_id=1, source_target_pairs={{0,4},{1,5},{64,68},{65,69},{8,12},{9,13},{72,76},{73,77},{16,20},... | collective-permute-start | bytes 393224 | tf_op jit(solution)/shard_map/sum_queries_over_x/ppermute | solution.py:40
  44.8 5.0 %collective-permute-start.18 = (bf16[512,128]{1,0:T(8,128)(2,1)S(1)}, bf16[512,128]{1,0:T(8,128)(2,1)S(1)}, u32[]{:S(2)}, u32[]{:S(2)}) collective-permute-start(bf16[512,128]{1,0:T(8,128)(2,1)S(1)} %get-tuple-element.67), channel_id=1, source_target_pairs={{0,2},{1,7},{64,66},{65,71},{8,10},{9,15},{72,74},{73,79},{16,18},... | collective-permute-start | bytes 393224 | tf_op jit(solution)/shard_map/sum_queries_over_x/ppermute | solution.py:40
  45.7 5.0 %collective-permute-start.19 = (bf16[256,256]{1,0:T(8,128)(2,1)S(1)}, bf16[256,256]{1,0:T(8,128)(2,1)S(1)}, u32[]{:S(2)}, u32[]{:S(2)}) collective-permute-start(bf16[256,256]{1,0:T(8,128)(2,1)S(1)} %get-tuple-element.68), channel_id=1, source_target_pairs={{0,64},{1,73},{64,0},{65,9},{8,72},{9,65},{72,8},{73,1},{16,80},{1... | collective-permute-start | bytes 393224 | tf_op jit(solution)/shard_map/sum_keys_over_z/ppermute | solution.py:40
  50.8 6.4 %collective-permute-start.20 = (bf16[128,256]{1,0:T(8,128)(2,1)S(1)}, bf16[128,256]{1,0:T(8,128)(2,1)S(1)}, u32[]{:S(2)}, u32[]{:S(2)}) collective-permute-start(bf16[128,256]{1,0:T(8,128)(2,1)S(1)} %get-tuple-element.69), channel_id=1, source_target_pairs={{0,32},{1,33},{64,96},{65,97},{8,40},{9,41},{72,104},{73,105},{16,... | collective-permute-start | bytes 196616 | tf_op jit(solution)/shard_map/back_over_y/ppermute | solution.py:40
  52.8 5.5 %collective-permute-start.21 = (bf16[128,256]{1,0:T(8,128)(2,1)S(1)}, bf16[128,256]{1,0:T(8,128)(2,1)S(1)}, u32[]{:S(2)}, u32[]{:S(2)}) collective-permute-start(bf16[128,256]{1,0:T(8,128)(2,1)S(1)} %get-tuple-element.71), channel_id=1, source_target_pairs={{0,48},{1,49},{64,112},{65,113},{8,56},{9,57},{72,120},{73,121},{1... | collective-permute-start | bytes 196616 | tf_op jit(solution)/shard_map/back_over_y/ppermute | solution.py:40
  55.1 5.5 %collective-permute-start.22 = (bf16[128,256]{1,0:T(8,128)(2,1)S(1)}, bf16[128,256]{1,0:T(8,128)(2,1)S(1)}, u32[]{:S(2)}, u32[]{:S(2)}) collective-permute-start(bf16[128,256]{1,0:T(8,128)(2,1)S(1)} %get-tuple-element.72), channel_id=1, source_target_pairs={{0,16},{1,17},{64,80},{65,81},{8,24},{9,25},{72,88},{73,89},{16,32... | collective-permute-start | bytes 196616 | tf_op jit(solution)/shard_map/back_over_y/ppermute | solution.py:40

commit v3 on v2

--- a/solution.py
+++ b/solution.py
@@ -17,6 +17,8 @@
 KR = 64
 AUX = 16
 TILE = 512
+HINT = 1.0
+LATE = 4 * 10**9
 BLK = QR + KR + AUX
 QS = 4 * QR
 KS = 4 * KR
@@ -44,10 +46,6 @@
     return move(value, lambda x, y, z, c: (x, y, z, 1 - c))
 
 
-def along_y(value, step):
-    return move(value, lambda x, y, z, c: (x, (y + step) % 4, z, c))
-
-
 def partner(place, core, kind):
     if kind == 2:
         return (place + 2) % 4
@@ -55,6 +53,10 @@
     return (place + (1 if up else -1)) % 4
 
 
+def swap_y(value, kind):
+    return move(value, lambda x, y, z, c: (x, partner(y, c, kind), z, c))
+
+
 def swap_x(value, kind):
     return move(value, lambda x, y, z, c: (partner(x, c, kind), y, z, c))
 
@@ -70,7 +72,17 @@
     return [high, middle, rest - middle]
 
 
-def pack_kernel(steps, *refs):
+def head_of(kind):
+    y = lax.axis_index("row") % 4
+    if kind is None:
+        return y
+    if kind == 2:
+        return lax.rem(y + 2, 4)
+    odd = lax.rem(y + kind + lax.axis_index("col"), 2)
+    return lax.rem(y + 1 + 2 * odd, 4)
+
+
+def pack_kernel(kinds, *refs):
     blocks, bufs, sem = refs[6:-7], refs[-7:-1], refs[-1]
     copies = [pltpu.make_async_copy(refs[i], bufs[i], sem.at[i]) for i in range(6)]
     for copy in copies:
@@ -78,9 +90,8 @@
     for copy in copies:
         copy.wait()
     q_ref, k_ref, v_ref, o_ref, g_ref, lse_ref = bufs
-    y = lax.axis_index("row") % 4
-    for step, block in zip(steps, blocks):
-        head = lax.rem(y + step, 4)
+    for kind, block in zip(kinds, blocks):
+        head = head_of(kind)
         cols = pl.ds(pl.multiple_of(head * DH, DH), DH)
         g = g_ref[:, cols]
         block[:QR, :DH] = q_ref[:, cols]
@@ -98,7 +109,7 @@
     out[...] = source[...]
 
 
-def join_kernel(b2, b0, b1, b3, q_out, kv_out):
+def join_kernel(b0, b1, b3, b2, q_out, kv_out):
     aux = []
     for j, block in enumerate((b0, b1, b2, b3)):
         q_out[j * QR : (j + 1) * QR, :] = block[:QR, :]
@@ -120,16 +131,14 @@
 
 
 def tile_terms(q_all, kv, terms, p_all, ds_all):
-    for first in range(0, 2 * QS, QS):
-        cols = slice(first, first + QS)
-        q, g = q_all[cols, :DH], q_all[cols, DH:]
-        s = lax.dot_general(kv[:, :DH], q, NT, preferred_element_type=F32)
-        p = jnp.exp2(s * (FACTOR * LOG2E) - terms[0:1, cols])
-        dp = lax.dot_general(kv[:, DH:], g, NT, preferred_element_type=F32)
-        p_all[:, cols] = p.astype(BF16)
-        ds_all[:, cols] = (p * (dp - terms[1:2, cols]) * FACTOR).astype(BF16)
-    dv = jnp.dot(p_all[...], q_all[:, DH:], preferred_element_type=F32)
-    dk = jnp.dot(ds_all[...], q_all[:, :DH], preferred_element_type=F32)
+    q, g = q_all[:, :DH], q_all[:, DH:]
+    s = lax.dot_general(kv[:, :DH], q, NT, preferred_element_type=F32)
+    p = jnp.exp2(s * (FACTOR * LOG2E) - terms[0:1, :])
+    dp = lax.dot_general(kv[:, DH:], g, NT, preferred_element_type=F32)
+    p_all[...] = p.astype(BF16)
+    ds_all[...] = (p * (dp - terms[1:2, :]) * FACTOR).astype(BF16)
+    dv = jnp.dot(p_all[...], g, preferred_element_type=F32)
+    dk = jnp.dot(ds_all[...], q, preferred_element_type=F32)
     dq = jnp.dot(kv[:, :DH].T, ds_all[...], preferred_element_type=F32)
     return dk, dv, dq
 
@@ -176,7 +185,7 @@
         out[...] = total.astype(out.dtype)
 
 
-def chip_sum_kernel(q23, q0, k0, q1, k1, *outs):
+def chip_sum_kernel(q23, q0, k0, k1, q1, *outs):
     dq = q0[...] + q1[...].astype(F32) + q23[...]
     dkv = k0[...] + k1[...].astype(F32)
     for j, out in enumerate(outs):
@@ -186,10 +195,9 @@
         out[KR:, :] = dkv[j * KR : (j + 1) * KR].astype(out.dtype)
 
 
-def unpack_kernel(b2, b0, b1, b3, dq, dk, dv):
-    y = lax.axis_index("row") % 4
-    for j, block in enumerate((b0, b1, b2, b3)):
-        cols = pl.ds(pl.multiple_of(lax.rem(y + j, 4) * DH, DH), DH)
+def unpack_kernel(b0, b1, b3, b2, dq, dk, dv):
+    for kind, block in ((None, b0), (0, b1), (2, b2), (1, b3)):
+        cols = pl.ds(pl.multiple_of(head_of(kind) * DH, DH), DH)
         dq[: QR // 2, cols] = block[:KR, :DH].astype(F32)
         dq[QR // 2 :, cols] = block[:KR, DH:].astype(F32)
         dk[:, cols] = block[KR:, :DH].astype(F32)
@@ -226,7 +234,7 @@
             pltpu.VMEM((TILE, rows), BF16),
             pltpu.VMEM((TILE, rows), BF16),
         ],
-        flops=10 * rows * TILE * len(tiles) * DH,
+        flops=int(10 * rows * TILE * len(tiles) * DH * HINT),
     )
     return outs[len(tiles) :], outs[: len(tiles)]
 
@@ -236,8 +244,8 @@
     with jax.named_scope("pack"):
         scratch = [pltpu.VMEM(a.shape, a.dtype) for a in args] + [pltpu.SemaphoreType.DMA((6,))]
         place = pl.BlockSpec(memory_space=pltpu.HBM)
-        far, plus, minus = call(
-            functools.partial(pack_kernel, (2, 1, 3)),
+        far, first, second = call(
+            functools.partial(pack_kernel, (2, 0, 1)),
             [((BLK, 2 * DH), BF16)] * 3,
             args,
             scratch=scratch,
@@ -245,7 +253,7 @@
             limit=56,
         )
         here = call(
-            functools.partial(pack_kernel, (0,)),
+            functools.partial(pack_kernel, (None,)),
             [((BLK, 2 * DH), BF16)],
             args,
             scratch=scratch,
@@ -254,7 +262,7 @@
         )[0]
         here = call(copy_kernel, [((BLK, 2 * DH), BF16)], (here,))[0]
     with jax.named_scope("heads_over_y"):
-        blocks = [along_y(far, 2), here, along_y(plus, 1), along_y(minus, 3)]
+        blocks = [here, swap_y(first, 0), swap_y(second, 1), swap_y(far, 2)]
     with jax.named_scope("join"):
         q, kv = call(join_kernel, [((QS + AUX, 2 * DH), BF16), ((KS, 2 * DH), BF16)], blocks)
     with jax.named_scope("queries_over_x"):
@@ -296,7 +304,7 @@
         )
     with jax.named_scope("sum_queries_over_x"):
         got1 = swap_x(dq1, 0)
-        got23 = call(add_kernel, [((QS, DH), F32)], (got2, got3), flops=4 * 10**9)[0]
+        got23 = call(add_kernel, [((QS, DH), F32)], (got2, got3), flops=LATE)[0]
     with jax.named_scope("sum_keys_over_z"):
         k_own, k_sent = call(
             split_kernel, [((KS, 2 * DH), F32), ((KS, 2 * DH), BF16)], (dkv_own, got_other, got_b)
@@ -306,11 +314,11 @@
         backs = call(
             chip_sum_kernel,
             [((2 * KR, 2 * DH), F32)] + [((2 * KR, 2 * DH), BF16)] * 3,
-            (got23, dq0, k_own, got1, k_got),
+            (got23, dq0, k_own, k_got, got1),
         )
     with jax.named_scope("back_over_y"):
-        far = along_y(backs[2], 2)
-        backs = [far, backs[0], along_y(backs[1], 3), along_y(backs[3], 1)]
+        far = swap_y(backs[2], 2)
+        backs = [backs[0], swap_y(backs[1], 0), swap_y(backs[3], 1), far]
     with jax.named_scope("unpack"):
         return tuple(
             call(

time: 61.7 us -> 60.7 us (0.984)
  starting transfers between devices: 28.9 us -> 26 us
  waiting for transfers between devices: 14 us -> 16.4 us
    ppermute x23, starting transfers between devices: 28.9 us -> 26 us  [move(): return lax.ppermute(value, AXES, pairs)]
    ppermute x23, waiting for transfers between devices: 14 us -> 16.4 us  [move(): return lax.ppermute(value, AXES, pairs)]
  transfers between devices with their start and end apart: 23 -> 23, of which waited for: 9 -> 11; matrix products, arithmetic and copies ran while one was open for 0% -> 0% of each run, Pallas kernels for 18% -> 18%
where the time goes in v3:
time: 60.7 us; the launch traced here: 60.5 us
  starting transfers between devices  26 us (43%)
  Pallas kernels  16.4 us (27%)
  waiting for transfers between devices  16.4 us (27%)
  local copies, waits for them, and re-layouts  0.89 us (1%)
  between operations  0.81 us (1%)
    ppermute x23, starting transfers between devices, move(): return lax.ppermute(value, AXES, pairs)  26 us
    pallas_call x16, Pallas kernels, call(): pl.pallas_call(kernel, out_shape=[jax.ShapeDtypeStruct(shape, kind) for s...  16.4 us
    ppermute x23, waiting for transfers between devices, move(): return lax.ppermute(value, AXES, pairs)  16.4 us
  transfers between devices with their start and end apart: 23, of which 11 were waited for; matrix products, arithmetic and copies ran while one was open for 0% of the time, Pallas kernels for 18%

profile of v3, /device:TPU:0, one launch (start us, length us, event | category | flops | bytes accessed | tf_op | source)
XLA Modules:
  0.0 60.5 jit_solution(9160625554256833089)
XLA Ops:
  0.6 2.0 %pack.5 = (bf16[208,256]{1,0:T(8,128)(2,1)}, bf16[208,256]{1,0:T(8,128)(2,1)}, bf16[208,256]{1,0:T(8,128)(2,1)}) custom-call(bf16[128,512]{1,0:T(8,128)(2,1)} %refs_0_.3, bf16[64,512]{1,0:T(8,128)(2,1)} %refs_1_.3, bf16[64,512]{1,0:T(8,128)(2,1)} %refs_2_.3, bf16[128,512]{1,0:T(8,128)(2,1)} %refs_3_.3, bf16[128,512]{1,0:T(8,128)(2,1)} %refs_4_.3, ...), custom_call_target="tpu_custom_call" | custom-call | bytes 845824 | tf_op jit(solution)/shard_map/pack/pallas_call | solution.py:211
  2.6 1.7 %collective-permute-start = (bf16[208,256]{1,0:T(8,128)(2,1)}, bf16[208,256]{1,0:T(8,128)(2,1)S(1)}, u32[]{:S(2)}, u32[]{:S(2)}) collective-permute-start(bf16[208,256]{1,0:T(8,128)(2,1)} %get-tuple-element.38), channel_id=1, source_target_pairs={{0,16},{1,49},{64,80},{65,113},{8,24},{9,57},{72,88},{73,121},{16,... | collective-permute-start | bytes 319496 | tf_op jit(solution)/shard_map/heads_over_y/ppermute | solution.py:42
  4.4 2.2 %collective-permute-start.1 = (bf16[208,256]{1,0:T(8,128)(2,1)}, bf16[208,256]{1,0:T(8,128)(2,1)S(1)}, u32[]{:S(2)}, u32[]{:S(2)}) collective-permute-start(bf16[208,256]{1,0:T(8,128)(2,1)} %get-tuple-element.39), channel_id=1, source_target_pairs={{0,48},{1,17},{64,112},{65,81},{8,56},{9,25},{72,120},{73,89},{16,... | collective-permute-start | bytes 319496 | tf_op jit(solution)/shard_map/heads_over_y/ppermute | solution.py:42
  7.3 1.9 %pack.3.source = bf16[208,256]{1,0:T(8,128)(2,1)} custom-call(bf16[128,512]{1,0:T(8,128)(2,1)} %refs_0_.3, bf16[64,512]{1,0:T(8,128)(2,1)} %refs_1_.3, bf16[64,512]{1,0:T(8,128)(2,1)} %refs_2_.3, bf16[128,512]{1,0:T(8,128)(2,1)} %refs_3_.3, bf16[128,512]{1,0:T(8,128)(2,1)} %refs_4_.3, f32[4,128]{1,0:T(4,128)} %refs_5_.3), custom_call_target="tpu_custom_call" | custom-call | bytes 632832 | tf_op jit(solution)/shard_map/pack/pallas_call | solution.py:211
  10.1 1.5 %collective-permute-done.1.b3 = bf16[208,256]{1,0:T(8,128)(2,1)S(1)} collective-permute-done((bf16[208,256]{1,0:T(8,128)(2,1)}, bf16[208,256]{1,0:T(8,128)(2,1)S(1)}, u32[]{:S(2)}, u32[]{:S(2)}) %collective-permute-start.1) | collective-permute-done | bytes 106528 | tf_op jit(solution)/shard_map/heads_over_y/ppermute | solution.py:42
  11.6 1.3 %collective-permute-done.2.b2 = bf16[208,256]{1,0:T(8,128)(2,1)S(1)} collective-permute-done((bf16[208,256]{1,0:T(8,128)(2,1)}, bf16[208,256]{1,0:T(8,128)(2,1)S(1)}, u32[]{:S(2)}, u32[]{:S(2)}) %collective-permute-start.2) | collective-permute-done | bytes 106528 | tf_op jit(solution)/shard_map/heads_over_y/ppermute | solution.py:42
  13.0 1.6 %collective-permute-start.7 = (bf16[528,256]{1,0:T(8,128)(2,1)S(1)}, bf16[528,256]{1,0:T(8,128)(2,1)S(1)}, u32[]{:S(2)}, u32[]{:S(2)}) collective-permute-start(bf16[528,256]{1,0:T(8,128)(2,1)S(1)} %get-tuple-element.42.refs_2_), channel_id=1, source_target_pairs={{0,2},{1,7},{64,66},{65,71},{8,10},{9,15},{72,74},{73,79},{16,18},... | collective-permute-start | bytes 811016 | tf_op jit(solution)/shard_map/queries_over_x/ppermute | solution.py:42
  14.6 2.1 %collective-permute-start.4 = (bf16[528,256]{1,0:T(8,128)(2,1)S(1)}, bf16[528,256]{1,0:T(8,128)(2,1)S(1)}, u32[]{:S(2)}, u32[]{:S(2)}) collective-permute-start(bf16[528,256]{1,0:T(8,128)(2,1)S(1)} %get-tuple-element.42.refs_2_), channel_id=1, source_target_pairs={{0,6},{1,3},{64,70},{65,67},{8,14},{9,11},{72,78},{73,75},{16,22},... | collective-permute-start | bytes 811016 | tf_op jit(solution)/shard_map/queries_over_x/ppermute | solution.py:42
  16.7 3.9 %collective-permute-start.6 = (bf16[256,256]{1,0:T(8,128)(2,1)S(1)}, bf16[256,256]{1,0:T(8,128)(2,1)S(1)}, u32[]{:S(2)}, u32[]{:S(2)}) collective-permute-start(bf16[256,256]{1,0:T(8,128)(2,1)S(1)} %get-tuple-element.41.refs_0_), channel_id=1, source_target_pairs={{0,8},{1,9},{64,72},{65,73},{8,0},{9,1},{72,64},{73,65},{16,24},{1... | collective-permute-start | bytes 393224 | tf_op jit(solution)/shard_map/keys_over_z/ppermute | solution.py:42
  23.6 3.1 %collective-permute-done.5.refs_0_.refs_2_ = bf16[256,256]{1,0:T(8,128)(2,1)S(1)} collective-permute-done((bf16[256,256]{1,0:T(8,128)(2,1)S(1)}, bf16[256,256]{1,0:T(8,128)(2,1)S(1)}, u32[]{:S(2)}, u32[]{:S(2)}) %collective-permute-start.5) | collective-permute-done | bytes 131104 | tf_op jit(solution)/shard_map/keys_over_z/ppermute | solution.py:42
  27.3 1.4 %attend_a_b.2 = (f32[512,256]{1,0:T(8,128)S(1)}, f32[128,1024]{1,0:T(8,128)S(1)}) custom-call(bf16[256,256]{1,0:T(8,128)(2,1)S(1)} %collective-permute-done.5.refs_0_.refs_2_, bf16[256,256]{1,0:T(8,128)(2,1)S(1)} %collective-permute-done.6.refs_1_.refs_3_, bf16[528,256]{1,0:T(8,128)(2,1)S(1)} %get-tuple-element.42.refs_2_, ...), custom_call_target="tpu_custom_call" | custom-call | flops 671088640 | bytes 1851392 | tf_op jit(solution)/shard_map/attend_a_b/pallas_call | solution.py:211
  28.8 1.4 %attend_a_b.3 = (f32[512,256]{1,0:T(8,128)S(1)}, f32[128,1024]{1,0:T(8,128)S(1)}) custom-call(bf16[256,256]{1,0:T(8,128)(2,1)S(1)} %collective-permute-done.11.refs_0_, bf16[256,256]{1,0:T(8,128)(2,1)S(1)} %collective-permute-done.12.refs_1_, bf16[528,256]{1,0:T(8,128)(2,1)S(1)} %get-tuple-element.42.refs_2_, ...), custom_call_target="tpu_custom_call" | custom-call | flops 671088640 | bytes 2375680 | tf_op jit(solution)/shard_map/attend_a_b/pallas_call | solution.py:211
  30.3 1.4 %attend_a_a_other.1 = (f32[512,256]{1,0:T(8,128)S(1)}, f32[128,1024]{1,0:T(8,128)S(1)}) custom-call(bf16[256,256]{1,0:T(8,128)(2,1)S(1)} %collective-permute-done.9.refs_0_, bf16[256,256]{1,0:T(8,128)(2,1)S(1)} %collective-permute-done.10.refs_1_, bf16[528,256]{1,0:T(8,128)(2,1)S(1)} %get-tuple-element.42.refs_2_, ...), custom_call_target="tpu_custom_call" | custom-call | flops 671088640 | bytes 2375680 | tf_op jit(solution)/shard_map/attend_a_a_other/pallas_call | solution.py:211
  31.7 2.7 %attend_b_b.1 = (bf16[512,256]{1,0:T(8,128)(2,1)S(1)}, f32[512,256]{1,0:T(8,128)S(1)}, f32[128,1024]{1,0:T(8,128)S(1)}) custom-call(bf16[256,256]{1,0:T(8,128)(2,1)S(1)} %collective-permute-done.11.refs_0_, bf16[256,256]{1,0:T(8,128)(2,1)S(1)} %collective-permute-done.12.refs_1_, bf16[256,256]{1,0:T(8,128)(2,1)S(1)} %collective-permute-done.5.refs_0_.refs_2_, ...), custom_call_target="tpu_custom_call" | custom-call | flops 1342177280 | bytes 3424256 | tf_op jit(solution)/shard_map/attend_b_b/pallas_call | solution.py:211
  34.9 1.5 %attend_b_a_other.1 = (bf16[512,256]{1,0:T(8,128)(2,1)S(1)}, f32[128,1024]{1,0:T(8,128)S(1)}) custom-call(bf16[256,256]{1,0:T(8,128)(2,1)S(1)} %collective-permute-done.9.refs_0_, bf16[256,256]{1,0:T(8,128)(2,1)S(1)} %collective-permute-done.10.refs_1_, bf16[528,256]{1,0:T(8,128)(2,1)S(1)} %collective-permute-done.4.refs_4_.refs_2_, ...), custom_call_target="tpu_custom_call" | custom-call | flops 671088640 | bytes 2637824 | tf_op jit(solution)/shard_map/attend_b_a_other/pallas_call | solution.py:211
  36.6 2.7 %collective-permute-start.17 = (bf16[512,256]{1,0:T(8,128)(2,1)S(1)}, bf16[512,256]{1,0:T(8,128)(2,1)S(1)}, u32[]{:S(2)}, u32[]{:S(2)}) collective-permute-start(bf16[512,256]{1,0:T(8,128)(2,1)S(1)} %sum_keys_over_core.1), channel_id=1, source_target_pairs={{0,72},{1,65},{64,8},{65,1},{8,64},{9,73},{72,0},{73,9},{16,88},{1... | collective-permute-start | bytes 786440 | tf_op jit(solution)/shard_map/sum_keys_over_z/ppermute | solution.py:42
  39.3 1.5 %attend_b_a.1 = (f32[512,256]{1,0:T(8,128)S(1)}, bf16[512,128]{1,0:T(8,128)(2,1)S(1)}, bf16[512,128]{1,0:T(8,128)(2,1)S(1)}) custom-call(bf16[256,256]{1,0:T(8,128)(2,1)S(1)} %get-tuple-element.41.refs_0_, bf16[256,256]{1,0:T(8,128)(2,1)S(1)} %collective-permute-done.3.refs_1_, bf16[528,256]{1,0:T(8,128)(2,1)S(1)} %collective-permute-done.4.refs_4_.refs_2_, ...), custom_call_target="tpu_custom_call" | custom-call | flops 671088640 | bytes 2113536 | tf_op jit(solution)/shard_map/attend_b_a/pallas_call | solution.py:211
  43.2 1.5 %attend_a_a.1 = (f32[512,256]{1,0:T(8,128)S(1)}, f32[512,128]{1,0:T(8,128)S(1)}, bf16[512,128]{1,0:T(8,128)(2,1)S(1)}) custom-call(bf16[256,256]{1,0:T(8,128)(2,1)S(1)} %get-tuple-element.41.refs_0_, bf16[256,256]{1,0:T(8,128)(2,1)S(1)} %collective-permute-done.3.refs_1_, bf16[528,256]{1,0:T(8,128)(2,1)S(1)} %get-tuple-element.42.refs_2_, ...), custom_call_target="tpu_custom_call" | custom-call | flops 671088640 | bytes 2768896 | tf_op jit(solution)/shard_map/attend_a_a/pallas_call | solution.py:211
  44.6 1.9 %collective-permute-start.19 = (bf16[512,128]{1,0:T(8,128)(2,1)S(1)}, bf16[512,128]{1,0:T(8,128)(2,1)S(1)}, u32[]{:S(2)}, u32[]{:S(2)}) collective-permute-start(bf16[512,128]{1,0:T(8,128)(2,1)S(1)} %get-tuple-element.68), channel_id=1, source_target_pairs={{0,2},{1,7},{64,66},{65,71},{8,10},{9,15},{72,74},{73,79},{16,18},... | collective-permute-start | bytes 393224 | tf_op jit(solution)/shard_map/sum_queries_over_x/ppermute | solution.py:42
  46.8 2.6 %collective-permute-done.14.a = bf16[512,128]{1,0:T(8,128)(2,1)S(1)} collective-permute-done((bf16[512,128]{1,0:T(8,128)(2,1)S(1)}, bf16[512,128]{1,0:T(8,128)(2,1)S(1)}, u32[]{:S(2)}, u32[]{:S(2)}) %collective-permute-start.14) | collective-permute-done | bytes 131104 | tf_op jit(solution)/shard_map/sum_queries_over_x/ppermute | solution.py:42
  49.7 2.0 %collective-permute-done.18.k1 = bf16[256,256]{1,0:T(8,128)(2,1)S(1)} collective-permute-done((bf16[256,256]{1,0:T(8,128)(2,1)S(1)}, bf16[256,256]{1,0:T(8,128)(2,1)S(1)}, u32[]{:S(2)}, u32[]{:S(2)}) %collective-permute-start.18) | collective-permute-done | bytes 131104 | tf_op jit(solution)/shard_map/sum_keys_over_z/ppermute | solution.py:42
  52.1 1.8 %collective-permute-start.21 = (bf16[128,256]{1,0:T(8,128)(2,1)S(1)}, bf16[128,256]{1,0:T(8,128)(2,1)S(1)}, u32[]{:S(2)}, u32[]{:S(2)}) collective-permute-start(bf16[128,256]{1,0:T(8,128)(2,1)S(1)} %get-tuple-element.71), channel_id=1, source_target_pairs={{0,48},{1,17},{64,112},{65,81},{8,56},{9,25},{72,120},{73,89},{16,... | collective-permute-start | bytes 196616 | tf_op jit(solution)/shard_map/back_over_y/ppermute | solution.py:42
  53.9 2.0 %collective-permute-start.22 = (bf16[128,256]{1,0:T(8,128)(2,1)S(1)}, bf16[128,256]{1,0:T(8,128)(2,1)S(1)}, u32[]{:S(2)}, u32[]{:S(2)}) collective-permute-start(bf16[128,256]{1,0:T(8,128)(2,1)S(1)} %get-tuple-element.72), channel_id=1, source_target_pairs={{0,32},{1,33},{64,96},{65,97},{8,40},{9,41},{72,104},{73,105},{16,... | collective-permute-start | bytes 196616 | tf_op jit(solution)/shard_map/back_over_y/ppermute | solution.py:42
  57.6 2.1 %collective-permute-done.22.b2 = bf16[128,256]{1,0:T(8,128)(2,1)S(1)} collective-permute-done((bf16[128,256]{1,0:T(8,128)(2,1)S(1)}, bf16[128,256]{1,0:T(8,128)(2,1)S(1)}, u32[]{:S(2)}, u32[]{:S(2)}) %collective-permute-start.22) | collective-permute-done | bytes 65568 | tf_op jit(solution)/shard_map/back_over_y/ppermute | solution.py:42
  (40 shorter events, 11.8 us)
Async XLA Ops:
  2.6 7.5 %collective-permute-start = (bf16[208,256]{1,0:T(8,128)(2,1)}, bf16[208,256]{1,0:T(8,128)(2,1)S(1)}, u32[]{:S(2)}, u32[]{:S(2)}) collective-permute-start(bf16[208,256]{1,0:T(8,128)(2,1)} %get-tuple-element.38), channel_id=1, source_target_pairs={{0,16},{1,49},{64,80},{65,113},{8,24},{9,57},{72,88},{73,121},{16,... | collective-permute-start | bytes 319496 | tf_op jit(solution)/shard_map/heads_over_y/ppermute | solution.py:42
  4.4 7.3 %collective-permute-start.1 = (bf16[208,256]{1,0:T(8,128)(2,1)}, bf16[208,256]{1,0:T(8,128)(2,1)S(1)}, u32[]{:S(2)}, u32[]{:S(2)}) collective-permute-start(bf16[208,256]{1,0:T(8,128)(2,1)} %get-tuple-element.39), channel_id=1, source_target_pairs={{0,48},{1,17},{64,112},{65,81},{8,56},{9,25},{72,120},{73,89},{16,... | collective-permute-start | bytes 319496 | tf_op jit(solution)/shard_map/heads_over_y/ppermute | solution.py:42
  6.6 6.4 %collective-permute-start.2 = (bf16[208,256]{1,0:T(8,128)(2,1)}, bf16[208,256]{1,0:T(8,128)(2,1)S(1)}, u32[]{:S(2)}, u32[]{:S(2)}) collective-permute-start(bf16[208,256]{1,0:T(8,128)(2,1)} %get-tuple-element.40), channel_id=1, source_target_pairs={{0,32},{1,33},{64,96},{65,97},{8,40},{9,41},{72,104},{73,105},{16,... | collective-permute-start | bytes 319496 | tf_op jit(solution)/shard_map/heads_over_y/ppermute | solution.py:42
  9.2 0.9 %copy-start = (bf16[208,256]{1,0:T(8,128)(2,1)S(1)}, bf16[208,256]{1,0:T(8,128)(2,1)}, u32[]{:S(2)}) copy-start(bf16[208,256]{1,0:T(8,128)(2,1)} %pack.3.source) | copy-start | bytes 319492
  13.0 9.4 %collective-permute-start.7 = (bf16[528,256]{1,0:T(8,128)(2,1)S(1)}, bf16[528,256]{1,0:T(8,128)(2,1)S(1)}, u32[]{:S(2)}, u32[]{:S(2)}) collective-permute-start(bf16[528,256]{1,0:T(8,128)(2,1)S(1)} %get-tuple-element.42.refs_2_), channel_id=1, source_target_pairs={{0,2},{1,7},{64,66},{65,71},{8,10},{9,15},{72,74},{73,79},{16,18},... | collective-permute-start | bytes 811016 | tf_op jit(solution)/shard_map/queries_over_x/ppermute | solution.py:42
  14.6 12.7 %collective-permute-start.4 = (bf16[528,256]{1,0:T(8,128)(2,1)S(1)}, bf16[528,256]{1,0:T(8,128)(2,1)S(1)}, u32[]{:S(2)}, u32[]{:S(2)}) collective-permute-start(bf16[528,256]{1,0:T(8,128)(2,1)S(1)} %get-tuple-element.42.refs_2_), channel_id=1, source_target_pairs={{0,6},{1,3},{64,70},{65,67},{8,14},{9,11},{72,78},{73,75},{16,22},... | collective-permute-start | bytes 811016 | tf_op jit(solution)/shard_map/queries_over_x/ppermute | solution.py:42
  16.7 6.9 %collective-permute-start.6 = (bf16[256,256]{1,0:T(8,128)(2,1)S(1)}, bf16[256,256]{1,0:T(8,128)(2,1)S(1)}, u32[]{:S(2)}, u32[]{:S(2)}) collective-permute-start(bf16[256,256]{1,0:T(8,128)(2,1)S(1)} %get-tuple-element.41.refs_0_), channel_id=1, source_target_pairs={{0,8},{1,9},{64,72},{65,73},{8,0},{9,1},{72,64},{73,65},{16,24},{1... | collective-permute-start | bytes 393224 | tf_op jit(solution)/shard_map/keys_over_z/ppermute | solution.py:42
  20.6 6.2 %collective-permute-start.5 = (bf16[256,256]{1,0:T(8,128)(2,1)S(1)}, bf16[256,256]{1,0:T(8,128)(2,1)S(1)}, u32[]{:S(2)}, u32[]{:S(2)}) collective-permute-start(bf16[256,256]{1,0:T(8,128)(2,1)S(1)} %get-tuple-element.41.refs_0_), channel_id=1, source_target_pairs={{0,72},{1,65},{64,8},{65,1},{8,64},{9,73},{72,0},{73,9},{16,88},{1... | collective-permute-start | bytes 393224 | tf_op jit(solution)/shard_map/keys_over_z/ppermute | solution.py:42
  21.3 5.5 %collective-permute-start.3 = (bf16[256,256]{1,0:T(8,128)(2,1)S(1)}, bf16[256,256]{1,0:T(8,128)(2,1)S(1)}, u32[]{:S(2)}, u32[]{:S(2)}) collective-permute-start(bf16[256,256]{1,0:T(8,128)(2,1)S(1)} %get-tuple-element.41.refs_0_), channel_id=1, source_target_pairs={{0,64},{1,73},{64,0},{65,9},{8,72},{9,65},{72,8},{73,1},{16,80},{1... | collective-permute-start | bytes 393224 | tf_op jit(solution)/shard_map/keys_over_z/ppermute | solution.py:42
  22.5 9.2 %collective-permute-start.8 = (bf16[528,256]{1,0:T(8,128)(2,1)S(1)}, bf16[528,256]{1,0:T(8,128)(2,1)S(1)}, u32[]{:S(2)}, u32[]{:S(2)}) collective-permute-start(bf16[528,256]{1,0:T(8,128)(2,1)S(1)} %collective-permute-done.7.refs_3_), channel_id=1, source_target_pairs={{0,6},{1,3},{64,70},{65,67},{8,14},{9,11},{72,78},{73,75},{16,22},... | collective-permute-start | bytes 811016 | tf_op jit(solution)/shard_map/queries_over_x/ppermute | solution.py:42
  23.6 5.2 %collective-permute-start.12 = (bf16[256,256]{1,0:T(8,128)(2,1)S(1)}, bf16[256,256]{1,0:T(8,128)(2,1)S(1)}, u32[]{:S(2)}, u32[]{:S(2)}) collective-permute-start(bf16[256,256]{1,0:T(8,128)(2,1)S(1)} %collective-permute-done.6.refs_1_.refs_3_), channel_id=1, source_target_pairs={{0,1},{1,0},{64,65},{65,64},{8,9},{9,8},{72,73},{73,72},{16,17},{1... | collective-permute-start | bytes 393224 | tf_op jit(solution)/shard_map/keys_over_z/ppermute | solution.py:42
  26.7 2.0 %collective-permute-start.11 = (bf16[256,256]{1,0:T(8,128)(2,1)S(1)}, bf16[256,256]{1,0:T(8,128)(2,1)S(1)}, u32[]{:S(2)}, u32[]{:S(2)}) collective-permute-start(bf16[256,256]{1,0:T(8,128)(2,1)S(1)} %collective-permute-done.5.refs_0_.refs_2_), channel_id=1, source_target_pairs={{0,1},{1,0},{64,65},{65,64},{8,9},{9,8},{72,73},{73,72},{16,17},{1... | collective-permute-start | bytes 393224 | tf_op jit(solution)/shard_map/keys_over_z/ppermute | solution.py:42
  26.7 3.5 %collective-permute-start.9 = (bf16[256,256]{1,0:T(8,128)(2,1)S(1)}, bf16[256,256]{1,0:T(8,128)(2,1)S(1)}, u32[]{:S(2)}, u32[]{:S(2)}) collective-permute-start(bf16[256,256]{1,0:T(8,128)(2,1)S(1)} %get-tuple-element.41.refs_0_), channel_id=1, source_target_pairs={{0,1},{1,0},{64,65},{65,64},{8,9},{9,8},{72,73},{73,72},{16,17},{1... | collective-permute-start | bytes 393224 | tf_op jit(solution)/shard_map/keys_over_z/ppermute | solution.py:42
  27.3 3.0 %collective-permute-start.10 = (bf16[256,256]{1,0:T(8,128)(2,1)S(1)}, bf16[256,256]{1,0:T(8,128)(2,1)S(1)}, u32[]{:S(2)}, u32[]{:S(2)}) collective-permute-start(bf16[256,256]{1,0:T(8,128)(2,1)S(1)} %collective-permute-done.3.refs_1_), channel_id=1, source_target_pairs={{0,1},{1,0},{64,65},{65,64},{8,9},{9,8},{72,73},{73,72},{16,17},{1... | collective-permute-start | bytes 393224 | tf_op jit(solution)/shard_map/keys_over_z/ppermute | solution.py:42
  34.4 2.1 %collective-permute-start.13 = (bf16[512,256]{1,0:T(8,128)(2,1)S(1)}, bf16[512,256]{1,0:T(8,128)(2,1)S(1)}, u32[]{:S(2)}, u32[]{:S(2)}) collective-permute-start(bf16[512,256]{1,0:T(8,128)(2,1)S(1)} %get-tuple-element.56), channel_id=1, source_target_pairs={{0,1},{1,0},{64,65},{65,64},{8,9},{9,8},{72,73},{73,72},{16,17},{1... | collective-permute-start | bytes 786440 | tf_op jit(solution)/shard_map/sum_keys_over_core/ppermute | solution.py:42
  36.4 10.2 %collective-permute-start.16 = (bf16[512,256]{1,0:T(8,128)(2,1)S(1)}, bf16[512,256]{1,0:T(8,128)(2,1)S(1)}, u32[]{:S(2)}, u32[]{:S(2)}) collective-permute-start(bf16[512,256]{1,0:T(8,128)(2,1)S(1)} %get-tuple-element.64), channel_id=1, source_target_pairs={{0,1},{1,0},{64,65},{65,64},{8,9},{9,8},{72,73},{73,72},{16,17},{1... | collective-permute-start | bytes 786440 | tf_op jit(solution)/shard_map/sum_keys_over_core/ppermute | solution.py:42
  36.6 10.0 %collective-permute-start.17 = (bf16[512,256]{1,0:T(8,128)(2,1)S(1)}, bf16[512,256]{1,0:T(8,128)(2,1)S(1)}, u32[]{:S(2)}, u32[]{:S(2)}) collective-permute-start(bf16[512,256]{1,0:T(8,128)(2,1)S(1)} %sum_keys_over_core.1), channel_id=1, source_target_pairs={{0,72},{1,65},{64,8},{65,1},{8,64},{9,73},{72,0},{73,9},{16,88},{1... | collective-permute-start | bytes 786440 | tf_op jit(solution)/shard_map/sum_keys_over_z/ppermute | solution.py:42
  40.8 8.5 %collective-permute-start.14 = (bf16[512,128]{1,0:T(8,128)(2,1)S(1)}, bf16[512,128]{1,0:T(8,128)(2,1)S(1)}, u32[]{:S(2)}, u32[]{:S(2)}) collective-permute-start(bf16[512,128]{1,0:T(8,128)(2,1)S(1)} %get-tuple-element.58), channel_id=1, source_target_pairs={{0,6},{1,3},{64,70},{65,67},{8,14},{9,11},{72,78},{73,75},{16,22},... | collective-permute-start | bytes 393224 | tf_op jit(solution)/shard_map/sum_queries_over_x/ppermute | solution.py:42
  41.9 7.5 %collective-permute-start.15 = (bf16[512,128]{1,0:T(8,128)(2,1)S(1)}, bf16[512,128]{1,0:T(8,128)(2,1)S(1)}, u32[]{:S(2)}, u32[]{:S(2)}) collective-permute-start(bf16[512,128]{1,0:T(8,128)(2,1)S(1)} %get-tuple-element.59), channel_id=1, source_target_pairs={{0,4},{1,5},{64,68},{65,69},{8,12},{9,13},{72,76},{73,77},{16,20},... | collective-permute-start | bytes 393224 | tf_op jit(solution)/shard_map/sum_queries_over_x/ppermute | solution.py:42
  44.6 5.0 %collective-permute-start.19 = (bf16[512,128]{1,0:T(8,128)(2,1)S(1)}, bf16[512,128]{1,0:T(8,128)(2,1)S(1)}, u32[]{:S(2)}, u32[]{:S(2)}) collective-permute-start(bf16[512,128]{1,0:T(8,128)(2,1)S(1)} %get-tuple-element.68), channel_id=1, source_target_pairs={{0,2},{1,7},{64,66},{65,71},{8,10},{9,15},{72,74},{73,79},{16,18},... | collective-permute-start | bytes 393224 | tf_op jit(solution)/shard_map/sum_queries_over_x/ppermute | solution.py:42
  46.7 5.0 %collective-permute-start.18 = (bf16[256,256]{1,0:T(8,128)(2,1)S(1)}, bf16[256,256]{1,0:T(8,128)(2,1)S(1)}, u32[]{:S(2)}, u32[]{:S(2)}) collective-permute-start(bf16[256,256]{1,0:T(8,128)(2,1)S(1)} %get-tuple-element.67), channel_id=1, source_target_pairs={{0,64},{1,73},{64,0},{65,9},{8,72},{9,65},{72,8},{73,1},{16,80},{1... | collective-permute-start | bytes 393224 | tf_op jit(solution)/shard_map/sum_keys_over_z/ppermute | solution.py:42
  51.8 4.5 %collective-permute-start.20 = (bf16[128,256]{1,0:T(8,128)(2,1)S(1)}, bf16[128,256]{1,0:T(8,128)(2,1)S(1)}, u32[]{:S(2)}, u32[]{:S(2)}) collective-permute-start(bf16[128,256]{1,0:T(8,128)(2,1)S(1)} %get-tuple-element.70), channel_id=1, source_target_pairs={{0,16},{1,49},{64,80},{65,113},{8,24},{9,57},{72,88},{73,121},{16,... | collective-permute-start | bytes 196616 | tf_op jit(solution)/shard_map/back_over_y/ppermute | solution.py:42
  52.1 5.5 %collective-permute-start.21 = (bf16[128,256]{1,0:T(8,128)(2,1)S(1)}, bf16[128,256]{1,0:T(8,128)(2,1)S(1)}, u32[]{:S(2)}, u32[]{:S(2)}) collective-permute-start(bf16[128,256]{1,0:T(8,128)(2,1)S(1)} %get-tuple-element.71), channel_id=1, source_target_pairs={{0,48},{1,17},{64,112},{65,81},{8,56},{9,25},{72,120},{73,89},{16,... | collective-permute-start | bytes 196616 | tf_op jit(solution)/shard_map/back_over_y/ppermute | solution.py:42
  53.9 5.8 %collective-permute-start.22 = (bf16[128,256]{1,0:T(8,128)(2,1)S(1)}, bf16[128,256]{1,0:T(8,128)(2,1)S(1)}, u32[]{:S(2)}, u32[]{:S(2)}) collective-permute-start(bf16[128,256]{1,0:T(8,128)(2,1)S(1)} %get-tuple-element.72), channel_id=1, source_target_pairs={{0,32},{1,33},{64,96},{65,97},{8,40},{9,41},{72,104},{73,105},{16,... | collective-permute-start | bytes 196616 | tf_op jit(solution)/shard_map/back_over_y/ppermute | solution.py:42

commit v4 on v3

--- a/solution.py
+++ b/solution.py
@@ -25,6 +25,7 @@
 FACTOR = 1.0 / math.sqrt(DH)
 LOG2E = math.log2(math.e)
 VMEM = pl.BlockSpec(memory_space=pltpu.VMEM)
+HBM = pl.BlockSpec(memory_space=pltpu.HBM)
 NT = (((1,), (1,)), ((), ()))
 
 
@@ -53,16 +54,16 @@
     return (place + (1 if up else -1)) % 4
 
 
-def swap_y(value, kind):
+def swap_heads(value, kind):
     return move(value, lambda x, y, z, c: (x, partner(y, c, kind), z, c))
 
 
-def swap_x(value, kind):
+def swap_queries(value, kind):
+    return move(value, lambda x, y, z, c: (x, y, partner(z, c, kind), c))
+
+
+def swap_keys(value, kind):
     return move(value, lambda x, y, z, c: (partner(x, c, kind), y, z, c))
-
-
-def swap_z(value, kind):
-    return move(value, lambda x, y, z, c: (x, y, partner(z, c, kind), c))
 
 
 def three_parts(value):
@@ -83,33 +84,55 @@
 
 
 def pack_kernel(kinds, *refs):
-    blocks, bufs, sem = refs[6:-7], refs[-7:-1], refs[-1]
-    copies = [pltpu.make_async_copy(refs[i], bufs[i], sem.at[i]) for i in range(6)]
-    for copy in copies:
+    count = len(kinds)
+    sources, blocks = refs[:6], refs[6 : 6 + count]
+    bufs, built, in_sem, out_sem = refs[6 + count : 12 + count], *refs[12 + count :]
+    loads = [
+        pltpu.make_async_copy(source, buf, in_sem.at[i])
+        for i, (source, buf) in enumerate(zip(sources, bufs))
+    ]
+    for copy in loads:
         copy.start()
-    for copy in copies:
+    q_buf, k_buf, v_buf, g_buf, o_buf, lse_buf = bufs
+    heads = [head_of(kind) for kind in kinds]
+    columns = [pl.ds(pl.multiple_of(head * DH, DH), DH) for head in heads]
+    sends = []
+
+    def send(j, part, first, rows):
+        copy = pltpu.make_async_copy(
+            built.at[j, pl.ds(first, rows), :],
+            blocks[j].at[pl.ds(first, rows), :],
+            out_sem.at[2 * j + part],
+        )
+        copy.start()
+        sends.append(copy)
+
+    for copy in loads[:4]:
         copy.wait()
-    q_ref, k_ref, v_ref, o_ref, g_ref, lse_ref = bufs
-    for kind, block in zip(kinds, blocks):
-        head = head_of(kind)
-        cols = pl.ds(pl.multiple_of(head * DH, DH), DH)
-        g = g_ref[:, cols]
-        block[:QR, :DH] = q_ref[:, cols]
-        block[:QR, DH:] = g
-        block[QR : QR + KR, :DH] = k_ref[:, cols]
-        block[QR : QR + KR, DH:] = v_ref[:, cols]
-        product = g.astype(F32) * o_ref[:, cols].astype(F32)
+    for j, cols in enumerate(columns):
+        built[j, :QR, :DH] = q_buf[:, cols]
+        built[j, :QR, DH:] = g_buf[:, cols]
+        built[j, QR : QR + KR, :DH] = k_buf[:, cols]
+        built[j, QR : QR + KR, DH:] = v_buf[:, cols]
+        send(j, 0, 0, QR + KR)
+    for copy in loads[4:]:
+        copy.wait()
+    for j, (head, cols) in enumerate(zip(heads, columns)):
+        product = g_buf[:, cols].astype(F32) * o_buf[:, cols].astype(F32)
         delta = jnp.sum(product.T, axis=0, keepdims=True)
-        both = jnp.concatenate([lse_ref[pl.ds(head, 1), :], delta], axis=1)
+        both = jnp.concatenate([lse_buf[pl.ds(head, 1), :], delta], axis=1)
         rows = three_parts(both) + [jnp.zeros((AUX - 3, 2 * DH), F32)]
-        block[QR + KR :, :] = jnp.concatenate(rows, axis=0).astype(BF16)
+        built[j, QR + KR :, :] = jnp.concatenate(rows, axis=0).astype(BF16)
+        send(j, 1, QR + KR, AUX)
+    for copy in sends:
+        copy.wait()
 
 
 def copy_kernel(source, out):
     out[...] = source[...]
 
 
-def join_kernel(b0, b1, b3, b2, q_out, kv_out):
+def join_kernel(b2, b0, b1, b3, q_out, kv_out):
     aux = []
     for j, block in enumerate((b0, b1, b2, b3)):
         q_out[j * QR : (j + 1) * QR, :] = block[:QR, :]
@@ -204,7 +227,7 @@
         dv[:, cols] = block[KR:, DH:].astype(F32)
 
 
-def call(kernel, outs, args, scratch=(), flops=0, space=VMEM, limit=40):
+def call(kernel, outs, args, scratch=(), flops=0, space=VMEM, out_space=VMEM, limit=40):
     total = sum(a.size * a.dtype.itemsize for a in args) + sum(
         math.prod(shape) * jnp.dtype(kind).itemsize for shape, kind in outs
     )
@@ -212,7 +235,7 @@
         kernel,
         out_shape=[jax.ShapeDtypeStruct(shape, kind) for shape, kind in outs],
         in_specs=[space] * len(args),
-        out_specs=[VMEM] * len(outs),
+        out_specs=[out_space] * len(outs),
         scratch_shapes=list(scratch),
         compiler_params=pltpu.CompilerParams(vmem_limit_bytes=limit * 1024 * 1024),
         cost_estimate=pl.CostEstimate(flops=flops, bytes_accessed=total, transcendentals=0),
@@ -240,37 +263,38 @@
 
 
 def per_device(queries, keys, values, outputs, d_out, lse):
-    args = (queries, keys, values, outputs, d_out, lse)
+    args = (queries, keys, values, d_out, outputs, lse)
     with jax.named_scope("pack"):
-        scratch = [pltpu.VMEM(a.shape, a.dtype) for a in args] + [pltpu.SemaphoreType.DMA((6,))]
-        place = pl.BlockSpec(memory_space=pltpu.HBM)
-        far, first, second = call(
-            functools.partial(pack_kernel, (2, 0, 1)),
-            [((BLK, 2 * DH), BF16)] * 3,
-            args,
-            scratch=scratch,
-            space=place,
-            limit=56,
-        )
-        here = call(
-            functools.partial(pack_kernel, (None,)),
-            [((BLK, 2 * DH), BF16)],
-            args,
-            scratch=scratch,
-            space=place,
-            limit=56,
-        )[0]
+        def pack(kinds):
+            count = len(kinds)
+            return call(
+                functools.partial(pack_kernel, kinds),
+                [((BLK, 2 * DH), BF16)] * count,
+                args,
+                scratch=[pltpu.VMEM(a.shape, a.dtype) for a in args]
+                + [
+                    pltpu.VMEM((count, BLK, 2 * DH), BF16),
+                    pltpu.SemaphoreType.DMA((6,)),
+                    pltpu.SemaphoreType.DMA((2 * count,)),
+                ],
+                space=HBM,
+                out_space=HBM,
+                limit=56,
+            )
+
+        far, first, second = pack((2, 0, 1))
+        here = pack((None,))[0]
         here = call(copy_kernel, [((BLK, 2 * DH), BF16)], (here,))[0]
-    with jax.named_scope("heads_over_y"):
-        blocks = [here, swap_y(first, 0), swap_y(second, 1), swap_y(far, 2)]
+    with jax.named_scope("heads_to_chips"):
+        blocks = [swap_heads(far, 2), here, swap_heads(first, 0), swap_heads(second, 1)]
     with jax.named_scope("join"):
         q, kv = call(join_kernel, [((QS + AUX, 2 * DH), BF16), ((KS, 2 * DH), BF16)], blocks)
-    with jax.named_scope("queries_over_x"):
-        q1 = swap_x(q, 0)
-        q2 = swap_x(q, 1)
-        q3 = swap_x(q1, 1)
-    with jax.named_scope("keys_over_z"):
-        near = [(kv, swap_z(kv, 0)), (swap_z(kv, 1), swap_z(kv, 2))]
+    with jax.named_scope("gather_queries"):
+        q1 = swap_queries(q, 0)
+        q2 = swap_queries(q, 1)
+        q3 = swap_queries(q1, 1)
+    with jax.named_scope("gather_keys"):
+        near = [(kv, swap_keys(kv, 0)), (swap_keys(kv, 1), swap_keys(kv, 2))]
         k_a, k_b = near
         o_a, o_b = [tuple(other_core(piece) for piece in pair) for pair in near]
     sums = [((DH, 2 * QS), F32)]
@@ -278,9 +302,7 @@
     q2, k_b = lax.optimization_barrier((q2, k_b))
     with jax.named_scope("attend_a_b"):
         (dq_a,), (dkv_b,) = attend(q_a, (k_b,), None, None, sums, (F32,))
-        (dq_a,), (dko_b,) = attend(q_a, (o_b,), dq_a, None, sums, (F32,))
-    with jax.named_scope("attend_a_a_other"):
-        (dq_a,), (dko_a,) = attend(q_a, (o_a,), dq_a, None, sums, (F32,))
+        (dq_a,), (dko_b, dko_a) = attend(q_a, (o_b, o_a), dq_a, None, sums, (F32,) * 2)
     q3, dq_a = lax.optimization_barrier((q3, dq_a))
     q_b = (q2, q3)
     with jax.named_scope("attend_b_b"):
@@ -292,33 +314,33 @@
     dq_b, sent_b = lax.optimization_barrier((dq_b, sent_b))
     with jax.named_scope("attend_b_a"):
         (dq2, dq3), (dkv_a,) = attend(q_b, (k_a,), dq_b, None, [((QS, DH), BF16)] * 2, (F32,))
-    with jax.named_scope("sum_queries_over_x"):
-        got2, got3 = swap_x(dq2, 1), swap_x(dq3, 2)
-    with jax.named_scope("sum_keys_over_z"):
-        got_b = swap_z(sent_b, 1)
+    with jax.named_scope("sum_queries"):
+        got2, got3 = swap_queries(dq2, 1), swap_queries(dq3, 2)
+    with jax.named_scope("sum_keys"):
+        got_b = swap_keys(sent_b, 1)
     with jax.named_scope("sum_keys_over_core"):
         got_other = other_core(dko_a)
     with jax.named_scope("attend_a_a"):
         (dq0, dq1), (dkv_own,) = attend(
             q_a, (k_a,), dq_a, (dkv_a,), [((QS, DH), F32), ((QS, DH), BF16)], (F32,)
         )
-    with jax.named_scope("sum_queries_over_x"):
-        got1 = swap_x(dq1, 0)
+    with jax.named_scope("sum_queries"):
+        got1 = swap_queries(dq1, 0)
         got23 = call(add_kernel, [((QS, DH), F32)], (got2, got3), flops=LATE)[0]
-    with jax.named_scope("sum_keys_over_z"):
+    with jax.named_scope("sum_keys"):
         k_own, k_sent = call(
             split_kernel, [((KS, 2 * DH), F32), ((KS, 2 * DH), BF16)], (dkv_own, got_other, got_b)
         )
-        k_got = swap_z(k_sent, 0)
+        k_got = swap_keys(k_sent, 0)
     with jax.named_scope("chip_sum"):
         backs = call(
             chip_sum_kernel,
             [((2 * KR, 2 * DH), F32)] + [((2 * KR, 2 * DH), BF16)] * 3,
             (got23, dq0, k_own, k_got, got1),
         )
-    with jax.named_scope("back_over_y"):
-        far = swap_y(backs[2], 2)
-        backs = [backs[0], swap_y(backs[1], 0), swap_y(backs[3], 1), far]
+    with jax.named_scope("back_to_rows"):
+        far = swap_heads(backs[2], 2)
+        backs = [backs[0], swap_heads(backs[1], 0), swap_heads(backs[3], 1), far]
     with jax.named_scope("unpack"):
         return tuple(
             call(

time: 60.7 us -> 60.1 us (level)
  waiting for transfers between devices: 16.4 us -> 14.6 us
  starting transfers between devices: 26 us -> 27.5 us
    ppermute x23, waiting for transfers between devices: 16.4 us -> 14.6 us  [move(): return lax.ppermute(value, AXES, pairs)]
    ppermute x23, starting transfers between devices: 26 us -> 27.5 us  [move(): return lax.ppermute(value, AXES, pairs)]
    pallas_call x16 -> x15, Pallas kernels: 16.4 us -> 16.1 us  [call(): pl.pallas_call(kernel, out_shape=[jax.ShapeDtypeStruct(shape, kind) for s...]
where the time goes in v4:
time: 60.1 us; the launch traced here: 60 us
  starting transfers between devices  27.5 us (46%)
  Pallas kernels  16.1 us (27%)
  waiting for transfers between devices  14.6 us (24%)
  local copies, waits for them, and re-layouts  0.89 us (1%)
  between operations  0.8 us (1%)
    ppermute x23, starting transfers between devices, move(): return lax.ppermute(value, AXES, pairs)  27.5 us
    pallas_call x15, Pallas kernels, call(): pl.pallas_call(kernel, out_shape=[jax.ShapeDtypeStruct(shape, kind) for s...  16.1 us
    ppermute x23, waiting for transfers between devices, move(): return lax.ppermute(value, AXES, pairs)  14.6 us
  transfers between devices with their start and end apart: 23, of which 11 were waited for; matrix products, arithmetic and copies ran while one was open for 0% of the time, Pallas kernels for 18%

profile of v4, /device:TPU:0, one launch (start us, length us, event | category | flops | bytes accessed | tf_op | source)
XLA Modules:
  0.0 60.0 jit_solution(3606054266934377118)
XLA Ops:
  0.6 2.0 %pack.3 = (bf16[208,256]{1,0:T(8,128)(2,1)}, bf16[208,256]{1,0:T(8,128)(2,1)}, bf16[208,256]{1,0:T(8,128)(2,1)}) custom-call(bf16[128,512]{1,0:T(8,128)(2,1)} %refs_0_.3, bf16[64,512]{1,0:T(8,128)(2,1)} %refs_1_.3, bf16[64,512]{1,0:T(8,128)(2,1)} %refs_2_.3, bf16[128,512]{1,0:T(8,128)(2,1)} %refs_3_.3, bf16[128,512]{1,0:T(8,128)(2,1)} %refs_4_.3, ...), custom_call_target="tpu_custom_call" | custom-call | bytes 845824 | tf_op jit(solution)/shard_map/pack/pallas_call | solution.py:234
  2.6 3.4 %collective-permute-start = (bf16[208,256]{1,0:T(8,128)(2,1)}, bf16[208,256]{1,0:T(8,128)(2,1)S(1)}, u32[]{:S(2)}, u32[]{:S(2)}) collective-permute-start(bf16[208,256]{1,0:T(8,128)(2,1)} %get-tuple-element.37), channel_id=1, source_target_pairs={{0,32},{1,33},{64,96},{65,97},{8,40},{9,41},{72,104},{73,105},{16,... | collective-permute-start | bytes 319496 | tf_op jit(solution)/shard_map/heads_to_chips/ppermute | solution.py:43
  7.0 1.9 %pack.4.source = bf16[208,256]{1,0:T(8,128)(2,1)} custom-call(bf16[128,512]{1,0:T(8,128)(2,1)} %refs_0_.3, bf16[64,512]{1,0:T(8,128)(2,1)} %refs_1_.3, bf16[64,512]{1,0:T(8,128)(2,1)} %refs_2_.3, bf16[128,512]{1,0:T(8,128)(2,1)} %refs_3_.3, bf16[128,512]{1,0:T(8,128)(2,1)} %refs_4_.3, f32[4,128]{1,0:T(4,128)} %refs_5_.3), custom_call_target="tpu_custom_call" | custom-call | bytes 632832 | tf_op jit(solution)/shard_map/pack/pallas_call | solution.py:234
  9.8 2.0 %collective-permute-done.1.b1 = bf16[208,256]{1,0:T(8,128)(2,1)S(1)} collective-permute-done((bf16[208,256]{1,0:T(8,128)(2,1)}, bf16[208,256]{1,0:T(8,128)(2,1)S(1)}, u32[]{:S(2)}, u32[]{:S(2)}) %collective-permute-start.1) | collective-permute-done | bytes 106528 | tf_op jit(solution)/shard_map/heads_to_chips/ppermute | solution.py:43
  12.8 2.0 %collective-permute-start.7 = (bf16[528,256]{1,0:T(8,128)(2,1)S(1)}, bf16[528,256]{1,0:T(8,128)(2,1)S(1)}, u32[]{:S(2)}, u32[]{:S(2)}) collective-permute-start(bf16[528,256]{1,0:T(8,128)(2,1)S(1)} %get-tuple-element.41.refs_2_.refs_4_), channel_id=1, source_target_pairs={{0,64},{1,73},{64,0},{65,9},{8,72},{9,65},{72,8},{73,1},{16,80},{1... | collective-permute-start | bytes 811016 | tf_op jit(solution)/shard_map/gather_queries/ppermute | solution.py:43
  14.8 2.5 %collective-permute-start.4 = (bf16[528,256]{1,0:T(8,128)(2,1)S(1)}, bf16[528,256]{1,0:T(8,128)(2,1)S(1)}, u32[]{:S(2)}, u32[]{:S(2)}) collective-permute-start(bf16[528,256]{1,0:T(8,128)(2,1)S(1)} %get-tuple-element.41.refs_2_.refs_4_), channel_id=1, source_target_pairs={{0,72},{1,65},{64,8},{65,1},{8,64},{9,73},{72,0},{73,9},{16,88},{1... | collective-permute-start | bytes 811016 | tf_op jit(solution)/shard_map/gather_queries/ppermute | solution.py:43
  17.3 3.0 %collective-permute-start.6 = (bf16[256,256]{1,0:T(8,128)(2,1)S(1)}, bf16[256,256]{1,0:T(8,128)(2,1)S(1)}, u32[]{:S(2)}, u32[]{:S(2)}) collective-permute-start(bf16[256,256]{1,0:T(8,128)(2,1)S(1)} %get-tuple-element.40.refs_0_), channel_id=1, source_target_pairs={{0,4},{1,5},{64,68},{65,69},{8,12},{9,13},{72,76},{73,77},{16,20},... | collective-permute-start | bytes 393224 | tf_op jit(solution)/shard_map/gather_keys/ppermute | solution.py:43
  20.3 1.1 %collective-permute-start.5 = (bf16[256,256]{1,0:T(8,128)(2,1)S(1)}, bf16[256,256]{1,0:T(8,128)(2,1)S(1)}, u32[]{:S(2)}, u32[]{:S(2)}) collective-permute-start(bf16[256,256]{1,0:T(8,128)(2,1)S(1)} %get-tuple-element.40.refs_0_), channel_id=1, source_target_pairs={{0,6},{1,3},{64,70},{65,67},{8,14},{9,11},{72,78},{73,75},{16,22},... | collective-permute-start | bytes 393224 | tf_op jit(solution)/shard_map/gather_keys/ppermute | solution.py:43
  21.7 2.4 %collective-permute-start.8 = (bf16[528,256]{1,0:T(8,128)(2,1)S(1)}, bf16[528,256]{1,0:T(8,128)(2,1)S(1)}, u32[]{:S(2)}, u32[]{:S(2)}) collective-permute-start(bf16[528,256]{1,0:T(8,128)(2,1)S(1)} %collective-permute-done.7.refs_3_.refs_5_), channel_id=1, source_target_pairs={{0,72},{1,65},{64,8},{65,1},{8,64},{9,73},{72,0},{73,9},{16,88},{1... | collective-permute-start | bytes 811016 | tf_op jit(solution)/shard_map/gather_queries/ppermute | solution.py:43
  24.1 2.4 %collective-permute-done.5.refs_0_.refs_2_ = bf16[256,256]{1,0:T(8,128)(2,1)S(1)} collective-permute-done((bf16[256,256]{1,0:T(8,128)(2,1)S(1)}, bf16[256,256]{1,0:T(8,128)(2,1)S(1)}, u32[]{:S(2)}, u32[]{:S(2)}) %collective-permute-start.5) | collective-permute-done | bytes 131104 | tf_op jit(solution)/shard_map/gather_keys/ppermute | solution.py:43
  27.1 1.4 %attend_a_b.2 = (f32[512,256]{1,0:T(8,128)S(1)}, f32[128,1024]{1,0:T(8,128)S(1)}) custom-call(bf16[256,256]{1,0:T(8,128)(2,1)S(1)} %collective-permute-done.5.refs_0_.refs_2_, bf16[256,256]{1,0:T(8,128)(2,1)S(1)} %collective-permute-done.6.refs_1_.refs_3_, bf16[528,256]{1,0:T(8,128)(2,1)S(1)} %get-tuple-element.41.refs_2_.refs_4_, ...), custom_call_target="tpu_custom_call" | custom-call | flops 671088640 | bytes 1851392 | tf_op jit(solution)/shard_map/attend_a_b/pallas_call | solution.py:234
  28.6 2.7 %attend_a_b.3 = (f32[512,256]{1,0:T(8,128)S(1)}, f32[512,256]{1,0:T(8,128)S(1)}, f32[128,1024]{1,0:T(8,128)S(1)}) custom-call(bf16[256,256]{1,0:T(8,128)(2,1)S(1)} %collective-permute-done.9.refs_0_, bf16[256,256]{1,0:T(8,128)(2,1)S(1)} %collective-permute-done.10.refs_1_, bf16[256,256]{1,0:T(8,128)(2,1)S(1)} %collective-permute-done.11.refs_2_.refs_0_, ...), custom_call_target="tpu_custom_call" | custom-call | flops 1342177280 | bytes 3162112 | tf_op jit(solution)/shard_map/attend_a_b/pallas_call | solution.py:234
  31.3 2.7 %attend_b_b.1 = (bf16[512,256]{1,0:T(8,128)(2,1)S(1)}, f32[512,256]{1,0:T(8,128)S(1)}, f32[128,1024]{1,0:T(8,128)S(1)}) custom-call(bf16[256,256]{1,0:T(8,128)(2,1)S(1)} %collective-permute-done.9.refs_0_, bf16[256,256]{1,0:T(8,128)(2,1)S(1)} %collective-permute-done.10.refs_1_, bf16[256,256]{1,0:T(8,128)(2,1)S(1)} %collective-permute-done.5.refs_0_.refs_2_, ...), custom_call_target="tpu_custom_call" | custom-call | flops 1342177280 | bytes 3424256 | tf_op jit(solution)/shard_map/attend_b_b/pallas_call | solution.py:234
  34.5 1.5 %attend_b_a_other.1 = (bf16[512,256]{1,0:T(8,128)(2,1)S(1)}, f32[128,1024]{1,0:T(8,128)S(1)}) custom-call(bf16[256,256]{1,0:T(8,128)(2,1)S(1)} %collective-permute-done.11.refs_2_.refs_0_, bf16[256,256]{1,0:T(8,128)(2,1)S(1)} %collective-permute-done.12.refs_3_.refs_1_, bf16[528,256]{1,0:T(8,128)(2,1)S(1)} %collective-permute-done.4.refs_4_.refs_2_, ...), custom_call_target="tpu_custom_call" | custom-call | flops 671088640 | bytes 2637824 | tf_op jit(solution)/shard_map/attend_b_a_other/pallas_call | solution.py:234
  36.2 2.2 %collective-permute-start.17 = (bf16[512,256]{1,0:T(8,128)(2,1)S(1)}, bf16[512,256]{1,0:T(8,128)(2,1)S(1)}, u32[]{:S(2)}, u32[]{:S(2)}) collective-permute-start(bf16[512,256]{1,0:T(8,128)(2,1)S(1)} %sum_keys_over_core.1), channel_id=1, source_target_pairs={{0,6},{1,3},{64,70},{65,67},{8,14},{9,11},{72,78},{73,75},{16,22},... | collective-permute-start | bytes 786440 | tf_op jit(solution)/shard_map/sum_keys/ppermute | solution.py:43
  38.4 1.5 %attend_b_a.1 = (f32[512,256]{1,0:T(8,128)S(1)}, bf16[512,128]{1,0:T(8,128)(2,1)S(1)}, bf16[512,128]{1,0:T(8,128)(2,1)S(1)}) custom-call(bf16[256,256]{1,0:T(8,128)(2,1)S(1)} %get-tuple-element.40.refs_0_, bf16[256,256]{1,0:T(8,128)(2,1)S(1)} %collective-permute-done.3.refs_1_, bf16[528,256]{1,0:T(8,128)(2,1)S(1)} %collective-permute-done.4.refs_4_.refs_2_, ...), custom_call_target="tpu_custom_call" | custom-call | flops 671088640 | bytes 2113536 | tf_op jit(solution)/shard_map/attend_b_a/pallas_call | solution.py:234
  39.9 1.4 %collective-permute-start.14 = (bf16[512,128]{1,0:T(8,128)(2,1)S(1)}, bf16[512,128]{1,0:T(8,128)(2,1)S(1)}, u32[]{:S(2)}, u32[]{:S(2)}) collective-permute-start(bf16[512,128]{1,0:T(8,128)(2,1)S(1)} %get-tuple-element.56), channel_id=1, source_target_pairs={{0,72},{1,65},{64,8},{65,1},{8,64},{9,73},{72,0},{73,9},{16,88},{1... | collective-permute-start | bytes 393224 | tf_op jit(solution)/shard_map/sum_queries/ppermute | solution.py:43
  41.3 1.9 %collective-permute-start.15 = (bf16[512,128]{1,0:T(8,128)(2,1)S(1)}, bf16[512,128]{1,0:T(8,128)(2,1)S(1)}, u32[]{:S(2)}, u32[]{:S(2)}) collective-permute-start(bf16[512,128]{1,0:T(8,128)(2,1)S(1)} %get-tuple-element.57), channel_id=1, source_target_pairs={{0,8},{1,9},{64,72},{65,73},{8,0},{9,1},{72,64},{73,65},{16,24},{1... | collective-permute-start | bytes 393224 | tf_op jit(solution)/shard_map/sum_queries/ppermute | solution.py:43
  43.1 1.5 %attend_a_a.1 = (f32[512,256]{1,0:T(8,128)S(1)}, f32[512,128]{1,0:T(8,128)S(1)}, bf16[512,128]{1,0:T(8,128)(2,1)S(1)}) custom-call(bf16[256,256]{1,0:T(8,128)(2,1)S(1)} %get-tuple-element.40.refs_0_, bf16[256,256]{1,0:T(8,128)(2,1)S(1)} %collective-permute-done.3.refs_1_, bf16[528,256]{1,0:T(8,128)(2,1)S(1)} %get-tuple-element.41.refs_2_.refs_4_, ...), custom_call_target="tpu_custom_call" | custom-call | flops 671088640 | bytes 2768896 | tf_op jit(solution)/shard_map/attend_a_a/pallas_call | solution.py:234
  45.8 2.8 %collective-permute-done.14.a = bf16[512,128]{1,0:T(8,128)(2,1)S(1)} collective-permute-done((bf16[512,128]{1,0:T(8,128)(2,1)S(1)}, bf16[512,128]{1,0:T(8,128)(2,1)S(1)}, u32[]{:S(2)}, u32[]{:S(2)}) %collective-permute-start.14) | collective-permute-done | bytes 131104 | tf_op jit(solution)/shard_map/sum_queries/ppermute | solution.py:43
  51.4 2.0 %collective-permute-start.21 = (bf16[128,256]{1,0:T(8,128)(2,1)S(1)}, bf16[128,256]{1,0:T(8,128)(2,1)S(1)}, u32[]{:S(2)}, u32[]{:S(2)}) collective-permute-start(bf16[128,256]{1,0:T(8,128)(2,1)S(1)} %get-tuple-element.69), channel_id=1, source_target_pairs={{0,48},{1,17},{64,112},{65,81},{8,56},{9,25},{72,120},{73,89},{16,... | collective-permute-start | bytes 196616 | tf_op jit(solution)/shard_map/back_to_rows/ppermute | solution.py:43
  53.3 1.6 %collective-permute-start.22 = (bf16[128,256]{1,0:T(8,128)(2,1)S(1)}, bf16[128,256]{1,0:T(8,128)(2,1)S(1)}, u32[]{:S(2)}, u32[]{:S(2)}) collective-permute-start(bf16[128,256]{1,0:T(8,128)(2,1)S(1)} %get-tuple-element.70), channel_id=1, source_target_pairs={{0,32},{1,33},{64,96},{65,97},{8,40},{9,41},{72,104},{73,105},{16,... | collective-permute-start | bytes 196616 | tf_op jit(solution)/shard_map/back_to_rows/ppermute | solution.py:43
  55.7 1.8 %collective-permute-done.21.b3 = bf16[128,256]{1,0:T(8,128)(2,1)S(1)} collective-permute-done((bf16[128,256]{1,0:T(8,128)(2,1)S(1)}, bf16[128,256]{1,0:T(8,128)(2,1)S(1)}, u32[]{:S(2)}, u32[]{:S(2)}) %collective-permute-start.21) | collective-permute-done | bytes 65568 | tf_op jit(solution)/shard_map/back_to_rows/ppermute | solution.py:43
  57.5 1.6 %collective-permute-done.22.b2 = bf16[128,256]{1,0:T(8,128)(2,1)S(1)} collective-permute-done((bf16[128,256]{1,0:T(8,128)(2,1)S(1)}, bf16[128,256]{1,0:T(8,128)(2,1)S(1)}, u32[]{:S(2)}, u32[]{:S(2)}) %collective-permute-start.22) | collective-permute-done | bytes 65568 | tf_op jit(solution)/shard_map/back_to_rows/ppermute | solution.py:43
  (39 shorter events, 9.9 us)
Async XLA Ops:
  2.6 7.2 %collective-permute-start = (bf16[208,256]{1,0:T(8,128)(2,1)}, bf16[208,256]{1,0:T(8,128)(2,1)S(1)}, u32[]{:S(2)}, u32[]{:S(2)}) collective-permute-start(bf16[208,256]{1,0:T(8,128)(2,1)} %get-tuple-element.37), channel_id=1, source_target_pairs={{0,32},{1,33},{64,96},{65,97},{8,40},{9,41},{72,104},{73,105},{16,... | collective-permute-start | bytes 319496 | tf_op jit(solution)/shard_map/heads_to_chips/ppermute | solution.py:43
  5.9 5.9 %collective-permute-start.1 = (bf16[208,256]{1,0:T(8,128)(2,1)}, bf16[208,256]{1,0:T(8,128)(2,1)S(1)}, u32[]{:S(2)}, u32[]{:S(2)}) collective-permute-start(bf16[208,256]{1,0:T(8,128)(2,1)} %get-tuple-element.38), channel_id=1, source_target_pairs={{0,16},{1,49},{64,80},{65,113},{8,24},{9,57},{72,88},{73,121},{16,... | collective-permute-start | bytes 319496 | tf_op jit(solution)/shard_map/heads_to_chips/ppermute | solution.py:43
  6.6 6.1 %collective-permute-start.2 = (bf16[208,256]{1,0:T(8,128)(2,1)}, bf16[208,256]{1,0:T(8,128)(2,1)S(1)}, u32[]{:S(2)}, u32[]{:S(2)}) collective-permute-start(bf16[208,256]{1,0:T(8,128)(2,1)} %get-tuple-element.39), channel_id=1, source_target_pairs={{0,48},{1,17},{64,112},{65,81},{8,56},{9,25},{72,120},{73,89},{16,... | collective-permute-start | bytes 319496 | tf_op jit(solution)/shard_map/heads_to_chips/ppermute | solution.py:43
  8.9 0.9 %copy-start = (bf16[208,256]{1,0:T(8,128)(2,1)S(1)}, bf16[208,256]{1,0:T(8,128)(2,1)}, u32[]{:S(2)}) copy-start(bf16[208,256]{1,0:T(8,128)(2,1)} %pack.4.source) | copy-start | bytes 319492
  12.8 8.9 %collective-permute-start.7 = (bf16[528,256]{1,0:T(8,128)(2,1)S(1)}, bf16[528,256]{1,0:T(8,128)(2,1)S(1)}, u32[]{:S(2)}, u32[]{:S(2)}) collective-permute-start(bf16[528,256]{1,0:T(8,128)(2,1)S(1)} %get-tuple-element.41.refs_2_.refs_4_), channel_id=1, source_target_pairs={{0,64},{1,73},{64,0},{65,9},{8,72},{9,65},{72,8},{73,1},{16,80},{1... | collective-permute-start | bytes 811016 | tf_op jit(solution)/shard_map/gather_queries/ppermute | solution.py:43
  14.8 12.2 %collective-permute-start.4 = (bf16[528,256]{1,0:T(8,128)(2,1)S(1)}, bf16[528,256]{1,0:T(8,128)(2,1)S(1)}, u32[]{:S(2)}, u32[]{:S(2)}) collective-permute-start(bf16[528,256]{1,0:T(8,128)(2,1)S(1)} %get-tuple-element.41.refs_2_.refs_4_), channel_id=1, source_target_pairs={{0,72},{1,65},{64,8},{65,1},{8,64},{9,73},{72,0},{73,9},{16,88},{1... | collective-permute-start | bytes 811016 | tf_op jit(solution)/shard_map/gather_queries/ppermute | solution.py:43
  17.3 6.8 %collective-permute-start.6 = (bf16[256,256]{1,0:T(8,128)(2,1)S(1)}, bf16[256,256]{1,0:T(8,128)(2,1)S(1)}, u32[]{:S(2)}, u32[]{:S(2)}) collective-permute-start(bf16[256,256]{1,0:T(8,128)(2,1)S(1)} %get-tuple-element.40.refs_0_), channel_id=1, source_target_pairs={{0,4},{1,5},{64,68},{65,69},{8,12},{9,13},{72,76},{73,77},{16,20},... | collective-permute-start | bytes 393224 | tf_op jit(solution)/shard_map/gather_keys/ppermute | solution.py:43
  20.3 6.2 %collective-permute-start.5 = (bf16[256,256]{1,0:T(8,128)(2,1)S(1)}, bf16[256,256]{1,0:T(8,128)(2,1)S(1)}, u32[]{:S(2)}, u32[]{:S(2)}) collective-permute-start(bf16[256,256]{1,0:T(8,128)(2,1)S(1)} %get-tuple-element.40.refs_0_), channel_id=1, source_target_pairs={{0,6},{1,3},{64,70},{65,67},{8,14},{9,11},{72,78},{73,75},{16,22},... | collective-permute-start | bytes 393224 | tf_op jit(solution)/shard_map/gather_keys/ppermute | solution.py:43
  21.5 5.0 %collective-permute-start.3 = (bf16[256,256]{1,0:T(8,128)(2,1)S(1)}, bf16[256,256]{1,0:T(8,128)(2,1)S(1)}, u32[]{:S(2)}, u32[]{:S(2)}) collective-permute-start(bf16[256,256]{1,0:T(8,128)(2,1)S(1)} %get-tuple-element.40.refs_0_), channel_id=1, source_target_pairs={{0,2},{1,7},{64,66},{65,71},{8,10},{9,15},{72,74},{73,79},{16,18},... | collective-permute-start | bytes 393224 | tf_op jit(solution)/shard_map/gather_keys/ppermute | solution.py:43
  21.7 9.6 %collective-permute-start.8 = (bf16[528,256]{1,0:T(8,128)(2,1)S(1)}, bf16[528,256]{1,0:T(8,128)(2,1)S(1)}, u32[]{:S(2)}, u32[]{:S(2)}) collective-permute-start(bf16[528,256]{1,0:T(8,128)(2,1)S(1)} %collective-permute-done.7.refs_3_.refs_5_), channel_id=1, source_target_pairs={{0,72},{1,65},{64,8},{65,1},{8,64},{9,73},{72,0},{73,9},{16,88},{1... | collective-permute-start | bytes 811016 | tf_op jit(solution)/shard_map/gather_queries/ppermute | solution.py:43
  24.1 4.4 %collective-permute-start.11 = (bf16[256,256]{1,0:T(8,128)(2,1)S(1)}, bf16[256,256]{1,0:T(8,128)(2,1)S(1)}, u32[]{:S(2)}, u32[]{:S(2)}) collective-permute-start(bf16[256,256]{1,0:T(8,128)(2,1)S(1)} %get-tuple-element.40.refs_0_), channel_id=1, source_target_pairs={{0,1},{1,0},{64,65},{65,64},{8,9},{9,8},{72,73},{73,72},{16,17},{1... | collective-permute-start | bytes 393224 | tf_op jit(solution)/shard_map/gather_keys/ppermute | solution.py:43
  26.5 2.0 %collective-permute-start.10 = (bf16[256,256]{1,0:T(8,128)(2,1)S(1)}, bf16[256,256]{1,0:T(8,128)(2,1)S(1)}, u32[]{:S(2)}, u32[]{:S(2)}) collective-permute-start(bf16[256,256]{1,0:T(8,128)(2,1)S(1)} %collective-permute-done.6.refs_1_.refs_3_), channel_id=1, source_target_pairs={{0,1},{1,0},{64,65},{65,64},{8,9},{9,8},{72,73},{73,72},{16,17},{1... | collective-permute-start | bytes 393224 | tf_op jit(solution)/shard_map/gather_keys/ppermute | solution.py:43
  26.5 2.0 %collective-permute-start.9 = (bf16[256,256]{1,0:T(8,128)(2,1)S(1)}, bf16[256,256]{1,0:T(8,128)(2,1)S(1)}, u32[]{:S(2)}, u32[]{:S(2)}) collective-permute-start(bf16[256,256]{1,0:T(8,128)(2,1)S(1)} %collective-permute-done.5.refs_0_.refs_2_), channel_id=1, source_target_pairs={{0,1},{1,0},{64,65},{65,64},{8,9},{9,8},{72,73},{73,72},{16,17},{1... | collective-permute-start | bytes 393224 | tf_op jit(solution)/shard_map/gather_keys/ppermute | solution.py:43
  27.0 1.5 %collective-permute-start.12 = (bf16[256,256]{1,0:T(8,128)(2,1)S(1)}, bf16[256,256]{1,0:T(8,128)(2,1)S(1)}, u32[]{:S(2)}, u32[]{:S(2)}) collective-permute-start(bf16[256,256]{1,0:T(8,128)(2,1)S(1)} %collective-permute-done.3.refs_1_), channel_id=1, source_target_pairs={{0,1},{1,0},{64,65},{65,64},{8,9},{9,8},{72,73},{73,72},{16,17},{1... | collective-permute-start | bytes 393224 | tf_op jit(solution)/shard_map/gather_keys/ppermute | solution.py:43
  34.0 2.1 %collective-permute-start.13 = (bf16[512,256]{1,0:T(8,128)(2,1)S(1)}, bf16[512,256]{1,0:T(8,128)(2,1)S(1)}, u32[]{:S(2)}, u32[]{:S(2)}) collective-permute-start(bf16[512,256]{1,0:T(8,128)(2,1)S(1)} %get-tuple-element.54), channel_id=1, source_target_pairs={{0,1},{1,0},{64,65},{65,64},{8,9},{9,8},{72,73},{73,72},{16,17},{1... | collective-permute-start | bytes 786440 | tf_op jit(solution)/shard_map/sum_keys_over_core/ppermute | solution.py:43
  36.0 9.7 %collective-permute-start.16 = (bf16[512,256]{1,0:T(8,128)(2,1)S(1)}, bf16[512,256]{1,0:T(8,128)(2,1)S(1)}, u32[]{:S(2)}, u32[]{:S(2)}) collective-permute-start(bf16[512,256]{1,0:T(8,128)(2,1)S(1)} %get-tuple-element.62), channel_id=1, source_target_pairs={{0,1},{1,0},{64,65},{65,64},{8,9},{9,8},{72,73},{73,72},{16,17},{1... | collective-permute-start | bytes 786440 | tf_op jit(solution)/shard_map/sum_keys_over_core/ppermute | solution.py:43
  36.2 9.4 %collective-permute-start.17 = (bf16[512,256]{1,0:T(8,128)(2,1)S(1)}, bf16[512,256]{1,0:T(8,128)(2,1)S(1)}, u32[]{:S(2)}, u32[]{:S(2)}) collective-permute-start(bf16[512,256]{1,0:T(8,128)(2,1)S(1)} %sum_keys_over_core.1), channel_id=1, source_target_pairs={{0,6},{1,3},{64,70},{65,67},{8,14},{9,11},{72,78},{73,75},{16,22},... | collective-permute-start | bytes 786440 | tf_op jit(solution)/shard_map/sum_keys/ppermute | solution.py:43
  39.9 8.7 %collective-permute-start.14 = (bf16[512,128]{1,0:T(8,128)(2,1)S(1)}, bf16[512,128]{1,0:T(8,128)(2,1)S(1)}, u32[]{:S(2)}, u32[]{:S(2)}) collective-permute-start(bf16[512,128]{1,0:T(8,128)(2,1)S(1)} %get-tuple-element.56), channel_id=1, source_target_pairs={{0,72},{1,65},{64,8},{65,1},{8,64},{9,73},{72,0},{73,9},{16,88},{1... | collective-permute-start | bytes 393224 | tf_op jit(solution)/shard_map/sum_queries/ppermute | solution.py:43
  41.3 7.4 %collective-permute-start.15 = (bf16[512,128]{1,0:T(8,128)(2,1)S(1)}, bf16[512,128]{1,0:T(8,128)(2,1)S(1)}, u32[]{:S(2)}, u32[]{:S(2)}) collective-permute-start(bf16[512,128]{1,0:T(8,128)(2,1)S(1)} %get-tuple-element.57), channel_id=1, source_target_pairs={{0,8},{1,9},{64,72},{65,73},{8,0},{9,1},{72,64},{73,65},{16,24},{1... | collective-permute-start | bytes 393224 | tf_op jit(solution)/shard_map/sum_queries/ppermute | solution.py:43
  44.6 5.0 %collective-permute-start.19 = (bf16[512,128]{1,0:T(8,128)(2,1)S(1)}, bf16[512,128]{1,0:T(8,128)(2,1)S(1)}, u32[]{:S(2)}, u32[]{:S(2)}) collective-permute-start(bf16[512,128]{1,0:T(8,128)(2,1)S(1)} %get-tuple-element.66), channel_id=1, source_target_pairs={{0,64},{1,73},{64,0},{65,9},{8,72},{9,65},{72,8},{73,1},{16,80},{1... | collective-permute-start | bytes 393224 | tf_op jit(solution)/shard_map/sum_queries/ppermute | solution.py:43
  45.7 5.0 %collective-permute-start.18 = (bf16[256,256]{1,0:T(8,128)(2,1)S(1)}, bf16[256,256]{1,0:T(8,128)(2,1)S(1)}, u32[]{:S(2)}, u32[]{:S(2)}) collective-permute-start(bf16[256,256]{1,0:T(8,128)(2,1)S(1)} %get-tuple-element.65), channel_id=1, source_target_pairs={{0,2},{1,7},{64,66},{65,71},{8,10},{9,15},{72,74},{73,79},{16,18},... | collective-permute-start | bytes 393224 | tf_op jit(solution)/shard_map/sum_keys/ppermute | solution.py:43
  50.8 4.9 %collective-permute-start.20 = (bf16[128,256]{1,0:T(8,128)(2,1)S(1)}, bf16[128,256]{1,0:T(8,128)(2,1)S(1)}, u32[]{:S(2)}, u32[]{:S(2)}) collective-permute-start(bf16[128,256]{1,0:T(8,128)(2,1)S(1)} %get-tuple-element.68), channel_id=1, source_target_pairs={{0,16},{1,49},{64,80},{65,113},{8,24},{9,57},{72,88},{73,121},{16,... | collective-permute-start | bytes 196616 | tf_op jit(solution)/shard_map/back_to_rows/ppermute | solution.py:43
  51.4 6.2 %collective-permute-start.21 = (bf16[128,256]{1,0:T(8,128)(2,1)S(1)}, bf16[128,256]{1,0:T(8,128)(2,1)S(1)}, u32[]{:S(2)}, u32[]{:S(2)}) collective-permute-start(bf16[128,256]{1,0:T(8,128)(2,1)S(1)} %get-tuple-element.69), channel_id=1, source_target_pairs={{0,48},{1,17},{64,112},{65,81},{8,56},{9,25},{72,120},{73,89},{16,... | collective-permute-start | bytes 196616 | tf_op jit(solution)/shard_map/back_to_rows/ppermute | solution.py:43
  53.3 5.8 %collective-permute-start.22 = (bf16[128,256]{1,0:T(8,128)(2,1)S(1)}, bf16[128,256]{1,0:T(8,128)(2,1)S(1)}, u32[]{:S(2)}, u32[]{:S(2)}) collective-permute-start(bf16[128,256]{1,0:T(8,128)(2,1)S(1)} %get-tuple-element.70), channel_id=1, source_target_pairs={{0,32},{1,33},{64,96},{65,97},{8,40},{9,41},{72,104},{73,105},{16,... | collective-permute-start | bytes 196616 | tf_op jit(solution)/shard_map/back_to_rows/ppermute | solution.py:43

commit v5 on v4

--- a/solution.py
+++ b/solution.py
@@ -17,7 +17,7 @@
 KR = 64
 AUX = 16
 TILE = 512
-HINT = 1.0
+HINT = 0.5
 LATE = 4 * 10**9
 BLK = QR + KR + AUX
 QS = 4 * QR
@@ -208,8 +208,8 @@
         out[...] = total.astype(out.dtype)
 
 
-def chip_sum_kernel(q23, q0, k0, k1, q1, *outs):
-    dq = q0[...] + q1[...].astype(F32) + q23[...]
+def chip_sum_kernel(q3, q0, k0, k1, q1, q2, *outs):
+    dq = q0[...] + q1[...].astype(F32) + q2[...].astype(F32) + q3[...].astype(F32)
     dkv = k0[...] + k1[...].astype(F32)
     for j, out in enumerate(outs):
         part = dq[j * QR : (j + 1) * QR]
@@ -326,7 +326,7 @@
         )
     with jax.named_scope("sum_queries"):
         got1 = swap_queries(dq1, 0)
-        got23 = call(add_kernel, [((QS, DH), F32)], (got2, got3), flops=LATE)[0]
+        got3 = call(copy_kernel, [((QS, DH), BF16)], (got3,), flops=LATE)[0]
     with jax.named_scope("sum_keys"):
         k_own, k_sent = call(
             split_kernel, [((KS, 2 * DH), F32), ((KS, 2 * DH), BF16)], (dkv_own, got_other, got_b)
@@ -336,7 +336,7 @@
         backs = call(
             chip_sum_kernel,
             [((2 * KR, 2 * DH), F32)] + [((2 * KR, 2 * DH), BF16)] * 3,
-            (got23, dq0, k_own, k_got, got1),
+            (got3, dq0, k_own, k_got, got1, got2),
         )
     with jax.named_scope("back_to_rows"):
         far = swap_heads(backs[2], 2)

time: 60.1 us -> 60.6 us (level)
  transfers between devices with their start and end apart: 23 -> 23, of which waited for: 11 -> 12; matrix products, arithmetic and copies ran while one was open for 0% -> 0% of each run, Pallas kernels for 18% -> 17%
where the time goes in v5:
time: 60.6 us; the launch traced here: 60.4 us
  starting transfers between devices  27.6 us (46%)
  Pallas kernels  16.1 us (27%)
  waiting for transfers between devices  14.9 us (25%)
  local copies, waits for them, and re-layouts  0.89 us (1%)
  between operations  0.8 us (1%)
    ppermute x23, starting transfers between devices, move(): return lax.ppermute(value, AXES, pairs)  27.6 us
    pallas_call x15, Pallas kernels, call(): pl.pallas_call(kernel, out_shape=[jax.ShapeDtypeStruct(shape, kind) for s...  16.1 us
    ppermute x23, waiting for transfers between devices, move(): return lax.ppermute(value, AXES, pairs)  14.9 us
  transfers between devices with their start and end apart: 23, of which 12 were waited for; matrix products, arithmetic and copies ran while one was open for 0% of the time, Pallas kernels for 17%

profile of v5, /device:TPU:0, one launch (start us, length us, event | category | flops | bytes accessed | tf_op | source)
XLA Modules:
  0.0 60.4 jit_solution(9480178313844250373)
XLA Ops:
  0.6 2.0 %pack.3 = (bf16[208,256]{1,0:T(8,128)(2,1)}, bf16[208,256]{1,0:T(8,128)(2,1)}, bf16[208,256]{1,0:T(8,128)(2,1)}) custom-call(bf16[128,512]{1,0:T(8,128)(2,1)} %refs_0_.3, bf16[64,512]{1,0:T(8,128)(2,1)} %refs_1_.3, bf16[64,512]{1,0:T(8,128)(2,1)} %refs_2_.3, bf16[128,512]{1,0:T(8,128)(2,1)} %refs_3_.3, bf16[128,512]{1,0:T(8,128)(2,1)} %refs_4_.3, ...), custom_call_target="tpu_custom_call" | custom-call | bytes 845824 | tf_op jit(solution)/shard_map/pack/pallas_call | solution.py:234
  2.6 3.4 %collective-permute-start = (bf16[208,256]{1,0:T(8,128)(2,1)}, bf16[208,256]{1,0:T(8,128)(2,1)S(1)}, u32[]{:S(2)}, u32[]{:S(2)}) collective-permute-start(bf16[208,256]{1,0:T(8,128)(2,1)} %get-tuple-element.37), channel_id=1, source_target_pairs={{0,32},{1,33},{64,96},{65,97},{8,40},{9,41},{72,104},{73,105},{16,... | collective-permute-start | bytes 319496 | tf_op jit(solution)/shard_map/heads_to_chips/ppermute | solution.py:43
  7.0 1.9 %pack.4.source = bf16[208,256]{1,0:T(8,128)(2,1)} custom-call(bf16[128,512]{1,0:T(8,128)(2,1)} %refs_0_.3, bf16[64,512]{1,0:T(8,128)(2,1)} %refs_1_.3, bf16[64,512]{1,0:T(8,128)(2,1)} %refs_2_.3, bf16[128,512]{1,0:T(8,128)(2,1)} %refs_3_.3, bf16[128,512]{1,0:T(8,128)(2,1)} %refs_4_.3, f32[4,128]{1,0:T(4,128)} %refs_5_.3), custom_call_target="tpu_custom_call" | custom-call | bytes 632832 | tf_op jit(solution)/shard_map/pack/pallas_call | solution.py:234
  9.8 2.0 %collective-permute-done.1.b1 = bf16[208,256]{1,0:T(8,128)(2,1)S(1)} collective-permute-done((bf16[208,256]{1,0:T(8,128)(2,1)}, bf16[208,256]{1,0:T(8,128)(2,1)S(1)}, u32[]{:S(2)}, u32[]{:S(2)}) %collective-permute-start.1) | collective-permute-done | bytes 106528 | tf_op jit(solution)/shard_map/heads_to_chips/ppermute | solution.py:43
  12.8 2.0 %collective-permute-start.7 = (bf16[528,256]{1,0:T(8,128)(2,1)S(1)}, bf16[528,256]{1,0:T(8,128)(2,1)S(1)}, u32[]{:S(2)}, u32[]{:S(2)}) collective-permute-start(bf16[528,256]{1,0:T(8,128)(2,1)S(1)} %get-tuple-element.41.refs_2_.refs_4_), channel_id=1, source_target_pairs={{0,64},{1,73},{64,0},{65,9},{8,72},{9,65},{72,8},{73,1},{16,80},{1... | collective-permute-start | bytes 811016 | tf_op jit(solution)/shard_map/gather_queries/ppermute | solution.py:43
  14.8 2.5 %collective-permute-start.4 = (bf16[528,256]{1,0:T(8,128)(2,1)S(1)}, bf16[528,256]{1,0:T(8,128)(2,1)S(1)}, u32[]{:S(2)}, u32[]{:S(2)}) collective-permute-start(bf16[528,256]{1,0:T(8,128)(2,1)S(1)} %get-tuple-element.41.refs_2_.refs_4_), channel_id=1, source_target_pairs={{0,72},{1,65},{64,8},{65,1},{8,64},{9,73},{72,0},{73,9},{16,88},{1... | collective-permute-start | bytes 811016 | tf_op jit(solution)/shard_map/gather_queries/ppermute | solution.py:43
  17.3 3.0 %collective-permute-start.6 = (bf16[256,256]{1,0:T(8,128)(2,1)S(1)}, bf16[256,256]{1,0:T(8,128)(2,1)S(1)}, u32[]{:S(2)}, u32[]{:S(2)}) collective-permute-start(bf16[256,256]{1,0:T(8,128)(2,1)S(1)} %get-tuple-element.40.refs_0_), channel_id=1, source_target_pairs={{0,4},{1,5},{64,68},{65,69},{8,12},{9,13},{72,76},{73,77},{16,20},... | collective-permute-start | bytes 393224 | tf_op jit(solution)/shard_map/gather_keys/ppermute | solution.py:43
  21.7 2.4 %collective-permute-start.8 = (bf16[528,256]{1,0:T(8,128)(2,1)S(1)}, bf16[528,256]{1,0:T(8,128)(2,1)S(1)}, u32[]{:S(2)}, u32[]{:S(2)}) collective-permute-start(bf16[528,256]{1,0:T(8,128)(2,1)S(1)} %collective-permute-done.7.refs_3_.refs_5_), channel_id=1, source_target_pairs={{0,72},{1,65},{64,8},{65,1},{8,64},{9,73},{72,0},{73,9},{16,88},{1... | collective-permute-start | bytes 811016 | tf_op jit(solution)/shard_map/gather_queries/ppermute | solution.py:43
  24.1 2.4 %collective-permute-done.5.refs_0_.refs_2_ = bf16[256,256]{1,0:T(8,128)(2,1)S(1)} collective-permute-done((bf16[256,256]{1,0:T(8,128)(2,1)S(1)}, bf16[256,256]{1,0:T(8,128)(2,1)S(1)}, u32[]{:S(2)}, u32[]{:S(2)}) %collective-permute-start.5) | collective-permute-done | bytes 131104 | tf_op jit(solution)/shard_map/gather_keys/ppermute | solution.py:43
  27.1 1.4 %attend_a_b.2 = (f32[512,256]{1,0:T(8,128)S(1)}, f32[128,1024]{1,0:T(8,128)S(1)}) custom-call(bf16[256,256]{1,0:T(8,128)(2,1)S(1)} %collective-permute-done.5.refs_0_.refs_2_, bf16[256,256]{1,0:T(8,128)(2,1)S(1)} %collective-permute-done.6.refs_1_.refs_3_, bf16[528,256]{1,0:T(8,128)(2,1)S(1)} %get-tuple-element.41.refs_2_.refs_4_, ...), custom_call_target="tpu_custom_call" | custom-call | flops 335544320 | bytes 1851392 | tf_op jit(solution)/shard_map/attend_a_b/pallas_call | solution.py:234
  28.6 2.7 %attend_a_b.3 = (f32[512,256]{1,0:T(8,128)S(1)}, f32[512,256]{1,0:T(8,128)S(1)}, f32[128,1024]{1,0:T(8,128)S(1)}) custom-call(bf16[256,256]{1,0:T(8,128)(2,1)S(1)} %collective-permute-done.9.refs_0_, bf16[256,256]{1,0:T(8,128)(2,1)S(1)} %collective-permute-done.10.refs_1_, bf16[256,256]{1,0:T(8,128)(2,1)S(1)} %collective-permute-done.11.refs_2_.refs_0_, ...), custom_call_target="tpu_custom_call" | custom-call | flops 671088640 | bytes 3162112 | tf_op jit(solution)/shard_map/attend_a_b/pallas_call | solution.py:234
  31.3 2.7 %attend_b_b.1 = (bf16[512,256]{1,0:T(8,128)(2,1)S(1)}, f32[512,256]{1,0:T(8,128)S(1)}, f32[128,1024]{1,0:T(8,128)S(1)}) custom-call(bf16[256,256]{1,0:T(8,128)(2,1)S(1)} %collective-permute-done.9.refs_0_, bf16[256,256]{1,0:T(8,128)(2,1)S(1)} %collective-permute-done.10.refs_1_, bf16[256,256]{1,0:T(8,128)(2,1)S(1)} %collective-permute-done.5.refs_0_.refs_2_, ...), custom_call_target="tpu_custom_call" | custom-call | flops 671088640 | bytes 3424256 | tf_op jit(solution)/shard_map/attend_b_b/pallas_call | solution.py:234
  34.5 1.5 %attend_b_a_other.1 = (bf16[512,256]{1,0:T(8,128)(2,1)S(1)}, f32[128,1024]{1,0:T(8,128)S(1)}) custom-call(bf16[256,256]{1,0:T(8,128)(2,1)S(1)} %collective-permute-done.11.refs_2_.refs_0_, bf16[256,256]{1,0:T(8,128)(2,1)S(1)} %collective-permute-done.12.refs_3_.refs_1_, bf16[528,256]{1,0:T(8,128)(2,1)S(1)} %collective-permute-done.4.refs_4_.refs_2_, ...), custom_call_target="tpu_custom_call" | custom-call | flops 335544320 | bytes 2637824 | tf_op jit(solution)/shard_map/attend_b_a_other/pallas_call | solution.py:234
  36.2 2.2 %collective-permute-start.16 = (bf16[512,256]{1,0:T(8,128)(2,1)S(1)}, bf16[512,256]{1,0:T(8,128)(2,1)S(1)}, u32[]{:S(2)}, u32[]{:S(2)}) collective-permute-start(bf16[512,256]{1,0:T(8,128)(2,1)S(1)} %sum_keys_over_core.1), channel_id=1, source_target_pairs={{0,6},{1,3},{64,70},{65,67},{8,14},{9,11},{72,78},{73,75},{16,22},... | collective-permute-start | bytes 786440 | tf_op jit(solution)/shard_map/sum_keys/ppermute | solution.py:43
  38.4 1.5 %attend_b_a.1 = (f32[512,256]{1,0:T(8,128)S(1)}, bf16[512,128]{1,0:T(8,128)(2,1)S(1)}, bf16[512,128]{1,0:T(8,128)(2,1)S(1)}) custom-call(bf16[256,256]{1,0:T(8,128)(2,1)S(1)} %get-tuple-element.40.refs_0_, bf16[256,256]{1,0:T(8,128)(2,1)S(1)} %collective-permute-done.3.refs_1_, bf16[528,256]{1,0:T(8,128)(2,1)S(1)} %collective-permute-done.4.refs_4_.refs_2_, ...), custom_call_target="tpu_custom_call" | custom-call | flops 335544320 | bytes 2113536 | tf_op jit(solution)/shard_map/attend_b_a/pallas_call | solution.py:234
  39.9 1.1 %collective-permute-start.14 = (bf16[512,128]{1,0:T(8,128)(2,1)S(1)}, bf16[512,128]{1,0:T(8,128)(2,1)S(1)}, u32[]{:S(2)}, u32[]{:S(2)}) collective-permute-start(bf16[512,128]{1,0:T(8,128)(2,1)S(1)} %get-tuple-element.56), channel_id=1, source_target_pairs={{0,8},{1,9},{64,72},{65,73},{8,0},{9,1},{72,64},{73,65},{16,24},{1... | collective-permute-start | bytes 393224 | tf_op jit(solution)/shard_map/sum_queries/ppermute | solution.py:43
  41.0 1.5 %attend_a_a.1 = (f32[512,256]{1,0:T(8,128)S(1)}, f32[512,128]{1,0:T(8,128)S(1)}, bf16[512,128]{1,0:T(8,128)(2,1)S(1)}) custom-call(bf16[256,256]{1,0:T(8,128)(2,1)S(1)} %get-tuple-element.40.refs_0_, bf16[256,256]{1,0:T(8,128)(2,1)S(1)} %collective-permute-done.3.refs_1_, bf16[528,256]{1,0:T(8,128)(2,1)S(1)} %get-tuple-element.41.refs_2_.refs_4_, ...), custom_call_target="tpu_custom_call" | custom-call | flops 335544320 | bytes 2768896 | tf_op jit(solution)/shard_map/attend_a_a/pallas_call | solution.py:234
  42.5 1.2 %collective-permute-start.18 = (bf16[512,128]{1,0:T(8,128)(2,1)S(1)}, bf16[512,128]{1,0:T(8,128)(2,1)S(1)}, u32[]{:S(2)}, u32[]{:S(2)}) collective-permute-start(bf16[512,128]{1,0:T(8,128)(2,1)S(1)} %get-tuple-element.65), channel_id=1, source_target_pairs={{0,64},{1,73},{64,0},{65,9},{8,72},{9,65},{72,8},{73,1},{16,80},{1... | collective-permute-start | bytes 393224 | tf_op jit(solution)/shard_map/sum_queries/ppermute | solution.py:43
  43.7 1.9 %collective-permute-start.19 = (bf16[512,128]{1,0:T(8,128)(2,1)S(1)}, bf16[512,128]{1,0:T(8,128)(2,1)S(1)}, u32[]{:S(2)}, u32[]{:S(2)}) collective-permute-start(bf16[512,128]{1,0:T(8,128)(2,1)S(1)} %get-tuple-element.66), channel_id=1, source_target_pairs={{0,72},{1,65},{64,8},{65,1},{8,64},{9,73},{72,0},{73,9},{16,88},{1... | collective-permute-start | bytes 393224 | tf_op jit(solution)/shard_map/sum_queries/ppermute | solution.py:43
  46.9 1.9 %collective-permute-done.18.q1 = bf16[512,128]{1,0:T(8,128)(2,1)S(1)} collective-permute-done((bf16[512,128]{1,0:T(8,128)(2,1)S(1)}, bf16[512,128]{1,0:T(8,128)(2,1)S(1)}, u32[]{:S(2)}, u32[]{:S(2)}) %collective-permute-start.18) | collective-permute-done | bytes 131104 | tf_op jit(solution)/shard_map/sum_queries/ppermute | solution.py:43
  51.4 2.3 %collective-permute-start.21 = (bf16[128,256]{1,0:T(8,128)(2,1)S(1)}, bf16[128,256]{1,0:T(8,128)(2,1)S(1)}, u32[]{:S(2)}, u32[]{:S(2)}) collective-permute-start(bf16[128,256]{1,0:T(8,128)(2,1)S(1)} %get-tuple-element.69), channel_id=1, source_target_pairs={{0,48},{1,17},{64,112},{65,81},{8,56},{9,25},{72,120},{73,89},{16,... | collective-permute-start | bytes 196616 | tf_op jit(solution)/shard_map/back_to_rows/ppermute | solution.py:43
  53.8 1.4 %collective-permute-start.22 = (bf16[128,256]{1,0:T(8,128)(2,1)S(1)}, bf16[128,256]{1,0:T(8,128)(2,1)S(1)}, u32[]{:S(2)}, u32[]{:S(2)}) collective-permute-start(bf16[128,256]{1,0:T(8,128)(2,1)S(1)} %get-tuple-element.70), channel_id=1, source_target_pairs={{0,32},{1,33},{64,96},{65,97},{8,40},{9,41},{72,104},{73,105},{16,... | collective-permute-start | bytes 196616 | tf_op jit(solution)/shard_map/back_to_rows/ppermute | solution.py:43
  55.8 1.7 %collective-permute-done.21.b3 = bf16[128,256]{1,0:T(8,128)(2,1)S(1)} collective-permute-done((bf16[128,256]{1,0:T(8,128)(2,1)S(1)}, bf16[128,256]{1,0:T(8,128)(2,1)S(1)}, u32[]{:S(2)}, u32[]{:S(2)}) %collective-permute-start.21) | collective-permute-done | bytes 65568 | tf_op jit(solution)/shard_map/back_to_rows/ppermute | solution.py:43
  57.5 2.0 %collective-permute-done.22.b2 = bf16[128,256]{1,0:T(8,128)(2,1)S(1)} collective-permute-done((bf16[128,256]{1,0:T(8,128)(2,1)S(1)}, bf16[128,256]{1,0:T(8,128)(2,1)S(1)}, u32[]{:S(2)}, u32[]{:S(2)}) %collective-permute-start.22) | collective-permute-done | bytes 65568 | tf_op jit(solution)/shard_map/back_to_rows/ppermute | solution.py:43
  (39 shorter events, 11.0 us)
Async XLA Ops:
  2.6 7.2 %collective-permute-start = (bf16[208,256]{1,0:T(8,128)(2,1)}, bf16[208,256]{1,0:T(8,128)(2,1)S(1)}, u32[]{:S(2)}, u32[]{:S(2)}) collective-permute-start(bf16[208,256]{1,0:T(8,128)(2,1)} %get-tuple-element.37), channel_id=1, source_target_pairs={{0,32},{1,33},{64,96},{65,97},{8,40},{9,41},{72,104},{73,105},{16,... | collective-permute-start | bytes 319496 | tf_op jit(solution)/shard_map/heads_to_chips/ppermute | solution.py:43
  5.9 5.9 %collective-permute-start.1 = (bf16[208,256]{1,0:T(8,128)(2,1)}, bf16[208,256]{1,0:T(8,128)(2,1)S(1)}, u32[]{:S(2)}, u32[]{:S(2)}) collective-permute-start(bf16[208,256]{1,0:T(8,128)(2,1)} %get-tuple-element.38), channel_id=1, source_target_pairs={{0,16},{1,49},{64,80},{65,113},{8,24},{9,57},{72,88},{73,121},{16,... | collective-permute-start | bytes 319496 | tf_op jit(solution)/shard_map/heads_to_chips/ppermute | solution.py:43
  6.6 6.1 %collective-permute-start.2 = (bf16[208,256]{1,0:T(8,128)(2,1)}, bf16[208,256]{1,0:T(8,128)(2,1)S(1)}, u32[]{:S(2)}, u32[]{:S(2)}) collective-permute-start(bf16[208,256]{1,0:T(8,128)(2,1)} %get-tuple-element.39), channel_id=1, source_target_pairs={{0,48},{1,17},{64,112},{65,81},{8,56},{9,25},{72,120},{73,89},{16,... | collective-permute-start | bytes 319496 | tf_op jit(solution)/shard_map/heads_to_chips/ppermute | solution.py:43
  8.9 0.9 %copy-start = (bf16[208,256]{1,0:T(8,128)(2,1)S(1)}, bf16[208,256]{1,0:T(8,128)(2,1)}, u32[]{:S(2)}) copy-start(bf16[208,256]{1,0:T(8,128)(2,1)} %pack.4.source) | copy-start | bytes 319492
  12.8 8.9 %collective-permute-start.7 = (bf16[528,256]{1,0:T(8,128)(2,1)S(1)}, bf16[528,256]{1,0:T(8,128)(2,1)S(1)}, u32[]{:S(2)}, u32[]{:S(2)}) collective-permute-start(bf16[528,256]{1,0:T(8,128)(2,1)S(1)} %get-tuple-element.41.refs_2_.refs_4_), channel_id=1, source_target_pairs={{0,64},{1,73},{64,0},{65,9},{8,72},{9,65},{72,8},{73,1},{16,80},{1... | collective-permute-start | bytes 811016 | tf_op jit(solution)/shard_map/gather_queries/ppermute | solution.py:43
  14.8 12.2 %collective-permute-start.4 = (bf16[528,256]{1,0:T(8,128)(2,1)S(1)}, bf16[528,256]{1,0:T(8,128)(2,1)S(1)}, u32[]{:S(2)}, u32[]{:S(2)}) collective-permute-start(bf16[528,256]{1,0:T(8,128)(2,1)S(1)} %get-tuple-element.41.refs_2_.refs_4_), channel_id=1, source_target_pairs={{0,72},{1,65},{64,8},{65,1},{8,64},{9,73},{72,0},{73,9},{16,88},{1... | collective-permute-start | bytes 811016 | tf_op jit(solution)/shard_map/gather_queries/ppermute | solution.py:43
  17.3 6.8 %collective-permute-start.6 = (bf16[256,256]{1,0:T(8,128)(2,1)S(1)}, bf16[256,256]{1,0:T(8,128)(2,1)S(1)}, u32[]{:S(2)}, u32[]{:S(2)}) collective-permute-start(bf16[256,256]{1,0:T(8,128)(2,1)S(1)} %get-tuple-element.40.refs_0_), channel_id=1, source_target_pairs={{0,4},{1,5},{64,68},{65,69},{8,12},{9,13},{72,76},{73,77},{16,20},... | collective-permute-start | bytes 393224 | tf_op jit(solution)/shard_map/gather_keys/ppermute | solution.py:43
  20.3 6.2 %collective-permute-start.5 = (bf16[256,256]{1,0:T(8,128)(2,1)S(1)}, bf16[256,256]{1,0:T(8,128)(2,1)S(1)}, u32[]{:S(2)}, u32[]{:S(2)}) collective-permute-start(bf16[256,256]{1,0:T(8,128)(2,1)S(1)} %get-tuple-element.40.refs_0_), channel_id=1, source_target_pairs={{0,6},{1,3},{64,70},{65,67},{8,14},{9,11},{72,78},{73,75},{16,22},... | collective-permute-start | bytes 393224 | tf_op jit(solution)/shard_map/gather_keys/ppermute | solution.py:43
  21.5 5.0 %collective-permute-start.3 = (bf16[256,256]{1,0:T(8,128)(2,1)S(1)}, bf16[256,256]{1,0:T(8,128)(2,1)S(1)}, u32[]{:S(2)}, u32[]{:S(2)}) collective-permute-start(bf16[256,256]{1,0:T(8,128)(2,1)S(1)} %get-tuple-element.40.refs_0_), channel_id=1, source_target_pairs={{0,2},{1,7},{64,66},{65,71},{8,10},{9,15},{72,74},{73,79},{16,18},... | collective-permute-start | bytes 393224 | tf_op jit(solution)/shard_map/gather_keys/ppermute | solution.py:43
  21.7 9.6 %collective-permute-start.8 = (bf16[528,256]{1,0:T(8,128)(2,1)S(1)}, bf16[528,256]{1,0:T(8,128)(2,1)S(1)}, u32[]{:S(2)}, u32[]{:S(2)}) collective-permute-start(bf16[528,256]{1,0:T(8,128)(2,1)S(1)} %collective-permute-done.7.refs_3_.refs_5_), channel_id=1, source_target_pairs={{0,72},{1,65},{64,8},{65,1},{8,64},{9,73},{72,0},{73,9},{16,88},{1... | collective-permute-start | bytes 811016 | tf_op jit(solution)/shard_map/gather_queries/ppermute | solution.py:43
  24.1 4.4 %collective-permute-start.11 = (bf16[256,256]{1,0:T(8,128)(2,1)S(1)}, bf16[256,256]{1,0:T(8,128)(2,1)S(1)}, u32[]{:S(2)}, u32[]{:S(2)}) collective-permute-start(bf16[256,256]{1,0:T(8,128)(2,1)S(1)} %get-tuple-element.40.refs_0_), channel_id=1, source_target_pairs={{0,1},{1,0},{64,65},{65,64},{8,9},{9,8},{72,73},{73,72},{16,17},{1... | collective-permute-start | bytes 393224 | tf_op jit(solution)/shard_map/gather_keys/ppermute | solution.py:43
  26.5 2.0 %collective-permute-start.10 = (bf16[256,256]{1,0:T(8,128)(2,1)S(1)}, bf16[256,256]{1,0:T(8,128)(2,1)S(1)}, u32[]{:S(2)}, u32[]{:S(2)}) collective-permute-start(bf16[256,256]{1,0:T(8,128)(2,1)S(1)} %collective-permute-done.6.refs_1_.refs_3_), channel_id=1, source_target_pairs={{0,1},{1,0},{64,65},{65,64},{8,9},{9,8},{72,73},{73,72},{16,17},{1... | collective-permute-start | bytes 393224 | tf_op jit(solution)/shard_map/gather_keys/ppermute | solution.py:43
  26.5 2.0 %collective-permute-start.9 = (bf16[256,256]{1,0:T(8,128)(2,1)S(1)}, bf16[256,256]{1,0:T(8,128)(2,1)S(1)}, u32[]{:S(2)}, u32[]{:S(2)}) collective-permute-start(bf16[256,256]{1,0:T(8,128)(2,1)S(1)} %collective-permute-done.5.refs_0_.refs_2_), channel_id=1, source_target_pairs={{0,1},{1,0},{64,65},{65,64},{8,9},{9,8},{72,73},{73,72},{16,17},{1... | collective-permute-start | bytes 393224 | tf_op jit(solution)/shard_map/gather_keys/ppermute | solution.py:43
  27.0 1.5 %collective-permute-start.12 = (bf16[256,256]{1,0:T(8,128)(2,1)S(1)}, bf16[256,256]{1,0:T(8,128)(2,1)S(1)}, u32[]{:S(2)}, u32[]{:S(2)}) collective-permute-start(bf16[256,256]{1,0:T(8,128)(2,1)S(1)} %collective-permute-done.3.refs_1_), channel_id=1, source_target_pairs={{0,1},{1,0},{64,65},{65,64},{8,9},{9,8},{72,73},{73,72},{16,17},{1... | collective-permute-start | bytes 393224 | tf_op jit(solution)/shard_map/gather_keys/ppermute | solution.py:43
  34.0 2.2 %collective-permute-start.13 = (bf16[512,256]{1,0:T(8,128)(2,1)S(1)}, bf16[512,256]{1,0:T(8,128)(2,1)S(1)}, u32[]{:S(2)}, u32[]{:S(2)}) collective-permute-start(bf16[512,256]{1,0:T(8,128)(2,1)S(1)} %get-tuple-element.54), channel_id=1, source_target_pairs={{0,1},{1,0},{64,65},{65,64},{8,9},{9,8},{72,73},{73,72},{16,17},{1... | collective-permute-start | bytes 786440 | tf_op jit(solution)/shard_map/sum_keys_over_core/ppermute | solution.py:43
  36.0 9.7 %collective-permute-start.15 = (bf16[512,256]{1,0:T(8,128)(2,1)S(1)}, bf16[512,256]{1,0:T(8,128)(2,1)S(1)}, u32[]{:S(2)}, u32[]{:S(2)}) collective-permute-start(bf16[512,256]{1,0:T(8,128)(2,1)S(1)} %get-tuple-element.61), channel_id=1, source_target_pairs={{0,1},{1,0},{64,65},{65,64},{8,9},{9,8},{72,73},{73,72},{16,17},{1... | collective-permute-start | bytes 786440 | tf_op jit(solution)/shard_map/sum_keys_over_core/ppermute | solution.py:43
  36.2 9.4 %collective-permute-start.16 = (bf16[512,256]{1,0:T(8,128)(2,1)S(1)}, bf16[512,256]{1,0:T(8,128)(2,1)S(1)}, u32[]{:S(2)}, u32[]{:S(2)}) collective-permute-start(bf16[512,256]{1,0:T(8,128)(2,1)S(1)} %sum_keys_over_core.1), channel_id=1, source_target_pairs={{0,6},{1,3},{64,70},{65,67},{8,14},{9,11},{72,78},{73,75},{16,22},... | collective-permute-start | bytes 786440 | tf_op jit(solution)/shard_map/sum_keys/ppermute | solution.py:43
  39.9 7.0 %collective-permute-start.14 = (bf16[512,128]{1,0:T(8,128)(2,1)S(1)}, bf16[512,128]{1,0:T(8,128)(2,1)S(1)}, u32[]{:S(2)}, u32[]{:S(2)}) collective-permute-start(bf16[512,128]{1,0:T(8,128)(2,1)S(1)} %get-tuple-element.56), channel_id=1, source_target_pairs={{0,8},{1,9},{64,72},{65,73},{8,0},{9,1},{72,64},{73,65},{16,24},{1... | collective-permute-start | bytes 393224 | tf_op jit(solution)/shard_map/sum_queries/ppermute | solution.py:43
  42.5 6.3 %collective-permute-start.18 = (bf16[512,128]{1,0:T(8,128)(2,1)S(1)}, bf16[512,128]{1,0:T(8,128)(2,1)S(1)}, u32[]{:S(2)}, u32[]{:S(2)}) collective-permute-start(bf16[512,128]{1,0:T(8,128)(2,1)S(1)} %get-tuple-element.65), channel_id=1, source_target_pairs={{0,64},{1,73},{64,0},{65,9},{8,72},{9,65},{72,8},{73,1},{16,80},{1... | collective-permute-start | bytes 393224 | tf_op jit(solution)/shard_map/sum_queries/ppermute | solution.py:43
  43.7 6.2 %collective-permute-start.19 = (bf16[512,128]{1,0:T(8,128)(2,1)S(1)}, bf16[512,128]{1,0:T(8,128)(2,1)S(1)}, u32[]{:S(2)}, u32[]{:S(2)}) collective-permute-start(bf16[512,128]{1,0:T(8,128)(2,1)S(1)} %get-tuple-element.66), channel_id=1, source_target_pairs={{0,72},{1,65},{64,8},{65,1},{8,64},{9,73},{72,0},{73,9},{16,88},{1... | collective-permute-start | bytes 393224 | tf_op jit(solution)/shard_map/sum_queries/ppermute | solution.py:43
  45.7 5.0 %collective-permute-start.17 = (bf16[256,256]{1,0:T(8,128)(2,1)S(1)}, bf16[256,256]{1,0:T(8,128)(2,1)S(1)}, u32[]{:S(2)}, u32[]{:S(2)}) collective-permute-start(bf16[256,256]{1,0:T(8,128)(2,1)S(1)} %get-tuple-element.64), channel_id=1, source_target_pairs={{0,2},{1,7},{64,66},{65,71},{8,10},{9,15},{72,74},{73,79},{16,18},... | collective-permute-start | bytes 393224 | tf_op jit(solution)/shard_map/sum_keys/ppermute | solution.py:43
  50.8 4.9 %collective-permute-start.20 = (bf16[128,256]{1,0:T(8,128)(2,1)S(1)}, bf16[128,256]{1,0:T(8,128)(2,1)S(1)}, u32[]{:S(2)}, u32[]{:S(2)}) collective-permute-start(bf16[128,256]{1,0:T(8,128)(2,1)S(1)} %get-tuple-element.68), channel_id=1, source_target_pairs={{0,16},{1,49},{64,80},{65,113},{8,24},{9,57},{72,88},{73,121},{16,... | collective-permute-start | bytes 196616 | tf_op jit(solution)/shard_map/back_to_rows/ppermute | solution.py:43
  51.4 6.1 %collective-permute-start.21 = (bf16[128,256]{1,0:T(8,128)(2,1)S(1)}, bf16[128,256]{1,0:T(8,128)(2,1)S(1)}, u32[]{:S(2)}, u32[]{:S(2)}) collective-permute-start(bf16[128,256]{1,0:T(8,128)(2,1)S(1)} %get-tuple-element.69), channel_id=1, source_target_pairs={{0,48},{1,17},{64,112},{65,81},{8,56},{9,25},{72,120},{73,89},{16,... | collective-permute-start | bytes 196616 | tf_op jit(solution)/shard_map/back_to_rows/ppermute | solution.py:43
  53.8 5.8 %collective-permute-start.22 = (bf16[128,256]{1,0:T(8,128)(2,1)S(1)}, bf16[128,256]{1,0:T(8,128)(2,1)S(1)}, u32[]{:S(2)}, u32[]{:S(2)}) collective-permute-start(bf16[128,256]{1,0:T(8,128)(2,1)S(1)} %get-tuple-element.70), channel_id=1, source_target_pairs={{0,32},{1,33},{64,96},{65,97},{8,40},{9,41},{72,104},{73,105},{16,... | collective-permute-start | bytes 196616 | tf_op jit(solution)/shard_map/back_to_rows/ppermute | solution.py:43

commit v6 on v4

--- a/solution.py
+++ b/solution.py
@@ -17,7 +17,7 @@
 KR = 64
 AUX = 16
 TILE = 512
-HINT = 1.0
+HINT = 0.5
 LATE = 4 * 10**9
 BLK = QR + KR + AUX
 QS = 4 * QR

time: 60.1 us -> 60.1 us (level)
  no operation moved by 1% of the time
where the time goes in v6:
time: 60.1 us; the launch traced here: 60 us
  starting transfers between devices  27.5 us (46%)
  Pallas kernels  16.1 us (27%)
  waiting for transfers between devices  14.6 us (24%)
  local copies, waits for them, and re-layouts  0.89 us (1%)
  between operations  0.8 us (1%)
    ppermute x23, starting transfers between devices, move(): return lax.ppermute(value, AXES, pairs)  27.5 us
    pallas_call x15, Pallas kernels, call(): pl.pallas_call(kernel, out_shape=[jax.ShapeDtypeStruct(shape, kind) for s...  16.1 us
    ppermute x23, waiting for transfers between devices, move(): return lax.ppermute(value, AXES, pairs)  14.6 us
  transfers between devices with their start and end apart: 23, of which 11 were waited for; matrix products, arithmetic and copies ran while one was open for 0% of the time, Pallas kernels for 18%

profile of v6, /device:TPU:0, one launch (start us, length us, event | category | flops | bytes accessed | tf_op | source)
XLA Modules:
  0.0 60.0 jit_solution(7220587584622505799)
XLA Ops:
  0.6 2.0 %pack.3 = (bf16[208,256]{1,0:T(8,128)(2,1)}, bf16[208,256]{1,0:T(8,128)(2,1)}, bf16[208,256]{1,0:T(8,128)(2,1)}) custom-call(bf16[128,512]{1,0:T(8,128)(2,1)} %refs_0_.3, bf16[64,512]{1,0:T(8,128)(2,1)} %refs_1_.3, bf16[64,512]{1,0:T(8,128)(2,1)} %refs_2_.3, bf16[128,512]{1,0:T(8,128)(2,1)} %refs_3_.3, bf16[128,512]{1,0:T(8,128)(2,1)} %refs_4_.3, ...), custom_call_target="tpu_custom_call" | custom-call | bytes 845824 | tf_op jit(solution)/shard_map/pack/pallas_call | solution.py:234
  2.6 3.4 %collective-permute-start = (bf16[208,256]{1,0:T(8,128)(2,1)}, bf16[208,256]{1,0:T(8,128)(2,1)S(1)}, u32[]{:S(2)}, u32[]{:S(2)}) collective-permute-start(bf16[208,256]{1,0:T(8,128)(2,1)} %get-tuple-element.37), channel_id=1, source_target_pairs={{0,32},{1,33},{64,96},{65,97},{8,40},{9,41},{72,104},{73,105},{16,... | collective-permute-start | bytes 319496 | tf_op jit(solution)/shard_map/heads_to_chips/ppermute | solution.py:43
  7.0 1.9 %pack.4.source = bf16[208,256]{1,0:T(8,128)(2,1)} custom-call(bf16[128,512]{1,0:T(8,128)(2,1)} %refs_0_.3, bf16[64,512]{1,0:T(8,128)(2,1)} %refs_1_.3, bf16[64,512]{1,0:T(8,128)(2,1)} %refs_2_.3, bf16[128,512]{1,0:T(8,128)(2,1)} %refs_3_.3, bf16[128,512]{1,0:T(8,128)(2,1)} %refs_4_.3, f32[4,128]{1,0:T(4,128)} %refs_5_.3), custom_call_target="tpu_custom_call" | custom-call | bytes 632832 | tf_op jit(solution)/shard_map/pack/pallas_call | solution.py:234
  9.8 2.0 %collective-permute-done.1.b1 = bf16[208,256]{1,0:T(8,128)(2,1)S(1)} collective-permute-done((bf16[208,256]{1,0:T(8,128)(2,1)}, bf16[208,256]{1,0:T(8,128)(2,1)S(1)}, u32[]{:S(2)}, u32[]{:S(2)}) %collective-permute-start.1) | collective-permute-done | bytes 106528 | tf_op jit(solution)/shard_map/heads_to_chips/ppermute | solution.py:43
  12.8 2.0 %collective-permute-start.7 = (bf16[528,256]{1,0:T(8,128)(2,1)S(1)}, bf16[528,256]{1,0:T(8,128)(2,1)S(1)}, u32[]{:S(2)}, u32[]{:S(2)}) collective-permute-start(bf16[528,256]{1,0:T(8,128)(2,1)S(1)} %get-tuple-element.41.refs_2_.refs_4_), channel_id=1, source_target_pairs={{0,64},{1,73},{64,0},{65,9},{8,72},{9,65},{72,8},{73,1},{16,80},{1... | collective-permute-start | bytes 811016 | tf_op jit(solution)/shard_map/gather_queries/ppermute | solution.py:43
  14.8 2.5 %collective-permute-start.4 = (bf16[528,256]{1,0:T(8,128)(2,1)S(1)}, bf16[528,256]{1,0:T(8,128)(2,1)S(1)}, u32[]{:S(2)}, u32[]{:S(2)}) collective-permute-start(bf16[528,256]{1,0:T(8,128)(2,1)S(1)} %get-tuple-element.41.refs_2_.refs_4_), channel_id=1, source_target_pairs={{0,72},{1,65},{64,8},{65,1},{8,64},{9,73},{72,0},{73,9},{16,88},{1... | collective-permute-start | bytes 811016 | tf_op jit(solution)/shard_map/gather_queries/ppermute | solution.py:43
  17.3 3.0 %collective-permute-start.6 = (bf16[256,256]{1,0:T(8,128)(2,1)S(1)}, bf16[256,256]{1,0:T(8,128)(2,1)S(1)}, u32[]{:S(2)}, u32[]{:S(2)}) collective-permute-start(bf16[256,256]{1,0:T(8,128)(2,1)S(1)} %get-tuple-element.40.refs_0_), channel_id=1, source_target_pairs={{0,4},{1,5},{64,68},{65,69},{8,12},{9,13},{72,76},{73,77},{16,20},... | collective-permute-start | bytes 393224 | tf_op jit(solution)/shard_map/gather_keys/ppermute | solution.py:43
  20.3 1.1 %collective-permute-start.5 = (bf16[256,256]{1,0:T(8,128)(2,1)S(1)}, bf16[256,256]{1,0:T(8,128)(2,1)S(1)}, u32[]{:S(2)}, u32[]{:S(2)}) collective-permute-start(bf16[256,256]{1,0:T(8,128)(2,1)S(1)} %get-tuple-element.40.refs_0_), channel_id=1, source_target_pairs={{0,6},{1,3},{64,70},{65,67},{8,14},{9,11},{72,78},{73,75},{16,22},... | collective-permute-start | bytes 393224 | tf_op jit(solution)/shard_map/gather_keys/ppermute | solution.py:43
  21.7 2.4 %collective-permute-start.8 = (bf16[528,256]{1,0:T(8,128)(2,1)S(1)}, bf16[528,256]{1,0:T(8,128)(2,1)S(1)}, u32[]{:S(2)}, u32[]{:S(2)}) collective-permute-start(bf16[528,256]{1,0:T(8,128)(2,1)S(1)} %collective-permute-done.7.refs_3_.refs_5_), channel_id=1, source_target_pairs={{0,72},{1,65},{64,8},{65,1},{8,64},{9,73},{72,0},{73,9},{16,88},{1... | collective-permute-start | bytes 811016 | tf_op jit(solution)/shard_map/gather_queries/ppermute | solution.py:43
  24.1 2.4 %collective-permute-done.5.refs_0_.refs_2_ = bf16[256,256]{1,0:T(8,128)(2,1)S(1)} collective-permute-done((bf16[256,256]{1,0:T(8,128)(2,1)S(1)}, bf16[256,256]{1,0:T(8,128)(2,1)S(1)}, u32[]{:S(2)}, u32[]{:S(2)}) %collective-permute-start.5) | collective-permute-done | bytes 131104 | tf_op jit(solution)/shard_map/gather_keys/ppermute | solution.py:43
  27.1 1.4 %attend_a_b.2 = (f32[512,256]{1,0:T(8,128)S(1)}, f32[128,1024]{1,0:T(8,128)S(1)}) custom-call(bf16[256,256]{1,0:T(8,128)(2,1)S(1)} %collective-permute-done.5.refs_0_.refs_2_, bf16[256,256]{1,0:T(8,128)(2,1)S(1)} %collective-permute-done.6.refs_1_.refs_3_, bf16[528,256]{1,0:T(8,128)(2,1)S(1)} %get-tuple-element.41.refs_2_.refs_4_, ...), custom_call_target="tpu_custom_call" | custom-call | flops 335544320 | bytes 1851392 | tf_op jit(solution)/shard_map/attend_a_b/pallas_call | solution.py:234
  28.6 2.7 %attend_a_b.3 = (f32[512,256]{1,0:T(8,128)S(1)}, f32[512,256]{1,0:T(8,128)S(1)}, f32[128,1024]{1,0:T(8,128)S(1)}) custom-call(bf16[256,256]{1,0:T(8,128)(2,1)S(1)} %collective-permute-done.9.refs_0_, bf16[256,256]{1,0:T(8,128)(2,1)S(1)} %collective-permute-done.10.refs_1_, bf16[256,256]{1,0:T(8,128)(2,1)S(1)} %collective-permute-done.11.refs_2_.refs_0_, ...), custom_call_target="tpu_custom_call" | custom-call | flops 671088640 | bytes 3162112 | tf_op jit(solution)/shard_map/attend_a_b/pallas_call | solution.py:234
  31.3 2.7 %attend_b_b.1 = (bf16[512,256]{1,0:T(8,128)(2,1)S(1)}, f32[512,256]{1,0:T(8,128)S(1)}, f32[128,1024]{1,0:T(8,128)S(1)}) custom-call(bf16[256,256]{1,0:T(8,128)(2,1)S(1)} %collective-permute-done.9.refs_0_, bf16[256,256]{1,0:T(8,128)(2,1)S(1)} %collective-permute-done.10.refs_1_, bf16[256,256]{1,0:T(8,128)(2,1)S(1)} %collective-permute-done.5.refs_0_.refs_2_, ...), custom_call_target="tpu_custom_call" | custom-call | flops 671088640 | bytes 3424256 | tf_op jit(solution)/shard_map/attend_b_b/pallas_call | solution.py:234
  34.5 1.5 %attend_b_a_other.1 = (bf16[512,256]{1,0:T(8,128)(2,1)S(1)}, f32[128,1024]{1,0:T(8,128)S(1)}) custom-call(bf16[256,256]{1,0:T(8,128)(2,1)S(1)} %collective-permute-done.11.refs_2_.refs_0_, bf16[256,256]{1,0:T(8,128)(2,1)S(1)} %collective-permute-done.12.refs_3_.refs_1_, bf16[528,256]{1,0:T(8,128)(2,1)S(1)} %collective-permute-done.4.refs_4_.refs_2_, ...), custom_call_target="tpu_custom_call" | custom-call | flops 335544320 | bytes 2637824 | tf_op jit(solution)/shard_map/attend_b_a_other/pallas_call | solution.py:234
  36.2 2.2 %collective-permute-start.17 = (bf16[512,256]{1,0:T(8,128)(2,1)S(1)}, bf16[512,256]{1,0:T(8,128)(2,1)S(1)}, u32[]{:S(2)}, u32[]{:S(2)}) collective-permute-start(bf16[512,256]{1,0:T(8,128)(2,1)S(1)} %sum_keys_over_core.1), channel_id=1, source_target_pairs={{0,6},{1,3},{64,70},{65,67},{8,14},{9,11},{72,78},{73,75},{16,22},... | collective-permute-start | bytes 786440 | tf_op jit(solution)/shard_map/sum_keys/ppermute | solution.py:43
  38.4 1.5 %attend_b_a.1 = (f32[512,256]{1,0:T(8,128)S(1)}, bf16[512,128]{1,0:T(8,128)(2,1)S(1)}, bf16[512,128]{1,0:T(8,128)(2,1)S(1)}) custom-call(bf16[256,256]{1,0:T(8,128)(2,1)S(1)} %get-tuple-element.40.refs_0_, bf16[256,256]{1,0:T(8,128)(2,1)S(1)} %collective-permute-done.3.refs_1_, bf16[528,256]{1,0:T(8,128)(2,1)S(1)} %collective-permute-done.4.refs_4_.refs_2_, ...), custom_call_target="tpu_custom_call" | custom-call | flops 335544320 | bytes 2113536 | tf_op jit(solution)/shard_map/attend_b_a/pallas_call | solution.py:234
  39.9 1.4 %collective-permute-start.14 = (bf16[512,128]{1,0:T(8,128)(2,1)S(1)}, bf16[512,128]{1,0:T(8,128)(2,1)S(1)}, u32[]{:S(2)}, u32[]{:S(2)}) collective-permute-start(bf16[512,128]{1,0:T(8,128)(2,1)S(1)} %get-tuple-element.56), channel_id=1, source_target_pairs={{0,72},{1,65},{64,8},{65,1},{8,64},{9,73},{72,0},{73,9},{16,88},{1... | collective-permute-start | bytes 393224 | tf_op jit(solution)/shard_map/sum_queries/ppermute | solution.py:43
  41.3 1.9 %collective-permute-start.15 = (bf16[512,128]{1,0:T(8,128)(2,1)S(1)}, bf16[512,128]{1,0:T(8,128)(2,1)S(1)}, u32[]{:S(2)}, u32[]{:S(2)}) collective-permute-start(bf16[512,128]{1,0:T(8,128)(2,1)S(1)} %get-tuple-element.57), channel_id=1, source_target_pairs={{0,8},{1,9},{64,72},{65,73},{8,0},{9,1},{72,64},{73,65},{16,24},{1... | collective-permute-start | bytes 393224 | tf_op jit(solution)/shard_map/sum_queries/ppermute | solution.py:43
  43.1 1.5 %attend_a_a.1 = (f32[512,256]{1,0:T(8,128)S(1)}, f32[512,128]{1,0:T(8,128)S(1)}, bf16[512,128]{1,0:T(8,128)(2,1)S(1)}) custom-call(bf16[256,256]{1,0:T(8,128)(2,1)S(1)} %get-tuple-element.40.refs_0_, bf16[256,256]{1,0:T(8,128)(2,1)S(1)} %collective-permute-done.3.refs_1_, bf16[528,256]{1,0:T(8,128)(2,1)S(1)} %get-tuple-element.41.refs_2_.refs_4_, ...), custom_call_target="tpu_custom_call" | custom-call | flops 335544320 | bytes 2768896 | tf_op jit(solution)/shard_map/attend_a_a/pallas_call | solution.py:234
  45.8 2.8 %collective-permute-done.14.a = bf16[512,128]{1,0:T(8,128)(2,1)S(1)} collective-permute-done((bf16[512,128]{1,0:T(8,128)(2,1)S(1)}, bf16[512,128]{1,0:T(8,128)(2,1)S(1)}, u32[]{:S(2)}, u32[]{:S(2)}) %collective-permute-start.14) | collective-permute-done | bytes 131104 | tf_op jit(solution)/shard_map/sum_queries/ppermute | solution.py:43
  51.4 2.0 %collective-permute-start.21 = (bf16[128,256]{1,0:T(8,128)(2,1)S(1)}, bf16[128,256]{1,0:T(8,128)(2,1)S(1)}, u32[]{:S(2)}, u32[]{:S(2)}) collective-permute-start(bf16[128,256]{1,0:T(8,128)(2,1)S(1)} %get-tuple-element.69), channel_id=1, source_target_pairs={{0,48},{1,17},{64,112},{65,81},{8,56},{9,25},{72,120},{73,89},{16,... | collective-permute-start | bytes 196616 | tf_op jit(solution)/shard_map/back_to_rows/ppermute | solution.py:43
  53.4 1.6 %collective-permute-start.22 = (bf16[128,256]{1,0:T(8,128)(2,1)S(1)}, bf16[128,256]{1,0:T(8,128)(2,1)S(1)}, u32[]{:S(2)}, u32[]{:S(2)}) collective-permute-start(bf16[128,256]{1,0:T(8,128)(2,1)S(1)} %get-tuple-element.70), channel_id=1, source_target_pairs={{0,32},{1,33},{64,96},{65,97},{8,40},{9,41},{72,104},{73,105},{16,... | collective-permute-start | bytes 196616 | tf_op jit(solution)/shard_map/back_to_rows/ppermute | solution.py:43
  55.7 1.9 %collective-permute-done.21.b3 = bf16[128,256]{1,0:T(8,128)(2,1)S(1)} collective-permute-done((bf16[128,256]{1,0:T(8,128)(2,1)S(1)}, bf16[128,256]{1,0:T(8,128)(2,1)S(1)}, u32[]{:S(2)}, u32[]{:S(2)}) %collective-permute-start.21) | collective-permute-done | bytes 65568 | tf_op jit(solution)/shard_map/back_to_rows/ppermute | solution.py:43
  57.5 1.6 %collective-permute-done.22.b2 = bf16[128,256]{1,0:T(8,128)(2,1)S(1)} collective-permute-done((bf16[128,256]{1,0:T(8,128)(2,1)S(1)}, bf16[128,256]{1,0:T(8,128)(2,1)S(1)}, u32[]{:S(2)}, u32[]{:S(2)}) %collective-permute-start.22) | collective-permute-done | bytes 65568 | tf_op jit(solution)/shard_map/back_to_rows/ppermute | solution.py:43
  (39 shorter events, 9.9 us)
Async XLA Ops:
  2.6 7.2 %collective-permute-start = (bf16[208,256]{1,0:T(8,128)(2,1)}, bf16[208,256]{1,0:T(8,128)(2,1)S(1)}, u32[]{:S(2)}, u32[]{:S(2)}) collective-permute-start(bf16[208,256]{1,0:T(8,128)(2,1)} %get-tuple-element.37), channel_id=1, source_target_pairs={{0,32},{1,33},{64,96},{65,97},{8,40},{9,41},{72,104},{73,105},{16,... | collective-permute-start | bytes 319496 | tf_op jit(solution)/shard_map/heads_to_chips/ppermute | solution.py:43
  5.9 5.9 %collective-permute-start.1 = (bf16[208,256]{1,0:T(8,128)(2,1)}, bf16[208,256]{1,0:T(8,128)(2,1)S(1)}, u32[]{:S(2)}, u32[]{:S(2)}) collective-permute-start(bf16[208,256]{1,0:T(8,128)(2,1)} %get-tuple-element.38), channel_id=1, source_target_pairs={{0,16},{1,49},{64,80},{65,113},{8,24},{9,57},{72,88},{73,121},{16,... | collective-permute-start | bytes 319496 | tf_op jit(solution)/shard_map/heads_to_chips/ppermute | solution.py:43
  6.6 6.1 %collective-permute-start.2 = (bf16[208,256]{1,0:T(8,128)(2,1)}, bf16[208,256]{1,0:T(8,128)(2,1)S(1)}, u32[]{:S(2)}, u32[]{:S(2)}) collective-permute-start(bf16[208,256]{1,0:T(8,128)(2,1)} %get-tuple-element.39), channel_id=1, source_target_pairs={{0,48},{1,17},{64,112},{65,81},{8,56},{9,25},{72,120},{73,89},{16,... | collective-permute-start | bytes 319496 | tf_op jit(solution)/shard_map/heads_to_chips/ppermute | solution.py:43
  8.9 0.9 %copy-start = (bf16[208,256]{1,0:T(8,128)(2,1)S(1)}, bf16[208,256]{1,0:T(8,128)(2,1)}, u32[]{:S(2)}) copy-start(bf16[208,256]{1,0:T(8,128)(2,1)} %pack.4.source) | copy-start | bytes 319492
  12.8 8.9 %collective-permute-start.7 = (bf16[528,256]{1,0:T(8,128)(2,1)S(1)}, bf16[528,256]{1,0:T(8,128)(2,1)S(1)}, u32[]{:S(2)}, u32[]{:S(2)}) collective-permute-start(bf16[528,256]{1,0:T(8,128)(2,1)S(1)} %get-tuple-element.41.refs_2_.refs_4_), channel_id=1, source_target_pairs={{0,64},{1,73},{64,0},{65,9},{8,72},{9,65},{72,8},{73,1},{16,80},{1... | collective-permute-start | bytes 811016 | tf_op jit(solution)/shard_map/gather_queries/ppermute | solution.py:43
  14.8 12.2 %collective-permute-start.4 = (bf16[528,256]{1,0:T(8,128)(2,1)S(1)}, bf16[528,256]{1,0:T(8,128)(2,1)S(1)}, u32[]{:S(2)}, u32[]{:S(2)}) collective-permute-start(bf16[528,256]{1,0:T(8,128)(2,1)S(1)} %get-tuple-element.41.refs_2_.refs_4_), channel_id=1, source_target_pairs={{0,72},{1,65},{64,8},{65,1},{8,64},{9,73},{72,0},{73,9},{16,88},{1... | collective-permute-start | bytes 811016 | tf_op jit(solution)/shard_map/gather_queries/ppermute | solution.py:43
  17.3 6.8 %collective-permute-start.6 = (bf16[256,256]{1,0:T(8,128)(2,1)S(1)}, bf16[256,256]{1,0:T(8,128)(2,1)S(1)}, u32[]{:S(2)}, u32[]{:S(2)}) collective-permute-start(bf16[256,256]{1,0:T(8,128)(2,1)S(1)} %get-tuple-element.40.refs_0_), channel_id=1, source_target_pairs={{0,4},{1,5},{64,68},{65,69},{8,12},{9,13},{72,76},{73,77},{16,20},... | collective-permute-start | bytes 393224 | tf_op jit(solution)/shard_map/gather_keys/ppermute | solution.py:43
  20.3 6.2 %collective-permute-start.5 = (bf16[256,256]{1,0:T(8,128)(2,1)S(1)}, bf16[256,256]{1,0:T(8,128)(2,1)S(1)}, u32[]{:S(2)}, u32[]{:S(2)}) collective-permute-start(bf16[256,256]{1,0:T(8,128)(2,1)S(1)} %get-tuple-element.40.refs_0_), channel_id=1, source_target_pairs={{0,6},{1,3},{64,70},{65,67},{8,14},{9,11},{72,78},{73,75},{16,22},... | collective-permute-start | bytes 393224 | tf_op jit(solution)/shard_map/gather_keys/ppermute | solution.py:43
  21.5 5.0 %collective-permute-start.3 = (bf16[256,256]{1,0:T(8,128)(2,1)S(1)}, bf16[256,256]{1,0:T(8,128)(2,1)S(1)}, u32[]{:S(2)}, u32[]{:S(2)}) collective-permute-start(bf16[256,256]{1,0:T(8,128)(2,1)S(1)} %get-tuple-element.40.refs_0_), channel_id=1, source_target_pairs={{0,2},{1,7},{64,66},{65,71},{8,10},{9,15},{72,74},{73,79},{16,18},... | collective-permute-start | bytes 393224 | tf_op jit(solution)/shard_map/gather_keys/ppermute | solution.py:43
  21.7 9.6 %collective-permute-start.8 = (bf16[528,256]{1,0:T(8,128)(2,1)S(1)}, bf16[528,256]{1,0:T(8,128)(2,1)S(1)}, u32[]{:S(2)}, u32[]{:S(2)}) collective-permute-start(bf16[528,256]{1,0:T(8,128)(2,1)S(1)} %collective-permute-done.7.refs_3_.refs_5_), channel_id=1, source_target_pairs={{0,72},{1,65},{64,8},{65,1},{8,64},{9,73},{72,0},{73,9},{16,88},{1... | collective-permute-start | bytes 811016 | tf_op jit(solution)/shard_map/gather_queries/ppermute | solution.py:43
  24.1 4.4 %collective-permute-start.11 = (bf16[256,256]{1,0:T(8,128)(2,1)S(1)}, bf16[256,256]{1,0:T(8,128)(2,1)S(1)}, u32[]{:S(2)}, u32[]{:S(2)}) collective-permute-start(bf16[256,256]{1,0:T(8,128)(2,1)S(1)} %get-tuple-element.40.refs_0_), channel_id=1, source_target_pairs={{0,1},{1,0},{64,65},{65,64},{8,9},{9,8},{72,73},{73,72},{16,17},{1... | collective-permute-start | bytes 393224 | tf_op jit(solution)/shard_map/gather_keys/ppermute | solution.py:43
  26.5 2.0 %collective-permute-start.10 = (bf16[256,256]{1,0:T(8,128)(2,1)S(1)}, bf16[256,256]{1,0:T(8,128)(2,1)S(1)}, u32[]{:S(2)}, u32[]{:S(2)}) collective-permute-start(bf16[256,256]{1,0:T(8,128)(2,1)S(1)} %collective-permute-done.6.refs_1_.refs_3_), channel_id=1, source_target_pairs={{0,1},{1,0},{64,65},{65,64},{8,9},{9,8},{72,73},{73,72},{16,17},{1... | collective-permute-start | bytes 393224 | tf_op jit(solution)/shard_map/gather_keys/ppermute | solution.py:43
  26.5 2.0 %collective-permute-start.9 = (bf16[256,256]{1,0:T(8,128)(2,1)S(1)}, bf16[256,256]{1,0:T(8,128)(2,1)S(1)}, u32[]{:S(2)}, u32[]{:S(2)}) collective-permute-start(bf16[256,256]{1,0:T(8,128)(2,1)S(1)} %collective-permute-done.5.refs_0_.refs_2_), channel_id=1, source_target_pairs={{0,1},{1,0},{64,65},{65,64},{8,9},{9,8},{72,73},{73,72},{16,17},{1... | collective-permute-start | bytes 393224 | tf_op jit(solution)/shard_map/gather_keys/ppermute | solution.py:43
  27.0 1.5 %collective-permute-start.12 = (bf16[256,256]{1,0:T(8,128)(2,1)S(1)}, bf16[256,256]{1,0:T(8,128)(2,1)S(1)}, u32[]{:S(2)}, u32[]{:S(2)}) collective-permute-start(bf16[256,256]{1,0:T(8,128)(2,1)S(1)} %collective-permute-done.3.refs_1_), channel_id=1, source_target_pairs={{0,1},{1,0},{64,65},{65,64},{8,9},{9,8},{72,73},{73,72},{16,17},{1... | collective-permute-start | bytes 393224 | tf_op jit(solution)/shard_map/gather_keys/ppermute | solution.py:43
  34.0 2.2 %collective-permute-start.13 = (bf16[512,256]{1,0:T(8,128)(2,1)S(1)}, bf16[512,256]{1,0:T(8,128)(2,1)S(1)}, u32[]{:S(2)}, u32[]{:S(2)}) collective-permute-start(bf16[512,256]{1,0:T(8,128)(2,1)S(1)} %get-tuple-element.54), channel_id=1, source_target_pairs={{0,1},{1,0},{64,65},{65,64},{8,9},{9,8},{72,73},{73,72},{16,17},{1... | collective-permute-start | bytes 786440 | tf_op jit(solution)/shard_map/sum_keys_over_core/ppermute | solution.py:43
  36.0 9.7 %collective-permute-start.16 = (bf16[512,256]{1,0:T(8,128)(2,1)S(1)}, bf16[512,256]{1,0:T(8,128)(2,1)S(1)}, u32[]{:S(2)}, u32[]{:S(2)}) collective-permute-start(bf16[512,256]{1,0:T(8,128)(2,1)S(1)} %get-tuple-element.62), channel_id=1, source_target_pairs={{0,1},{1,0},{64,65},{65,64},{8,9},{9,8},{72,73},{73,72},{16,17},{1... | collective-permute-start | bytes 786440 | tf_op jit(solution)/shard_map/sum_keys_over_core/ppermute | solution.py:43
  36.2 9.4 %collective-permute-start.17 = (bf16[512,256]{1,0:T(8,128)(2,1)S(1)}, bf16[512,256]{1,0:T(8,128)(2,1)S(1)}, u32[]{:S(2)}, u32[]{:S(2)}) collective-permute-start(bf16[512,256]{1,0:T(8,128)(2,1)S(1)} %sum_keys_over_core.1), channel_id=1, source_target_pairs={{0,6},{1,3},{64,70},{65,67},{8,14},{9,11},{72,78},{73,75},{16,22},... | collective-permute-start | bytes 786440 | tf_op jit(solution)/shard_map/sum_keys/ppermute | solution.py:43
  39.9 8.8 %collective-permute-start.14 = (bf16[512,128]{1,0:T(8,128)(2,1)S(1)}, bf16[512,128]{1,0:T(8,128)(2,1)S(1)}, u32[]{:S(2)}, u32[]{:S(2)}) collective-permute-start(bf16[512,128]{1,0:T(8,128)(2,1)S(1)} %get-tuple-element.56), channel_id=1, source_target_pairs={{0,72},{1,65},{64,8},{65,1},{8,64},{9,73},{72,0},{73,9},{16,88},{1... | collective-permute-start | bytes 393224 | tf_op jit(solution)/shard_map/sum_queries/ppermute | solution.py:43
  41.3 7.4 %collective-permute-start.15 = (bf16[512,128]{1,0:T(8,128)(2,1)S(1)}, bf16[512,128]{1,0:T(8,128)(2,1)S(1)}, u32[]{:S(2)}, u32[]{:S(2)}) collective-permute-start(bf16[512,128]{1,0:T(8,128)(2,1)S(1)} %get-tuple-element.57), channel_id=1, source_target_pairs={{0,8},{1,9},{64,72},{65,73},{8,0},{9,1},{72,64},{73,65},{16,24},{1... | collective-permute-start | bytes 393224 | tf_op jit(solution)/shard_map/sum_queries/ppermute | solution.py:43
  44.6 5.0 %collective-permute-start.19 = (bf16[512,128]{1,0:T(8,128)(2,1)S(1)}, bf16[512,128]{1,0:T(8,128)(2,1)S(1)}, u32[]{:S(2)}, u32[]{:S(2)}) collective-permute-start(bf16[512,128]{1,0:T(8,128)(2,1)S(1)} %get-tuple-element.66), channel_id=1, source_target_pairs={{0,64},{1,73},{64,0},{65,9},{8,72},{9,65},{72,8},{73,1},{16,80},{1... | collective-permute-start | bytes 393224 | tf_op jit(solution)/shard_map/sum_queries/ppermute | solution.py:43
  45.7 5.0 %collective-permute-start.18 = (bf16[256,256]{1,0:T(8,128)(2,1)S(1)}, bf16[256,256]{1,0:T(8,128)(2,1)S(1)}, u32[]{:S(2)}, u32[]{:S(2)}) collective-permute-start(bf16[256,256]{1,0:T(8,128)(2,1)S(1)} %get-tuple-element.65), channel_id=1, source_target_pairs={{0,2},{1,7},{64,66},{65,71},{8,10},{9,15},{72,74},{73,79},{16,18},... | collective-permute-start | bytes 393224 | tf_op jit(solution)/shard_map/sum_keys/ppermute | solution.py:43
  50.8 4.8 %collective-permute-start.20 = (bf16[128,256]{1,0:T(8,128)(2,1)S(1)}, bf16[128,256]{1,0:T(8,128)(2,1)S(1)}, u32[]{:S(2)}, u32[]{:S(2)}) collective-permute-start(bf16[128,256]{1,0:T(8,128)(2,1)S(1)} %get-tuple-element.68), channel_id=1, source_target_pairs={{0,16},{1,49},{64,80},{65,113},{8,24},{9,57},{72,88},{73,121},{16,... | collective-permute-start | bytes 196616 | tf_op jit(solution)/shard_map/back_to_rows/ppermute | solution.py:43
  51.4 6.2 %collective-permute-start.21 = (bf16[128,256]{1,0:T(8,128)(2,1)S(1)}, bf16[128,256]{1,0:T(8,128)(2,1)S(1)}, u32[]{:S(2)}, u32[]{:S(2)}) collective-permute-start(bf16[128,256]{1,0:T(8,128)(2,1)S(1)} %get-tuple-element.69), channel_id=1, source_target_pairs={{0,48},{1,17},{64,112},{65,81},{8,56},{9,25},{72,120},{73,89},{16,... | collective-permute-start | bytes 196616 | tf_op jit(solution)/shard_map/back_to_rows/ppermute | solution.py:43
  53.4 5.8 %collective-permute-start.22 = (bf16[128,256]{1,0:T(8,128)(2,1)S(1)}, bf16[128,256]{1,0:T(8,128)(2,1)S(1)}, u32[]{:S(2)}, u32[]{:S(2)}) collective-permute-start(bf16[128,256]{1,0:T(8,128)(2,1)S(1)} %get-tuple-element.70), channel_id=1, source_target_pairs={{0,32},{1,33},{64,96},{65,97},{8,40},{9,41},{72,104},{73,105},{16,... | collective-permute-start | bytes 196616 | tf_op jit(solution)/shard_map/back_to_rows/ppermute | solution.py:43
